TPU v7x, 32 devices: a whole 2x2x4 slice. The times are simulated.
32 devices in a mesh: dp: 2 (over x), ctx: 16 (over z, y, core).
Axes of the slice: x: 2, y: 2, z: 4, core: 2. Of those that a mesh axis runs over, the one named last changes fastest.
Arguments:
- q_proj: float32 [8192, 512], P(('dp', 'ctx')), parts along dimension 0, may hold values from -6 to 6
- k_proj: float32 [8192, 512], P(('dp', 'ctx')), parts along dimension 0, may hold values from -6 to 6
- v_proj: float32 [8192, 512], P(('dp', 'ctx')), parts along dimension 0, may hold values from -6 to 6
- short_filter: float32 [3, 3, 512], replicated, may hold values from -3 to 3
- skip_gain: float32 [512], replicated, may hold values from -4 to 4
- filter_spec: float32 [2, 8192, 512], P(None, 'ctx'), may hold values from -6 to 6
Outputs:
- gated: float32 [8192, 512], P(('dp', 'ctx')), parts along dimension 0
There are 2 independent parts, one for each index of `dp`. A program takes and returns all parts, laid end to end along the dimension named above; an argument that names none is the same for every part. Nothing has to cross between parts.
All inputs are finite; a program needn't handle non-finite values.
Results may differ from a plain program's by a relative error of at most 0.000061.
Values sent between devices are 32-bit elements; how exact they have to be, the bound alone decides.
No kernel may reach another device: no remote copies, remote signals or barrier semaphores. Data moves between devices by JAX's collectives and lax.ppermute only.
A program may use at most 64 MiB of HBM per device.

v0:
```python
import math

import jax
import jax.numpy as jnp
from jax import lax
from jax.sharding import PartitionSpec as P

precise_mode = lax.Precision.HIGHEST


def shifted(block, axis, distance):
    devices = range(lax.axis_size(axis))
    route = [(i - distance, i) for i in devices if i - distance in devices]
    return lax.ppermute(block, axis, route)


def causal_short(signal, rim_rows, tap_gains):
    padded = jnp.concatenate([rim_rows, signal], axis=0)
    return tap_gains[0] * signal + tap_gains[1] * padded[1:-1] + tap_gains[2] * padded[:-2]


def channel_conv(mixed_in, filter_spec, devices):
    local_rows = mixed_in.shape[0]
    seq_len = local_rows * devices
    freq_len = 2 * seq_len
    outer_len = 2 * devices
    half_inner = local_rows // 2
    columns = lax.all_to_all(mixed_in, "ctx", split_axis=1, concat_axis=0, tiled=True)
    spec_cols = lax.all_to_all(filter_spec, "ctx", split_axis=2, concat_axis=1, tiled=True)
    few_channels = columns.shape[1]
    grid = columns.reshape(half_inner, outer_len, few_channels)
    row_index = lax.iota(jnp.int32, half_inner)
    inner_freq = lax.iota(jnp.int32, local_rows)
    outer_index = lax.iota(jnp.int32, outer_len)
    first_angle = (
        2.0
        * math.pi
        * (row_index[:, None] * inner_freq[None, :] % local_rows).astype(jnp.float32)
        / local_rows
    )
    first_cos = jnp.cos(first_angle)
    first_sin = jnp.sin(first_angle)
    twist_angle = (
        2.0
        * math.pi
        * (inner_freq[:, None] * outer_index[None, :] % freq_len).astype(jnp.float32)
        / freq_len
    )
    twist_cos = jnp.cos(twist_angle)[:, :, None]
    twist_sin = jnp.sin(twist_angle)[:, :, None]
    last_angle = (
        2.0
        * math.pi
        * (outer_index[:, None] * outer_index[None, :] % outer_len).astype(jnp.float32)
        / outer_len
    )
    last_cos = jnp.cos(last_angle)
    last_sin = jnp.sin(last_angle)
    section_re = jnp.einsum("bk,bac->kac", first_cos, grid, precision=precise_mode)
    section_im = -jnp.einsum("bk,bac->kac", first_sin, grid, precision=precise_mode)
    turned_re = section_re * twist_cos + section_im * twist_sin
    turned_im = section_im * twist_cos - section_re * twist_sin
    spec_re = jnp.einsum("kac,aj->kjc", turned_re, last_cos, precision=precise_mode) + jnp.einsum(
        "kac,aj->kjc", turned_im, last_sin, precision=precise_mode
    )
    spec_im = jnp.einsum("kac,aj->kjc", turned_im, last_cos, precision=precise_mode) - jnp.einsum(
        "kac,aj->kjc", turned_re, last_sin, precision=precise_mode
    )
    resp = jnp.transpose(spec_cols.reshape(2, outer_len, local_rows, few_channels), (0, 2, 1, 3))
    prod_re = spec_re * resp[0] - spec_im * resp[1]
    prod_im = spec_re * resp[1] + spec_im * resp[0]
    undo_re = jnp.einsum("kjc,aj->kac", prod_re, last_cos, precision=precise_mode) - jnp.einsum(
        "kjc,aj->kac", prod_im, last_sin, precision=precise_mode
    )
    undo_im = jnp.einsum("kjc,aj->kac", prod_im, last_cos, precision=precise_mode) + jnp.einsum(
        "kjc,aj->kac", prod_re, last_sin, precision=precise_mode
    )
    back_re = undo_re * twist_cos - undo_im * twist_sin
    back_im = undo_im * twist_cos + undo_re * twist_sin
    signal_out = jnp.einsum("bk,kac->bac", first_cos, back_re, precision=precise_mode) - jnp.einsum(
        "bk,kac->bac", first_sin, back_im, precision=precise_mode
    )
    conv_cols = signal_out.reshape(seq_len, few_channels) / freq_len
    return lax.all_to_all(conv_cols, "ctx", split_axis=0, concat_axis=1, tiled=True)


def per_device(q_proj, k_proj, v_proj, short_filter, skip_gain, filter_spec):
    devices = lax.axis_size("ctx")
    tail_rows = jnp.stack([q_proj[-2:], k_proj[-2:], v_proj[-2:]])
    rim_rows = shifted(tail_rows, "ctx", 1)
    query_seq = causal_short(q_proj, rim_rows[0], short_filter[0])
    key_seq = causal_short(k_proj, rim_rows[1], short_filter[1])
    value_seq = causal_short(v_proj, rim_rows[2], short_filter[2])
    mixed_in = key_seq * value_seq
    conv_out = channel_conv(mixed_in, filter_spec, devices)
    return query_seq * (conv_out + skip_gain[None, :] * mixed_in)


def solution(mesh):
    placed = (
        P(("dp", "ctx"), None),
        P(("dp", "ctx"), None),
        P(("dp", "ctx"), None),
        P(),
        P(),
        P(None, "ctx", None),
    )
    return jax.shard_map(
        per_device, mesh=mesh, in_specs=placed, out_specs=P(("dp", "ctx"), None), check_vma=False
    )
```

profile of v0, /device:TPU:0, one launch (start us, length us, event | category | flops | bytes accessed | tf_op | source)
XLA Modules:
  0.0 128.1 jit_solution(12305204240670483899)
XLA Ops:
  1.5 2.4 %collective-permute-start = (f32[3,2,512]{2,1,0:T(2,128)S(1)}, f32[3,2,512]{2,1,0:T(2,128)S(1)}, u32[]{:S(2)}, u32[]{:S(2)}) collective-permute-start(f32[3,2,512]{2,1,0:T(2,128)S(1)} %pad_maximum_fusion.3), channel_id=1, source_target_pairs={{0,1},{1,2},{2,3},{3,4},{4,5},{5,6},{6,7},{7,8},{8,9},{9,10},{10,1... | collective-permute-start | bytes 36872 | tf_op jit(solution)/shard_map/ppermute | solution.py:14
  3.8 0.9 fusion.127
  4.7 1.2 copy.52
  6.0 1.2 copy.55
  7.4 0.9 copy.89
  8.3 2.9 %fusion.14 = f32[256,512]{0,1:T(8,128)} fusion(f32[2,512]{0,1:T(8,128)} %bitcast.121, f32[256,512]{0,1:T(8,128)S(1)} %copy.55, f32[2,512]{0,1:T(8,128)S(1)} %bitcast.120, f32[256,512]{0,1:T(8,128)S(1)} %copy.52, f32[512]{0:T(512)S(1)} %bitcast.129, f32[512]{0:T(512)S(1)} %bitcast.130, f32[512]{0:T(512)S(1)} %bitcast.125, f32[512]{0:T(512)S(1)} %bitcast.126, ...), kind=kLoop, calls=%fused_computation.34 | loop fusion | flops 1966080 | bytes 1593344 | tf_op jit(solution)/shard_map/mul | solution.py:94
  11.2 7.2 %all-to-all-start = ((f32[256,16,32]{0,2,1:T(8,128)}), f32[256,16,32]{0,2,1:T(8,128)S(1)}, u32[]{:S(2)}, u32[]{:S(2)}) async-start(f32[256,16,32]{0,2,1:T(8,128)} %bitcast.17), calls=%async_computation | async-start | bytes 1048576 | tf_op jit(solution)/shard_map/all_to_all | solution.py:28
  18.4 2.5 %copy.65 = f32[2,512,512]{1,0,2:T(2,128)} copy(f32[2,512,512]{2,1,0:T(8,128)S(1)} %copy-done) | data formatting | bytes 4194304 | tf_op args[5]
  20.9 12.0 %all-to-all-done = f32[256,16,32]{0,2,1:T(8,128)S(1)} async-done(((f32[256,16,32]{0,2,1:T(8,128)}), f32[256,16,32]{0,2,1:T(8,128)S(1)}, u32[]{:S(2)}, u32[]{:S(2)}) %all-to-all-start) | async-done | bytes 524320 | tf_op jit(solution)/shard_map/all_to_all | solution.py:28
  32.9 4.4 %all-to-all-start.1 = ((f32[2,512,512]{1,0,2:T(2,128)}), f32[2,512,512]{1,0,2:T(2,128)}, u32[]{:S(2)}, u32[]{:S(2)}) async-start(f32[2,512,512]{1,0,2:T(2,128)} %copy.65), calls=%async_computation.1 | async-start | bytes 4194304 | tf_op jit(solution)/shard_map/all_to_all | solution.py:29
  39.0 1.5 %fusion.37 = f32[256,1024]{0,1:S(1)} fusion(f32[128,1024]{0,1:T(8,128)S(1)} %bitcast.109), kind=kOutput, calls=%fused_computation.64 | convolution fusion | flops 403111936 | bytes 1572864
  40.5 1.5 %fusion.41 = f32[256,1024]{0,1:S(1)} fusion(f32[128,1024]{0,1:T(8,128)S(1)} %bitcast.110), kind=kOutput, calls=%fused_computation.66 | convolution fusion | flops 403111936 | bytes 1572864
  42.4 1.6 %fusion.8 = f32[32,256,32]{1,0,2:T(8,128)S(1)} fusion(f32[256,32,32]{0,2,1:T(8,128)S(1)} %get-tuple-element.9), kind=kOutput, calls=%fused_computation.22 | convolution fusion | flops 100677632 | bytes 2097152 | tf_op jit(solution)/shard_map/kac,aj->kjc/dot_general | solution.py:63
  44.1 2.7 %fusion.4 = f32[32,256,32]{1,0,2:T(8,128)} fusion(f32[256,32,32]{0,2,1:T(8,128)S(1)} %get-tuple-element.10), kind=kOutput, calls=%fused_computation.18 | convolution fusion | flops 100677632 | bytes 2097152 | tf_op jit(solution)/shard_map/kac,aj->kjc/dot_general | solution.py:66
  46.7 2.6 %fusion.1 = f32[256,32,32]{0,1,2:T(8,128)} fusion(f32[32,256,32]{1,0,2:T(8,128)S(1)} %fusion.8, f32[256,32,32]{0,2,1:T(8,128)S(1)} %get-tuple-element.10), kind=kOutput, calls=%fused_computation.3 | convolution fusion | flops 100939776 | bytes 3145728 | tf_op jit(solution)/shard_map/kac,aj->kjc/dot_general | solution.py:63
  49.3 29.1 %all-to-all-done.1 = f32[2,512,512]{1,0,2:T(2,128)} async-done(((f32[2,512,512]{1,0,2:T(2,128)}), f32[2,512,512]{1,0,2:T(2,128)}, u32[]{:S(2)}, u32[]{:S(2)}) %all-to-all-start.1) | async-done | bytes 2097184 | tf_op jit(solution)/shard_map/all_to_all | solution.py:29
  78.4 2.0 %copy.66 = f32[2,512,512]{1,2,0:T(8,128)S(1)} copy(f32[2,512,512]{1,0,2:T(2,128)} %all-to-all-done.1) | data formatting | bytes 4194304 | tf_op jit(solution)/shard_map/all_to_all | solution.py:29
  80.4 1.2 copy.67
  81.7 1.5 %reshape.74 = f32[2,32,256,32]{2,1,3,0:T(8,128)} reshape(f32[2,16,512,32]{2,1,3,0:T(8,128)S(1)} %copy.67) | data formatting | bytes 4194304 | tf_op jit(solution)/shard_map/reshape | solution.py:69
  83.2 4.1 %multiply_subtract_fusion = (f32[256,32,32]{0,1,2:T(8,128)S(1)}, f32[256,32,32]{0,1,2:T(8,128)S(1)}) fusion(f32[256,32,32]{0,1,2:T(8,128)} %fusion.1, f32[2,256,32,32]{1,2,3,0:T(8,128)} %bitcast.111, f32[32,256,32]{1,0,2:T(8,128)} %fusion.4, f32[256,32,32]{0,2,1:T(8,128)S(1)} %get-tuple-element.9), kind=kOutput, calls=%fused_computation.15 | convolution fusion | flops 102512640 | bytes 7340032 | tf_op jit(solution)/shard_map/kac,aj->kjc/dot_general | solution.py:66
  87.3 1.1 fusion.54
  88.4 1.1 fusion.60
  89.4 1.1 fusion.52
  90.5 1.1 fusion.62
  91.6 2.4 %fusion.3 = (f32[256,32,32]{0,2,1:T(8,128)S(1)}, f32[256,32,32]{0,2,1:T(8,128)S(1)}) fusion(f32[256,32]{0,1:T(8,128)S(1)} %get-tuple-element.25, f32[256,32]{0,1:T(8,128)S(1)} %get-tuple-element.26, f32[32,256,32]{1,0,2:T(8,128)S(1)} %fusion.54, f32[32,256,32]{1,0,2:T(8,128)S(1)} %fusion.62, f32[32,256,32]{1,0,2:T(8,128)S(1)} %fusion.52, ...), kind=kLoop, calls=%fused_computation.9 | loop fusion | flops 2097152 | bytes 6356992 | tf_op jit(solution)/shard_map/add | solution.py:79
  94.0 1.5 %fusion.35 = f32[128,1024]{0,1:S(1)} fusion(f32[256,1024]{0,1:T(8,128)S(1)} %bitcast.113), kind=kOutput, calls=%fused_computation.63 | convolution fusion | flops 403111936 | bytes 1572864
  95.5 1.5 %fusion.39 = f32[128,1024]{0,1:S(1)} fusion(f32[256,1024]{0,1:T(8,128)S(1)} %bitcast.112), kind=kOutput, calls=%fused_computation.65 | convolution fusion | flops 403111936 | bytes 1572864
  98.6 1.1 copy.77
  99.7 11.2 %all-to-all-start.2 = ((f32[16,256,32]{1,2,0:T(8,128)}), f32[16,256,32]{1,2,0:T(8,128)S(1)}, u32[]{:S(2)}, u32[]{:S(2)}) async-start(f32[16,256,32]{1,2,0:T(8,128)} %copy.77), calls=%async_computation.2 | async-start | bytes 1048576 | tf_op jit(solution)/shard_map/all_to_all | solution.py:84
  111.3 14.1 %all-to-all-done.2 = f32[16,256,32]{1,2,0:T(8,128)S(1)} async-done(((f32[16,256,32]{1,2,0:T(8,128)}), f32[16,256,32]{1,2,0:T(8,128)S(1)}, u32[]{:S(2)}, u32[]{:S(2)}) %all-to-all-start.2) | async-done | bytes 524320 | tf_op jit(solution)/shard_map/all_to_all | solution.py:84
  125.4 1.8 %fusion.23 = f32[256,512]{0,1:T(8,128)S(1)} fusion(f32[2,512]{0,1:T(8,128)S(1)} %bitcast.119, f32[256,512]{0,1:T(8,128)S(1)} %copy.49, f32[16,256,32]{1,2,0:T(8,128)S(1)} %all-to-all-done.2, f32[256,512]{0,1:T(8,128)} %fusion.14, f32[512]{0:T(512)S(1)} %copy-done.2, f32[512]{0:T(512)S(1)} %bitcast.123, f32[512]{0:T(512)S(1)} %bitcast.124, f32[512]{0:T(512)S(1)} %bitcast.122), kind=kLoop, calls=%fused_computation.43 | loop fusion | flops 1310720 | bytes 2109440 | tf_op jit(solution)/shard_map/mul | solution.py:96
  127.1 1.0 copy.78
  (22 shorter events, 5.5 us)
Async XLA Ops:
  1.5 5.8 %collective-permute-start = (f32[3,2,512]{2,1,0:T(2,128)S(1)}, f32[3,2,512]{2,1,0:T(2,128)S(1)}, u32[]{:S(2)}, u32[]{:S(2)}) collective-permute-start(f32[3,2,512]{2,1,0:T(2,128)S(1)} %pad_maximum_fusion.3), channel_id=1, source_target_pairs={{0,1},{1,2},{2,3},{3,4},{4,5},{5,6},{6,7},{7,8},{8,9},{9,10},{10,1... | collective-permute-start | bytes 36872 | tf_op jit(solution)/shard_map/ppermute | solution.py:14
  7.2 11.2 %copy-start = (f32[2,512,512]{2,1,0:T(8,128)S(1)}, f32[2,512,512]{2,1,0:T(8,128)}, u32[]{:S(2)}) copy-start(f32[2,512,512]{2,1,0:T(8,128)} %param.11) | copy-start | bytes 6291460
  11.2 21.7 %all-to-all-start = ((f32[256,16,32]{0,2,1:T(8,128)}), f32[256,16,32]{0,2,1:T(8,128)S(1)}, u32[]{:S(2)}, u32[]{:S(2)}) async-start(f32[256,16,32]{0,2,1:T(8,128)} %bitcast.17), calls=%async_computation | async-start | bytes 1048576 | tf_op jit(solution)/shard_map/all_to_all | solution.py:28
  32.9 45.5 %all-to-all-start.1 = ((f32[2,512,512]{1,0,2:T(2,128)}), f32[2,512,512]{1,0,2:T(2,128)}, u32[]{:S(2)}, u32[]{:S(2)}) async-start(f32[2,512,512]{1,0,2:T(2,128)} %copy.65), calls=%async_computation.1 | async-start | bytes 4194304 | tf_op jit(solution)/shard_map/all_to_all | solution.py:29
  98.0 12.9 %copy-start.1 = (f32[256,512]{1,0:T(8,128)S(1)}, f32[256,512]{1,0:T(8,128)}, u32[]{:S(2)}) copy-start(f32[256,512]{1,0:T(8,128)} %param.6) | copy-start | bytes 1572868
  98.6 26.8 %copy-start.2 = (f32[512]{0:T(512)S(1)}, f32[512]{0:T(512)}, u32[]{:S(2)}) copy-start(f32[512]{0:T(512)} %param.10) | copy-start | bytes 6148
  99.7 25.7 %all-to-all-start.2 = ((f32[16,256,32]{1,2,0:T(8,128)}), f32[16,256,32]{1,2,0:T(8,128)S(1)}, u32[]{:S(2)}, u32[]{:S(2)}) async-start(f32[16,256,32]{1,2,0:T(8,128)} %copy.77), calls=%async_computation.2 | async-start | bytes 1048576 | tf_op jit(solution)/shard_map/all_to_all | solution.py:84
where the time goes:
time: 129 us; the launch traced here: 128 us
  waiting for transfers between devices  55.2 us (43%)
  starting transfers between devices  25.2 us (20%)
  matrix products  21.4 us (17%)
  local copies, waits for them, and re-layouts  18.4 us (14%)
  other arithmetic  7.67 us (6%)
    all_to_all x1, waiting for transfers between devices, channel_conv(): lax.all_to_all(filter_spec, 'ctx', split_axis=2, concat_axis=1, tiled=True)  29.1 us
    all_to_all x1, waiting for transfers between devices, channel_conv(): lax.all_to_all(conv_cols, 'ctx', split_axis=0, concat_axis=1, tiled=True)  14.1 us
    all_to_all x1, waiting for transfers between devices, channel_conv(): lax.all_to_all(mixed_in, 'ctx', split_axis=1, concat_axis=0, tiled=True)  12 us
    all_to_all x1, starting transfers between devices, channel_conv(): lax.all_to_all(conv_cols, 'ctx', split_axis=0, concat_axis=1, tiled=True)  11.2 us
    all_to_all x1, starting transfers between devices, channel_conv(): lax.all_to_all(mixed_in, 'ctx', split_axis=1, concat_axis=0, tiled=True)  7.22 us
    unnamed x13, local copies, waits for them, and re-layouts  6.31 us
    unnamed x4, matrix products  6 us
    all_to_all x1, starting transfers between devices, channel_conv(): lax.all_to_all(filter_spec, 'ctx', split_axis=2, concat_axis=1, tiled=True)  4.44 us
  transfers between devices with their start and end apart: 4, of which 3 were waited for; matrix products, arithmetic and copies ran while one was open for 14% of the time, Pallas kernels for 0%

commit v1 on v0

v1 whole, which is shorter than its diff:
```python
import functools
import math

import jax
import jax.numpy as jnp
import numpy as np
from jax import lax
from jax.experimental import pallas as pl
from jax.experimental.pallas import tpu as pltpu
from jax.sharding import PartitionSpec as P

precise_mode = lax.Precision.HIGHEST
LANES = 128
BF16 = jnp.bfloat16
F32 = jnp.float32


def causal_short(signal, rim_rows, tap_gains):
    padded = jnp.concatenate([rim_rows, signal], axis=0)
    return tap_gains[0] * signal + tap_gains[1] * padded[1:-1] + tap_gains[2] * padded[:-2]


def shifted(block, axis, distance):
    devices = range(lax.axis_size(axis))
    route = [(i - distance, i) for i in devices if i - distance in devices]
    return lax.ppermute(block, axis, route)


def channel_conv(mixed_in, filter_spec, devices):
    local_rows = mixed_in.shape[0]
    seq_len = local_rows * devices
    freq_len = 2 * seq_len
    outer_len = 2 * devices
    half_inner = local_rows // 2
    columns = lax.all_to_all(mixed_in, "ctx", split_axis=1, concat_axis=0, tiled=True)
    spec_cols = lax.all_to_all(filter_spec, "ctx", split_axis=2, concat_axis=1, tiled=True)
    few_channels = columns.shape[1]
    grid = columns.reshape(half_inner, outer_len, few_channels)
    row_index = lax.iota(jnp.int32, half_inner)
    inner_freq = lax.iota(jnp.int32, local_rows)
    outer_index = lax.iota(jnp.int32, outer_len)

    def cos_sin(left, right, period):
        turns = (left[:, None] * right[None, :] % period).astype(F32) / period
        return jnp.cos(2.0 * math.pi * turns), jnp.sin(2.0 * math.pi * turns)

    first_cos, first_sin = cos_sin(row_index, inner_freq, local_rows)
    twist_cos, twist_sin = cos_sin(inner_freq, outer_index, freq_len)
    twist_cos, twist_sin = twist_cos[:, :, None], twist_sin[:, :, None]
    last_cos, last_sin = cos_sin(outer_index, outer_index, outer_len)
    dots = functools.partial(jnp.einsum, precision=precise_mode)
    section_re = dots("bk,bac->kac", first_cos, grid)
    section_im = -dots("bk,bac->kac", first_sin, grid)
    turned_re = section_re * twist_cos + section_im * twist_sin
    turned_im = section_im * twist_cos - section_re * twist_sin
    fore = "kac,aj->kjc"
    spec_re = dots(fore, turned_re, last_cos) + dots(fore, turned_im, last_sin)
    spec_im = dots(fore, turned_im, last_cos) - dots(fore, turned_re, last_sin)
    resp = jnp.transpose(spec_cols.reshape(2, outer_len, local_rows, few_channels), (0, 2, 1, 3))
    prod_re = spec_re * resp[0] - spec_im * resp[1]
    prod_im = spec_re * resp[1] + spec_im * resp[0]
    back = "kjc,aj->kac"
    undo_re = dots(back, prod_re, last_cos) - dots(back, prod_im, last_sin)
    undo_im = dots(back, prod_im, last_cos) + dots(back, prod_re, last_sin)
    back_re = undo_re * twist_cos - undo_im * twist_sin
    back_im = undo_im * twist_cos + undo_re * twist_sin
    signal_out = dots("bk,kac->bac", first_cos, back_re) - dots("bk,kac->bac", first_sin, back_im)
    conv_cols = signal_out.reshape(seq_len, few_channels) / freq_len
    return lax.all_to_all(conv_cols, "ctx", split_axis=0, concat_axis=1, tiled=True)


def per_device_general(q_proj, k_proj, v_proj, short_filter, skip_gain, filter_spec):
    devices = lax.axis_size("ctx")
    tail_rows = jnp.stack([q_proj[-2:], k_proj[-2:], v_proj[-2:]])
    rim_rows = shifted(tail_rows, "ctx", 1)
    query_seq = causal_short(q_proj, rim_rows[0], short_filter[0])
    key_seq = causal_short(k_proj, rim_rows[1], short_filter[1])
    value_seq = causal_short(v_proj, rim_rows[2], short_filter[2])
    mixed_in = key_seq * value_seq
    conv_out = channel_conv(mixed_in, filter_spec, devices)
    return query_seq * (conv_out + skip_gain[None, :] * mixed_in)


def split_np(table):
    high = table.astype(BF16)
    low = (table - high.astype(np.float64)).astype(BF16)
    return high, low


@functools.lru_cache(maxsize=None)
def tables(parts, devices, rows):
    outer, seq = 2 * devices, devices * rows
    freq = 2 * seq
    p, s, r = np.arange(devices), np.arange(outer), np.arange(rows)
    chunks = rows * 2 // parts // 64
    low_bit, chunk, part, dev = np.meshgrid(
        np.arange(2), np.arange(chunks), np.arange(parts), np.arange(devices), indexing="ij"
    )
    k = (dev * (2 * rows // outer) + part * (2 * rows // parts // outer) + 2 * chunk + low_bit).ravel()

    def angle(left, right, period):
        return 2.0 * np.pi * (np.outer(left, right) % period) / period

    first = angle(s, p, outer)
    w1h, w1l = split_np(np.concatenate([np.cos(first), -np.sin(first)]))
    w1 = np.concatenate([w1h, w1h, w1l], axis=1)
    last = np.concatenate([np.cos(first.T), -np.sin(first.T)], axis=1) / freq
    w2h, w2l = split_np(last)
    w2 = np.concatenate([w2h, w2h, w2l], axis=1)
    twist = angle(s, r, freq)
    inner = angle(r, k, rows)
    c, d = np.cos(inner), np.sin(inner)
    fore = split_np(np.block([[c, -d], [d, c]]))
    back = split_np(np.block([[c.T, d.T], [-d.T, c.T]]))
    return (w1, w2, np.cos(twist).astype(np.float32), np.sin(twist).astype(np.float32), *fore, *back)


def split(x):
    high = x.astype(BF16)
    return high, (x - high.astype(F32)).astype(BF16)


def dot(a, b):
    return jnp.dot(a, b, preferred_element_type=F32)


def causal(x, rim, taps):
    row = lax.broadcasted_iota(jnp.int32, x.shape, 0)
    one = jnp.where(row == 0, rim[1:2], pltpu.roll(x, 1, 0))
    two = jnp.where(row == 0, rim[0:1], jnp.where(row == 1, rim[1:2], pltpu.roll(x, 2, 0)))
    return taps[0:1] * x + taps[1:2] * one + taps[2:3] * two


def spec_kernel(few, part_ref, spec_ref, out_ref):
    del part_ref
    for m in range(spec_ref.shape[1] // 64):
        both = jnp.concatenate(
            [spec_ref[0, 64 * m : 64 * m + 64], spec_ref[1, 64 * m : 64 * m + 64]], axis=0
        )
        out_ref[:, few * m : few * m + few, :] = both.T.reshape(LANES // few, few, LANES)


def mixed_kernel(few, k_ref, v_ref, rim_ref, taps_ref, held_ref, out_ref):
    del held_ref
    key_seq = causal(k_ref[...], rim_ref[2:4], taps_ref[1])
    value_seq = causal(v_ref[...], rim_ref[4:6], taps_ref[2])
    mixed_in = key_seq * value_seq
    for h in range(mixed_in.shape[0] // LANES):
        turned = mixed_in[LANES * h : LANES * h + LANES].T
        out_ref[:, few * h : few * h + few, :] = turned.reshape(LANES // few, few, LANES)


def local_kernel(q_ref, k_ref, v_ref, rim_ref, taps_ref, gain_ref, query_ref, direct_ref):
    query_seq = causal(q_ref[...], rim_ref[0:2], taps_ref[0])
    key_seq = causal(k_ref[...], rim_ref[2:4], taps_ref[1])
    value_seq = causal(v_ref[...], rim_ref[4:6], taps_ref[2])
    query_ref[...] = query_seq
    direct_ref[...] = query_seq * (gain_ref[...] * (key_seq * value_seq))


def gate_kernel(conv_ref, query_ref, direct_ref, out_ref):
    few, rows = conv_ref.shape[1:]
    conv = conv_ref[...].reshape(conv_ref.shape[0] * few, rows)
    out_ref[...] = query_ref[...] * conv.T + direct_ref[...]


def conv_kernel(
    parts, few, chunks, in_ref, w1_ref, w2_ref, cos_ref, sin_ref, fh_ref, fl_ref, bh_ref, bl_ref,
    out_ref, yh, yl, ph, pq,
):
    devices = in_ref.shape[0] // parts
    outer = 2 * devices
    rows = out_ref.shape[2]
    base = few * chunks
    cosines, sines = cos_ref[...], sin_ref[...]

    def keep(high_ref, low_ref, at, real, imag):
        for col, x in ((0, real), (rows, imag)):
            high, low = split(x)
            high_ref[at : at + outer, col : col + rows] = high
            low_ref[at : at + outer, col : col + rows] = low

    for c in range(few):
        for q in range(parts):
            block = slice(q * devices, (q + 1) * devices)
            x = jnp.concatenate(
                [in_ref[block, base + few * h + c, :] for h in range(rows // LANES)], axis=1
            )
            high, low = split(x)
            y = dot(w1_ref[...], jnp.concatenate([high, low, high], axis=0))
            re, im = y[:outer], y[outer:]
            keep(yh, yl, (c * parts + q) * outer, re * cosines + im * sines, im * cosines - re * sines)

    group = 4
    step = group * parts * outer
    for g in range(few // group):
        span = slice(g * step, (g + 1) * step)
        spec = dot(yh[span], fh_ref[...]) + dot(yl[span], fh_ref[...]) + dot(yh[span], fl_ref[...])
        for i in range(group):
            c = g * group + i
            resp = jnp.concatenate([in_ref[:, few * m + c, :] for m in range(chunks)], axis=0).T
            h_re = jnp.concatenate([resp[:outer], resp[outer : 2 * outer]], axis=1)
            h_im = jnp.concatenate([resp[2 * outer : 3 * outer], resp[3 * outer :]], axis=1)
            for q in range(parts):
                at = (i * parts + q) * outer
                re, im = spec[at : at + outer, :rows], spec[at : at + outer, rows:]
                keep(ph, pq, g * step + at, re * h_re - im * h_im, re * h_im + im * h_re)
        undo = dot(ph[span], bh_ref[...]) + dot(pq[span], bh_ref[...]) + dot(ph[span], bl_ref[...])
        for i in range(group):
            c = g * group + i
            for q in range(parts):
                at = (i * parts + q) * outer
                re, im = undo[at : at + outer, :rows], undo[at : at + outer, rows:]
                turned = jnp.concatenate([re * cosines - im * sines, im * cosines + re * sines], axis=0)
                high, low = split(turned)
                y = dot(w2_ref[...], jnp.concatenate([high, low, high], axis=0))
                out_ref[q * devices : (q + 1) * devices, c, :] = y


def per_device_tiled(q_proj, k_proj, v_proj, short_filter, skip_gain, filter_spec):
    parts, devices = lax.axis_size("dp"), lax.axis_size("ctx")
    everyone = parts * devices
    rows, channels = q_proj.shape
    few = channels // everyone
    chunks = 2 * rows // parts // 64
    halves = rows // LANES
    blocks = channels // LANES
    near = LANES // few
    depth = few * (chunks + halves)
    outer = 2 * devices
    whole = pl.BlockSpec(memory_space=pltpu.VMEM)

    tails = jnp.concatenate([q_proj[-2:], k_proj[-2:], v_proj[-2:]], axis=0)
    rim = shifted(tails, "ctx", 1)

    part = lax.axis_index("dp").reshape(1)
    packed = jax.ShapeDtypeStruct((everyone, depth, LANES), F32)
    held = pl.pallas_call(
        functools.partial(spec_kernel, few),
        out_shape=packed,
        grid_spec=pltpu.PrefetchScalarGridSpec(
            num_scalar_prefetch=1,
            grid=(blocks,),
            in_specs=[pl.BlockSpec((2, 64 * chunks, LANES), lambda i, s: (0, s[0], i))],
            out_specs=pl.BlockSpec((near, few * chunks, LANES), lambda i, s: (i, 0, 0)),
        ),
        cost_estimate=pl.CostEstimate(flops=0, bytes_accessed=1 << 21, transcendentals=0),
    )(part, filter_spec)

    column = pl.BlockSpec((rows, LANES), lambda i: (0, i))
    rim_spec = pl.BlockSpec((6, LANES), lambda i: (0, i))
    taps_spec = pl.BlockSpec((3, 3, LANES), lambda i: (0, 0, i))
    sent = pl.pallas_call(
        functools.partial(mixed_kernel, few),
        out_shape=packed,
        grid=(blocks,),
        in_specs=[column, column, rim_spec, taps_spec, pl.BlockSpec(memory_space=pl.ANY)],
        out_specs=pl.BlockSpec((near, few * halves, LANES), lambda i: (i, chunks // halves, 0)),
        input_output_aliases={4: 0},
        cost_estimate=pl.CostEstimate(flops=0, bytes_accessed=3 << 19, transcendentals=0),
    )(k_proj, v_proj, rim, short_filter, held)

    come = lax.all_to_all(sent, ("dp", "ctx"), 0, 0, tiled=True)

    query_seq, direct = pl.pallas_call(
        local_kernel,
        out_shape=[jax.ShapeDtypeStruct((rows, channels), F32)] * 2,
        grid=(blocks,),
        in_specs=[column, column, column, rim_spec, taps_spec, pl.BlockSpec((1, LANES), lambda i: (0, i))],
        out_specs=[column, column],
        cost_estimate=pl.CostEstimate(flops=0, bytes_accessed=5 << 19, transcendentals=0),
    )(q_proj, k_proj, v_proj, rim, short_filter, skip_gain[None, :])

    total = few * parts * outer
    conv = pl.pallas_call(
        functools.partial(conv_kernel, parts, few, chunks),
        out_shape=jax.ShapeDtypeStruct((everyone, few, rows), F32),
        in_specs=[whole] * 9,
        out_specs=whole,
        scratch_shapes=[pltpu.VMEM((total, 2 * rows), BF16)] * 4,
        compiler_params=pltpu.CompilerParams(vmem_limit_bytes=48 << 20),
        cost_estimate=pl.CostEstimate(flops=0, bytes_accessed=4 << 20, transcendentals=0),
    )(come, *(jnp.asarray(t) for t in tables(parts, devices, rows)))

    back = lax.all_to_all(conv, ("dp", "ctx"), 0, 0, tiled=True)
    return pl.pallas_call(
        gate_kernel,
        out_shape=jax.ShapeDtypeStruct((rows, channels), F32),
        grid=(blocks,),
        in_specs=[pl.BlockSpec((near, few, rows), lambda i: (i, 0, 0)), column, column],
        out_specs=column,
        cost_estimate=pl.CostEstimate(flops=0, bytes_accessed=1 << 21, transcendentals=0),
    )(back, query_seq, direct)


def fits_tiles(mesh, rows, channels):
    parts, devices = mesh.shape["dp"], mesh.shape["ctx"]
    few, rest = divmod(channels, parts * devices)
    chunks = 2 * rows // parts // 64
    return (
        rest == 0
        and few % 8 == 0
        and 2 * devices == 32
        and rows % LANES == 0
        and parts * devices * chunks == LANES
        and chunks % (rows // LANES) == 0
    )


def solution(mesh):
    placed = (
        P(("dp", "ctx"), None),
        P(("dp", "ctx"), None),
        P(("dp", "ctx"), None),
        P(),
        P(),
        P(None, "ctx", None),
    )

    def per_device(q_proj, *rest):
        form = per_device_tiled if fits_tiles(mesh, *q_proj.shape) else per_device_general
        return form(q_proj, *rest)

    return jax.shard_map(
        per_device, mesh=mesh, in_specs=placed, out_specs=P(("dp", "ctx"), None), check_vma=False
    )
```

time: 129 us -> 88 us (0.68)
  blocking collectives: 0 us -> 45.6 us
  waiting for transfers between devices: 55.2 us -> 12.2 us
  matrix products: 21.4 us -> 0 us
  Pallas kernels: 0 us -> 20.8 us
  starting transfers between devices: 25.2 us -> 4.96 us
  local copies, waits for them, and re-layouts: 18.4 us -> 3.64 us
  other arithmetic: 7.67 us -> 0.01 us
    all_to_all x0 -> x1, blocking collectives: none -> 45.6 us  [per_device_tiled(): come = lax.all_to_all(sent, ('dp', 'ctx'), 0, 0, tiled=True)]
    all_to_all x3 -> x1, waiting for transfers between devices: 55.2 us -> 12.2 us  [per_device_tiled(): back = lax.all_to_all(conv, ('dp', 'ctx'), 0, 0, tiled=True)]
    pallas_call x0 -> x5, Pallas kernels: none -> 20.8 us  [the longest x1 6.26 us: per_device_tiled(): pl.pallas_call(functools.partial(conv_kernel, parts, few, chunks), out_sh...]
    all_to_all x3 -> x1, starting transfers between devices: 22.8 us -> 2.61 us  [per_device_tiled(): back = lax.all_to_all(conv, ('dp', 'ctx'), 0, 0, tiled=True)]
    dot_general x8 -> x0, matrix products: 15.3 us -> none  [the longest x1 4.09 us: channel_conv(): jnp.einsum('kac,aj->kjc', turned_re, last_sin, precision=precise_mode)]
    unnamed x4 -> x0, matrix products: 6 us -> none
    unnamed x13 -> x20, local copies, waits for them, and re-layouts: 6.31 us -> 1.48 us
    mul x2 -> x0, other arithmetic: 4.7 us -> none  [the longest x1 2.95 us: per_device(): mixed_in = key_seq * value_seq]
  transfers between devices with their start and end apart: 4 -> 2, of which waited for: 3 -> 1; matrix products, arithmetic and copies ran while one was open for 14% -> 0% of each run, Pallas kernels for 0% -> 8%
where the time goes in v1:
time: 88 us; the launch traced here: 87.3 us
  blocking collectives  45.6 us (52%)
  Pallas kernels  20.8 us (24%)
  waiting for transfers between devices  12.2 us (14%)
  starting transfers between devices  4.96 us (6%)
  local copies, waits for them, and re-layouts  3.64 us (4%)
    all_to_all x1, blocking collectives, per_device_tiled(): come = lax.all_to_all(sent, ('dp', 'ctx'), 0, 0, tiled=True)  45.6 us
    all_to_all x1, waiting for transfers between devices, per_device_tiled(): back = lax.all_to_all(conv, ('dp', 'ctx'), 0, 0, tiled=True)  12.2 us
    pallas_call x1, Pallas kernels, per_device_tiled(): pl.pallas_call(functools.partial(conv_kernel, parts, few, chunks), out_sh...  6.26 us
    pallas_call x1, Pallas kernels, per_device_tiled(): pl.pallas_call(local_kernel, out_shape=[jax.ShapeDtypeStruct((rows, chann...  3.72 us
    pallas_call x1, Pallas kernels, per_device_tiled(): pl.pallas_call(functools.partial(spec_kernel, few), out_shape=packed, gri...  3.65 us
    pallas_call x1, Pallas kernels, per_device_tiled(): pl.pallas_call(functools.partial(mixed_kernel, few), out_shape=packed, gr...  3.62 us
    pallas_call x1, Pallas kernels, per_device_tiled(): pl.pallas_call(gate_kernel, out_shape=jax.ShapeDtypeStruct((rows, channel...  3.59 us
    all_to_all x1, starting transfers between devices, per_device_tiled(): back = lax.all_to_all(conv, ('dp', 'ctx'), 0, 0, tiled=True)  2.61 us
  transfers between devices with their start and end apart: 2, of which 1 were waited for; matrix products, arithmetic and copies ran while one was open for 0% of the time, Pallas kernels for 8%

profile of v1, /device:TPU:0, one launch (start us, length us, event | category | flops | bytes accessed | tf_op | source)
XLA Modules:
  0.0 87.3 jit_solution(16566868354447525094)
XLA Ops:
  0.0 0.7 slice.11
  0.7 0.7 slice.10
  1.4 0.7 slice.9
  2.2 2.4 %collective-permute-start = (f32[6,512]{1,0:T(8,128)S(1)}, f32[6,512]{1,0:T(8,128)S(1)}, u32[]{:S(2)}, u32[]{:S(2)}) collective-permute-start(f32[6,512]{1,0:T(8,128)S(1)} %pad_maximum_fusion), channel_id=1, source_target_pairs={{0,1},{1,2},{2,3},{3,4},{4,5},{5,6},{6,7},{7,8},{8,9},{9,10},{10,1... | collective-permute-start | bytes 36872 | tf_op jit(solution)/shard_map/ppermute | solution.py:26
  4.5 3.6 %shard_map.136.held_ref = f32[32,96,128]{2,1,0:T(8,128)} custom-call(s32[1]{0:T(128)} %bitcast.part_ref, f32[2,512,512]{2,1,0:T(8,128)} %spec_ref.1), custom_call_target="tpu_custom_call" | custom-call | bytes 2097152 | tf_op jit(solution)/shard_map/pallas_call | solution.py:238
  8.2 0.0 collective-permute-done.rim_ref
  8.2 0.0 copy-start.9
  8.2 0.6 copy-done.9
  8.8 3.6 %shard_map.137 = f32[32,96,128]{2,1,0:T(8,128)} custom-call(f32[256,512]{1,0:T(8,128)} %k_ref.3, f32[256,512]{1,0:T(8,128)} %v_ref.3, f32[6,512]{1,0:T(8,128)} %copy-done.9, f32[3,3,512]{2,1,0:T(4,128)} %taps_ref.3, f32[32,96,128]{2,1,0:T(8,128)} %shard_map.136.held_ref), custom_call_target="tpu_custom_call", output_to_operand_aliasing={{}: (4, {})} | custom-call | bytes 1572864 | tf_op jit(solution)/shard_map/pallas_call | solution.py:253
  12.4 0.0 copy-start
  12.4 0.0 copy-start.1
  12.4 0.0 copy-start.2
  12.4 0.0 copy-start.3
  12.4 0.0 copy-start.4
  12.5 0.0 copy-start.5
  12.5 0.0 copy-start.6
  12.5 0.0 copy-start.7
  12.5 45.6 %all_to_all.10.in_ref = f32[32,96,128]{2,1,0:T(8,128)S(1)} all-to-all(f32[32,96,128]{2,1,0:T(8,128)} %shard_map.137), channel_id=1, replica_groups=mesh['dp'=2,'ctx'=16] {'dp','ctx'}, dimensions={0} | all-to-all | bytes 3145728 | tf_op jit(solution)/shard_map/all_to_all | solution.py:263
  58.1 0.0 copy-done
  58.1 0.0 copy-done.1
  58.1 0.0 copy-done.2
  58.1 0.0 copy-done.3
  58.1 0.0 copy-done.4
  58.1 0.0 copy-done.5
  58.1 0.0 copy-done.6
  58.1 0.0 copy-done.7
  58.1 6.3 %shard_map.138 = f32[32,16,256]{2,1,0:T(8,128)} custom-call(f32[32,96,128]{2,1,0:T(8,128)S(1)} %all_to_all.10.in_ref, bf16[64,48]{1,0:T(8,128)(2,1)S(1)} %copy-done.6, bf16[16,192]{1,0:T(8,128)(2,1)S(1)} %copy-done.7, f32[32,256]{1,0:T(8,128)S(1)} %copy-done.4, f32[32,256]{1,0:T(8,128)S(1)} %copy-done.5, bf16[512,512]{1,0:T(8,128)(2,1)S(1)} %copy-done, ...), custom_call_target="tpu_custom_call" | custom-call | bytes 4194304 | tf_op jit(solution)/shard_map/pallas_call | solution.py:275
  64.4 2.6 %all-to-all-start.1 = ((f32[32,16,256]{2,1,0:T(8,128)}), f32[32,16,256]{2,1,0:T(8,128)S(1)}, u32[]{:S(2)}, u32[]{:S(2)}) async-start(f32[32,16,256]{2,1,0:T(8,128)} %shard_map.138), calls=%async_computation.1 | async-start | bytes 1048576 | tf_op jit(solution)/shard_map/all_to_all | solution.py:285
  67.0 3.7 %shard_map.139 = (f32[256,512]{1,0:T(8,128)}, f32[256,512]{1,0:T(8,128)}) custom-call(f32[256,512]{1,0:T(8,128)} %q_ref.1, f32[256,512]{1,0:T(8,128)} %k_ref.3, f32[256,512]{1,0:T(8,128)} %v_ref.3, f32[6,512]{1,0:T(8,128)} %copy-done.9, f32[3,3,512]{2,1,0:T(4,128)} %taps_ref.3, f32[1,512]{1,0:T(1,128)} %bitcast.2), custom_call_target="tpu_custom_call" | custom-call | bytes 2621440 | tf_op jit(solution)/shard_map/pallas_call | solution.py:265
  70.7 12.2 %all-to-all-done.1.conv_ref = f32[32,16,256]{2,1,0:T(8,128)S(1)} async-done(((f32[32,16,256]{2,1,0:T(8,128)}), f32[32,16,256]{2,1,0:T(8,128)S(1)}, u32[]{:S(2)}, u32[]{:S(2)}) %all-to-all-start.1) | async-done | bytes 524320 | tf_op jit(solution)/shard_map/all_to_all | solution.py:285
  82.9 0.8 copy-done.8
  83.7 3.6 %shard_map.140 = f32[256,512]{1,0:T(8,128)} custom-call(f32[32,16,256]{2,1,0:T(8,128)} %copy-done.8, f32[256,512]{1,0:T(8,128)} %get-tuple-element.7.query_ref, f32[256,512]{1,0:T(8,128)} %get-tuple-element.8.direct_ref), custom_call_target="tpu_custom_call" | custom-call | bytes 2097152 | tf_op jit(solution)/shard_map/pallas_call | solution.py:286
  (2 shorter events, 0.0 us)
Async XLA Ops:
  2.2 6.0 %collective-permute-start = (f32[6,512]{1,0:T(8,128)S(1)}, f32[6,512]{1,0:T(8,128)S(1)}, u32[]{:S(2)}, u32[]{:S(2)}) collective-permute-start(f32[6,512]{1,0:T(8,128)S(1)} %pad_maximum_fusion), channel_id=1, source_target_pairs={{0,1},{1,2},{2,3},{3,4},{4,5},{5,6},{6,7},{7,8},{8,9},{9,10},{10,1... | collective-permute-start | bytes 36872 | tf_op jit(solution)/shard_map/ppermute | solution.py:26
  8.2 0.6 copy-start.9
  12.4 45.6 %copy-start = (bf16[512,512]{1,0:T(8,128)(2,1)S(1)}, bf16[512,512]{1,0:T(8,128)(2,1)}, u32[]{:S(2)}) copy-start(bf16[512,512]{1,0:T(8,128)(2,1)} %constant.26.clone.fh_ref) | copy-start | bytes 1572868
  12.4 45.6 %copy-start.1 = (bf16[512,512]{1,0:T(8,128)(2,1)S(1)}, bf16[512,512]{1,0:T(8,128)(2,1)}, u32[]{:S(2)}) copy-start(bf16[512,512]{1,0:T(8,128)(2,1)} %constant.27.clone.fl_ref) | copy-start | bytes 1572868
  12.4 45.6 %copy-start.2 = (bf16[512,512]{1,0:T(8,128)(2,1)S(1)}, bf16[512,512]{1,0:T(8,128)(2,1)}, u32[]{:S(2)}) copy-start(bf16[512,512]{1,0:T(8,128)(2,1)} %constant.28.clone.bh_ref) | copy-start | bytes 1572868
  12.4 45.6 %copy-start.3 = (bf16[512,512]{1,0:T(8,128)(2,1)S(1)}, bf16[512,512]{1,0:T(8,128)(2,1)}, u32[]{:S(2)}) copy-start(bf16[512,512]{1,0:T(8,128)(2,1)} %constant.29.clone.bl_ref) | copy-start | bytes 1572868
  12.4 45.6 %copy-start.4 = (f32[32,256]{1,0:T(8,128)S(1)}, f32[32,256]{1,0:T(8,128)}, u32[]{:S(2)}) copy-start(f32[32,256]{1,0:T(8,128)} %constant.24.clone.cos_ref) | copy-start | bytes 98308
  12.5 45.6 %copy-start.5 = (f32[32,256]{1,0:T(8,128)S(1)}, f32[32,256]{1,0:T(8,128)}, u32[]{:S(2)}) copy-start(f32[32,256]{1,0:T(8,128)} %constant.25.clone.sin_ref) | copy-start | bytes 98308
  12.5 45.6 %copy-start.6 = (bf16[64,48]{1,0:T(8,128)(2,1)S(1)}, bf16[64,48]{1,0:T(8,128)(2,1)}, u32[]{:S(2)}) copy-start(bf16[64,48]{1,0:T(8,128)(2,1)} %constant.22.clone.w1_ref) | copy-start | bytes 18436
  12.5 45.6 %copy-start.7 = (bf16[16,192]{1,0:T(8,128)(2,1)S(1)}, bf16[16,192]{1,0:T(8,128)(2,1)}, u32[]{:S(2)}) copy-start(bf16[16,192]{1,0:T(8,128)(2,1)} %constant.23.clone.w2_ref) | copy-start | bytes 18436
  64.4 18.5 %all-to-all-start.1 = ((f32[32,16,256]{2,1,0:T(8,128)}), f32[32,16,256]{2,1,0:T(8,128)S(1)}, u32[]{:S(2)}, u32[]{:S(2)}) async-start(f32[32,16,256]{2,1,0:T(8,128)} %shard_map.138), calls=%async_computation.1 | async-start | bytes 1048576 | tf_op jit(solution)/shard_map/all_to_all | solution.py:285
  82.9 0.8 copy-start.8

commit v2 on v1

--- a/solution.py
+++ b/solution.py
@@ -131,37 +131,72 @@
     return taps[0:1] * x + taps[1:2] * one + taps[2:3] * two
 
 
-def spec_kernel(few, part_ref, spec_ref, out_ref):
-    del part_ref
-    for m in range(spec_ref.shape[1] // 64):
-        both = jnp.concatenate(
-            [spec_ref[0, 64 * m : 64 * m + 64], spec_ref[1, 64 * m : 64 * m + 64]], axis=0
+def tail_kernel(q_ref, k_ref, v_ref, out_ref, buf, sems):
+    rows = q_ref.shape[0]
+    copies = [
+        pltpu.make_async_copy(ref.at[rows - 8 : rows], buf.at[i], sems.at[i])
+        for i, ref in enumerate((q_ref, k_ref, v_ref))
+    ]
+    for copy in copies:
+        copy.start()
+    for i, copy in enumerate(copies):
+        copy.wait()
+        out_ref[2 * i : 2 * i + 2] = buf[i, 6:8]
+
+
+def spec_kernel(few, chunks, part_ref, spec_ref, out_ref, buf, sems):
+    blocks = spec_ref.shape[2] // LANES
+    near = LANES // few
+    start = pl.multiple_of(part_ref[0] * (64 * chunks), 64 * chunks)
+    copies = [
+        pltpu.make_async_copy(
+            spec_ref.at[:, pl.ds(start + 64 * m, 64), :], buf.at[m], sems.at[m]
         )
-        out_ref[:, few * m : few * m + few, :] = both.T.reshape(LANES // few, few, LANES)
-
-
-def mixed_kernel(few, k_ref, v_ref, rim_ref, taps_ref, held_ref, out_ref):
+        for m in range(chunks)
+    ]
+    for copy in copies:
+        copy.start()
+    for m, copy in enumerate(copies):
+        copy.wait()
+        for i in range(blocks):
+            both = buf[m, :, :, LANES * i : LANES * i + LANES].reshape(LANES, LANES)
+            out_ref[near * i : near * i + near, few * m : few * m + few, :] = both.T.reshape(near, few, LANES)
+
+
+def mixed_kernel(few, chunks, k_ref, v_ref, rim_ref, taps_ref, held_ref, out_ref):
     del held_ref
-    key_seq = causal(k_ref[...], rim_ref[2:4], taps_ref[1])
-    value_seq = causal(v_ref[...], rim_ref[4:6], taps_ref[2])
-    mixed_in = key_seq * value_seq
-    for h in range(mixed_in.shape[0] // LANES):
-        turned = mixed_in[LANES * h : LANES * h + LANES].T
-        out_ref[:, few * h : few * h + few, :] = turned.reshape(LANES // few, few, LANES)
+    near = LANES // few
+    base = few * chunks
+    for i in range(k_ref.shape[1] // LANES):
+        col = slice(LANES * i, LANES * i + LANES)
+        key_seq = causal(k_ref[:, col], rim_ref[2:4, col], taps_ref[1, :, col])
+        value_seq = causal(v_ref[:, col], rim_ref[4:6, col], taps_ref[2, :, col])
+        mixed_in = key_seq * value_seq
+        for h in range(mixed_in.shape[0] // LANES):
+            turned = mixed_in[LANES * h : LANES * h + LANES].T
+            at = base + few * h
+            out_ref[near * i : near * i + near, at : at + few, :] = turned.reshape(near, few, LANES)
 
 
 def local_kernel(q_ref, k_ref, v_ref, rim_ref, taps_ref, gain_ref, query_ref, direct_ref):
-    query_seq = causal(q_ref[...], rim_ref[0:2], taps_ref[0])
-    key_seq = causal(k_ref[...], rim_ref[2:4], taps_ref[1])
-    value_seq = causal(v_ref[...], rim_ref[4:6], taps_ref[2])
-    query_ref[...] = query_seq
-    direct_ref[...] = query_seq * (gain_ref[...] * (key_seq * value_seq))
+    for i in range(q_ref.shape[1] // LANES):
+        col = slice(LANES * i, LANES * i + LANES)
+        query_seq = causal(q_ref[:, col], rim_ref[0:2, col], taps_ref[0, :, col])
+        key_seq = causal(k_ref[:, col], rim_ref[2:4, col], taps_ref[1, :, col])
+        value_seq = causal(v_ref[:, col], rim_ref[4:6, col], taps_ref[2, :, col])
+        query_ref[:, col] = query_seq
+        direct_ref[:, col] = query_seq * (gain_ref[:, col] * (key_seq * value_seq))
 
 
 def gate_kernel(conv_ref, query_ref, direct_ref, out_ref):
-    few, rows = conv_ref.shape[1:]
-    conv = conv_ref[...].reshape(conv_ref.shape[0] * few, rows)
-    out_ref[...] = query_ref[...] * conv.T + direct_ref[...]
+    few = conv_ref.shape[1]
+    near = LANES // few
+    for i in range(conv_ref.shape[0] // near):
+        col = slice(LANES * i, LANES * i + LANES)
+        for h in range(conv_ref.shape[2] // LANES):
+            row = slice(LANES * h, LANES * h + LANES)
+            conv = conv_ref[near * i : near * i + near, :, row].reshape(LANES, LANES)
+            out_ref[row, col] = query_ref[row, col] * conv.T + direct_ref[row, col]
 
 
 def conv_kernel(
@@ -224,39 +259,41 @@
     few = channels // everyone
     chunks = 2 * rows // parts // 64
     halves = rows // LANES
-    blocks = channels // LANES
-    near = LANES // few
     depth = few * (chunks + halves)
     outer = 2 * devices
     whole = pl.BlockSpec(memory_space=pltpu.VMEM)
 
-    tails = jnp.concatenate([q_proj[-2:], k_proj[-2:], v_proj[-2:]], axis=0)
+    small = pltpu.CompilerParams(vmem_limit_bytes=16 << 20)
+    in_hbm = pl.BlockSpec(memory_space=pltpu.HBM)
+    tails = pl.pallas_call(
+        tail_kernel,
+        out_shape=jax.ShapeDtypeStruct((6, channels), F32),
+        in_specs=[in_hbm] * 3,
+        out_specs=whole,
+        compiler_params=small,
+        scratch_shapes=[pltpu.VMEM((3, 8, channels), F32), pltpu.SemaphoreType.DMA((3,))],
+    )(q_proj, k_proj, v_proj)
     rim = shifted(tails, "ctx", 1)
 
     part = lax.axis_index("dp").reshape(1)
     packed = jax.ShapeDtypeStruct((everyone, depth, LANES), F32)
     held = pl.pallas_call(
-        functools.partial(spec_kernel, few),
+        functools.partial(spec_kernel, few, chunks),
         out_shape=packed,
-        grid_spec=pltpu.PrefetchScalarGridSpec(
-            num_scalar_prefetch=1,
-            grid=(blocks,),
-            in_specs=[pl.BlockSpec((2, 64 * chunks, LANES), lambda i, s: (0, s[0], i))],
-            out_specs=pl.BlockSpec((near, few * chunks, LANES), lambda i, s: (i, 0, 0)),
-        ),
+        in_specs=[pl.BlockSpec(memory_space=pltpu.SMEM), in_hbm],
+        out_specs=whole,
+        scratch_shapes=[pltpu.VMEM((chunks, 2, 64, channels), F32), pltpu.SemaphoreType.DMA((chunks,))],
+        compiler_params=small,
         cost_estimate=pl.CostEstimate(flops=0, bytes_accessed=1 << 21, transcendentals=0),
     )(part, filter_spec)
 
-    column = pl.BlockSpec((rows, LANES), lambda i: (0, i))
-    rim_spec = pl.BlockSpec((6, LANES), lambda i: (0, i))
-    taps_spec = pl.BlockSpec((3, 3, LANES), lambda i: (0, 0, i))
     sent = pl.pallas_call(
-        functools.partial(mixed_kernel, few),
+        functools.partial(mixed_kernel, few, chunks),
         out_shape=packed,
-        grid=(blocks,),
-        in_specs=[column, column, rim_spec, taps_spec, pl.BlockSpec(memory_space=pl.ANY)],
-        out_specs=pl.BlockSpec((near, few * halves, LANES), lambda i: (i, chunks // halves, 0)),
+        in_specs=[whole] * 5,
+        out_specs=whole,
         input_output_aliases={4: 0},
+        compiler_params=small,
         cost_estimate=pl.CostEstimate(flops=0, bytes_accessed=3 << 19, transcendentals=0),
     )(k_proj, v_proj, rim, short_filter, held)
 
@@ -265,9 +302,9 @@
     query_seq, direct = pl.pallas_call(
         local_kernel,
         out_shape=[jax.ShapeDtypeStruct((rows, channels), F32)] * 2,
-        grid=(blocks,),
-        in_specs=[column, column, column, rim_spec, taps_spec, pl.BlockSpec((1, LANES), lambda i: (0, i))],
-        out_specs=[column, column],
+        in_specs=[whole] * 6,
+        out_specs=[whole] * 2,
+        compiler_params=small,
         cost_estimate=pl.CostEstimate(flops=0, bytes_accessed=5 << 19, transcendentals=0),
     )(q_proj, k_proj, v_proj, rim, short_filter, skip_gain[None, :])
 
@@ -278,7 +315,7 @@
         in_specs=[whole] * 9,
         out_specs=whole,
         scratch_shapes=[pltpu.VMEM((total, 2 * rows), BF16)] * 4,
-        compiler_params=pltpu.CompilerParams(vmem_limit_bytes=48 << 20),
+        compiler_params=small,
         cost_estimate=pl.CostEstimate(flops=0, bytes_accessed=4 << 20, transcendentals=0),
     )(come, *(jnp.asarray(t) for t in tables(parts, devices, rows)))
 
@@ -286,9 +323,9 @@
     return pl.pallas_call(
         gate_kernel,
         out_shape=jax.ShapeDtypeStruct((rows, channels), F32),
-        grid=(blocks,),
-        in_specs=[pl.BlockSpec((near, few, rows), lambda i: (i, 0, 0)), column, column],
-        out_specs=column,
+        in_specs=[whole] * 3,
+        out_specs=whole,
+        compiler_params=small,
         cost_estimate=pl.CostEstimate(flops=0, bytes_accessed=1 << 21, transcendentals=0),
     )(back, query_seq, direct)
 

time: 88 us -> 80.6 us (0.916)
  Pallas kernels: 20.8 us -> 8.92 us
  waiting for transfers between devices: 12.2 us -> 15.4 us
  local copies, waits for them, and re-layouts: 3.64 us -> 5.31 us
    pallas_call x2 -> x3, Pallas kernels: 7.26 us -> 1.12 us  [the longest x1 0.65 us: per_device_tiled(): pl.pallas_call(functools.partial(spec_kernel, few, chunks), out_shape=pac...]
    unnamed x20 -> x34, local copies, waits for them, and re-layouts: 1.48 us -> 5.31 us
    pallas_call x1, Pallas kernels: 3.72 us -> 0.52 us  [per_device_tiled(): pl.pallas_call(local_kernel, out_shape=[jax.ShapeDtypeStruct((rows, chann...]
    all_to_all x1, waiting for transfers between devices: 12.2 us -> 15.3 us  [per_device_tiled(): back = lax.all_to_all(conv, ('dp', 'ctx'), 0, 0, tiled=True)]
    pallas_call x1, Pallas kernels: 3.59 us -> 1 us  [per_device_tiled(): pl.pallas_call(gate_kernel, out_shape=jax.ShapeDtypeStruct((rows, channel...]
    slice x3 -> x0, local copies, waits for them, and re-layouts: 2.16 us -> none  [per_device_tiled(): tails = jnp.concatenate([q_proj[-2:], k_proj[-2:], v_proj[-2:]], axis=0)]
  transfers between devices with their start and end apart: 2 -> 2, of which waited for: 1 -> 1; matrix products, arithmetic and copies ran while one was open for 0% -> 0% of each run, Pallas kernels for 8% -> 1%
where the time goes in v2:
time: 80.6 us; the launch traced here: 80.2 us
  blocking collectives  45.4 us (56%)
  waiting for transfers between devices  15.4 us (19%)
  Pallas kernels  8.92 us (11%)
  local copies, waits for them, and re-layouts  5.31 us (7%)
  starting transfers between devices  4.96 us (6%)
    all_to_all x1, blocking collectives, per_device_tiled(): come = lax.all_to_all(sent, ('dp', 'ctx'), 0, 0, tiled=True)  45.4 us
    all_to_all x1, waiting for transfers between devices, per_device_tiled(): back = lax.all_to_all(conv, ('dp', 'ctx'), 0, 0, tiled=True)  15.3 us
    pallas_call x1, Pallas kernels, per_device_tiled(): pl.pallas_call(functools.partial(conv_kernel, parts, few, chunks), out_sh...  6.28 us
    unnamed x34, local copies, waits for them, and re-layouts  5.31 us
    all_to_all x1, starting transfers between devices, per_device_tiled(): back = lax.all_to_all(conv, ('dp', 'ctx'), 0, 0, tiled=True)  2.61 us
    ppermute x1, starting transfers between devices, shifted(): return lax.ppermute(block, axis, route)  2.36 us
  transfers between devices with their start and end apart: 2, of which 1 were waited for; matrix products, arithmetic and copies ran while one was open for 0% of the time, Pallas kernels for 1%

profile of v2, /device:TPU:0, one launch (start us, length us, event | category | flops | bytes accessed | tf_op | source)
XLA Modules:
  0.0 80.2 jit_solution(4440366735986194954)
XLA Ops:
  0.0 1.0 %copy-done = f32[256,512]{1,0:T(8,128)S(1)} copy-done((f32[256,512]{1,0:T(8,128)S(1)}, f32[256,512]{1,0:T(8,128)}, u32[]{:S(2)}) %copy-start) | copy-done | bytes 524312
  1.0 1.0 %copy-done.2 = f32[256,512]{1,0:T(8,128)S(1)} copy-done((f32[256,512]{1,0:T(8,128)S(1)}, f32[256,512]{1,0:T(8,128)}, u32[]{:S(2)}) %copy-start.2) | copy-done | bytes 524312
  2.1 1.0 %copy-done.4 = f32[256,512]{1,0:T(8,128)S(1)} copy-done((f32[256,512]{1,0:T(8,128)S(1)}, f32[256,512]{1,0:T(8,128)}, u32[]{:S(2)}) %copy-start.4) | copy-done | bytes 524312
  3.1 0.1 shard_map.136
  3.2 2.4 %collective-permute-start = (f32[6,512]{1,0:T(8,128)S(1)}, f32[6,512]{1,0:T(8,128)S(1)}, u32[]{:S(2)}, u32[]{:S(2)}) collective-permute-start(f32[6,512]{1,0:T(8,128)S(1)} %shard_map.136), channel_id=1, source_target_pairs={{0,1},{1,2},{2,3},{3,4},{4,5},{5,6},{6,7},{7,8},{8,9},{9,10},{10,1... | collective-permute-start | bytes 36872 | tf_op jit(solution)/shard_map/ppermute | solution.py:26
  5.6 0.0 copy-start.6
  5.6 1.6 %copy-done.6 = f32[2,512,512]{2,1,0:T(8,128)S(1)} copy-done((f32[2,512,512]{2,1,0:T(8,128)S(1)}, f32[2,512,512]{2,1,0:T(8,128)}, u32[]{:S(2)}) %copy-start.6) | copy-done | bytes 2097176
  7.2 0.6 shard_map.137.held_ref
  7.8 0.0 collective-permute-done.rim_ref
  7.8 0.4 copy-done.1
  8.2 0.2 copy-done.3
  8.4 0.4 shard_map.138
  8.8 0.0 copy-start.8
  8.8 0.0 copy-start.9
  8.8 0.0 copy-start.10
  8.8 0.0 copy-start.12
  8.8 0.0 copy-start.13
  8.8 0.0 copy-start.14
  8.9 0.0 copy-start.15
  8.9 45.4 %all_to_all.10.in_ref = f32[32,96,128]{2,1,0:T(8,128)S(1)} all-to-all(f32[32,96,128]{2,1,0:T(8,128)S(1)} %shard_map.138), channel_id=1, replica_groups=mesh['dp'=2,'ctx'=16] {'dp','ctx'}, dimensions={0} | all-to-all | bytes 3145728 | tf_op jit(solution)/shard_map/all_to_all | solution.py:300
  54.3 0.0 copy-done.10
  54.3 0.0 copy-done.12
  54.3 0.0 copy-done.13
  54.3 0.0 copy-done.14
  54.3 0.0 copy-done.15
  54.4 0.0 copy-start.5
  54.4 0.0 copy-start.16
  54.4 6.3 %shard_map.139 = f32[32,16,256]{2,1,0:T(8,128)} custom-call(f32[32,96,128]{2,1,0:T(8,128)S(1)} %all_to_all.10.in_ref, bf16[64,48]{1,0:T(8,128)(2,1)S(1)} %copy-done.14, bf16[16,192]{1,0:T(8,128)(2,1)S(1)} %copy-done.15, f32[32,256]{1,0:T(8,128)S(1)} %copy-done.12, f32[32,256]{1,0:T(8,128)S(1)} %copy-done.13, bf16[512,512]{1,0:T(8,128)(2,1)S(1)} %copy-done.7, ...), custom_call_target="tpu_custom_call" | custom-call | bytes 4194304 | tf_op jit(solution)/shard_map/pallas_call | solution.py:312
  60.7 2.6 %all-to-all-start.1 = ((f32[32,16,256]{2,1,0:T(8,128)}), f32[32,16,256]{2,1,0:T(8,128)S(1)}, u32[]{:S(2)}, u32[]{:S(2)}) async-start(f32[32,16,256]{2,1,0:T(8,128)} %shard_map.139), calls=%async_computation.1 | async-start | bytes 1048576 | tf_op jit(solution)/shard_map/all_to_all | solution.py:322
  63.3 0.5 shard_map.140
  63.8 15.3 %all-to-all-done.1.conv_ref = f32[32,16,256]{2,1,0:T(8,128)S(1)} async-done(((f32[32,16,256]{2,1,0:T(8,128)}), f32[32,16,256]{2,1,0:T(8,128)S(1)}, u32[]{:S(2)}, u32[]{:S(2)}) %all-to-all-start.1) | async-done | bytes 524320 | tf_op jit(solution)/shard_map/all_to_all | solution.py:322
  79.2 1.0 %shard_map.141 = f32[256,512]{1,0:T(8,128)} custom-call(f32[32,16,256]{2,1,0:T(8,128)S(1)} %all-to-all-done.1.conv_ref, f32[256,512]{1,0:T(8,128)S(1)} %get-tuple-element.7.query_ref, f32[256,512]{1,0:T(8,128)S(1)} %get-tuple-element.8.direct_ref), custom_call_target="tpu_custom_call" | custom-call | bytes 2097152 | tf_op jit(solution)/shard_map/pallas_call | solution.py:323
  (13 shorter events, 0.0 us)
Async XLA Ops:
  0.0 1.0 %copy-start = (f32[256,512]{1,0:T(8,128)S(1)}, f32[256,512]{1,0:T(8,128)}, u32[]{:S(2)}) copy-start(f32[256,512]{1,0:T(8,128)} %k_ref.5) | copy-start | bytes 1572868
  1.0 1.0 %copy-start.2 = (f32[256,512]{1,0:T(8,128)S(1)}, f32[256,512]{1,0:T(8,128)}, u32[]{:S(2)}) copy-start(f32[256,512]{1,0:T(8,128)} %v_ref.5) | copy-start | bytes 1572868
  2.1 1.0 %copy-start.4 = (f32[256,512]{1,0:T(8,128)S(1)}, f32[256,512]{1,0:T(8,128)}, u32[]{:S(2)}) copy-start(f32[256,512]{1,0:T(8,128)} %q_ref.3) | copy-start | bytes 1572868
  3.2 4.6 %collective-permute-start = (f32[6,512]{1,0:T(8,128)S(1)}, f32[6,512]{1,0:T(8,128)S(1)}, u32[]{:S(2)}, u32[]{:S(2)}) collective-permute-start(f32[6,512]{1,0:T(8,128)S(1)} %shard_map.136), channel_id=1, source_target_pairs={{0,1},{1,2},{2,3},{3,4},{4,5},{5,6},{6,7},{7,8},{8,9},{9,10},{10,1... | collective-permute-start | bytes 36872 | tf_op jit(solution)/shard_map/ppermute | solution.py:26
  5.6 1.6 %copy-start.6 = (f32[2,512,512]{2,1,0:T(8,128)S(1)}, f32[2,512,512]{2,1,0:T(8,128)}, u32[]{:S(2)}) copy-start(f32[2,512,512]{2,1,0:T(8,128)} %spec_ref.1) | copy-start | bytes 6291460
  7.2 1.0 %copy-start.1 = (f32[256,512]{1,0:T(8,128)S(1)}, f32[256,512]{1,0:T(8,128)}, u32[]{:S(2)}) copy-start(f32[256,512]{1,0:T(8,128)} %k_ref.5) | copy-start | bytes 1572868
  7.2 1.2 %copy-start.3 = (f32[256,512]{1,0:T(8,128)S(1)}, f32[256,512]{1,0:T(8,128)}, u32[]{:S(2)}) copy-start(f32[256,512]{1,0:T(8,128)} %v_ref.5) | copy-start | bytes 1572868
  7.2 1.2 %copy-start.11 = (f32[3,3,512]{2,1,0:T(4,128)S(1)}, f32[3,3,512]{2,1,0:T(4,128)}, u32[]{:S(2)}) copy-start(f32[3,3,512]{2,1,0:T(4,128)} %taps_ref.3) | copy-start | bytes 55300
  8.8 45.5 %copy-start.7 = (bf16[512,512]{1,0:T(8,128)(2,1)S(1)}, bf16[512,512]{1,0:T(8,128)(2,1)}, u32[]{:S(2)}) copy-start(bf16[512,512]{1,0:T(8,128)(2,1)} %constant.26.clone.fh_ref) | copy-start | bytes 1572868
  8.8 45.5 %copy-start.8 = (bf16[512,512]{1,0:T(8,128)(2,1)S(1)}, bf16[512,512]{1,0:T(8,128)(2,1)}, u32[]{:S(2)}) copy-start(bf16[512,512]{1,0:T(8,128)(2,1)} %constant.27.clone.fl_ref) | copy-start | bytes 1572868
  8.8 45.5 %copy-start.9 = (bf16[512,512]{1,0:T(8,128)(2,1)S(1)}, bf16[512,512]{1,0:T(8,128)(2,1)}, u32[]{:S(2)}) copy-start(bf16[512,512]{1,0:T(8,128)(2,1)} %constant.28.clone.bh_ref) | copy-start | bytes 1572868
  8.8 45.5 %copy-start.10 = (bf16[512,512]{1,0:T(8,128)(2,1)S(1)}, bf16[512,512]{1,0:T(8,128)(2,1)}, u32[]{:S(2)}) copy-start(bf16[512,512]{1,0:T(8,128)(2,1)} %constant.29.clone.bl_ref) | copy-start | bytes 1572868
  8.8 45.5 %copy-start.12 = (f32[32,256]{1,0:T(8,128)S(1)}, f32[32,256]{1,0:T(8,128)}, u32[]{:S(2)}) copy-start(f32[32,256]{1,0:T(8,128)} %constant.24.clone.cos_ref) | copy-start | bytes 98308
  8.8 45.5 %copy-start.13 = (f32[32,256]{1,0:T(8,128)S(1)}, f32[32,256]{1,0:T(8,128)}, u32[]{:S(2)}) copy-start(f32[32,256]{1,0:T(8,128)} %constant.25.clone.sin_ref) | copy-start | bytes 98308
  8.8 45.5 %copy-start.14 = (bf16[64,48]{1,0:T(8,128)(2,1)S(1)}, bf16[64,48]{1,0:T(8,128)(2,1)}, u32[]{:S(2)}) copy-start(bf16[64,48]{1,0:T(8,128)(2,1)} %constant.22.clone.w1_ref) | copy-start | bytes 18436
  8.9 45.5 %copy-start.15 = (bf16[16,192]{1,0:T(8,128)(2,1)S(1)}, bf16[16,192]{1,0:T(8,128)(2,1)}, u32[]{:S(2)}) copy-start(bf16[16,192]{1,0:T(8,128)(2,1)} %constant.23.clone.w2_ref) | copy-start | bytes 18436
  54.4 8.9 %copy-start.5 = (f32[256,512]{1,0:T(8,128)S(1)}, f32[256,512]{1,0:T(8,128)}, u32[]{:S(2)}) copy-start(f32[256,512]{1,0:T(8,128)} %q_ref.3) | copy-start | bytes 1572868
  54.4 8.9 %copy-start.16 = (f32[512]{0:T(512)S(1)}, f32[512]{0:T(512)}, u32[]{:S(2)}) copy-start(f32[512]{0:T(512)} %param.18) | copy-start | bytes 6148
  60.7 18.5 %all-to-all-start.1 = ((f32[32,16,256]{2,1,0:T(8,128)}), f32[32,16,256]{2,1,0:T(8,128)S(1)}, u32[]{:S(2)}, u32[]{:S(2)}) async-start(f32[32,16,256]{2,1,0:T(8,128)} %shard_map.139), calls=%async_computation.1 | async-start | bytes 1048576 | tf_op jit(solution)/shard_map/all_to_all | solution.py:322

commit v3 on v2

--- a/solution.py
+++ b/solution.py
@@ -131,35 +131,29 @@
     return taps[0:1] * x + taps[1:2] * one + taps[2:3] * two
 
 
-def tail_kernel(q_ref, k_ref, v_ref, out_ref, buf, sems):
+def load_kernel(chunks, part_ref, q_ref, k_ref, v_ref, spec_ref, tail_ref, held_ref, buf, sems, held_sem):
     rows = q_ref.shape[0]
     copies = [
         pltpu.make_async_copy(ref.at[rows - 8 : rows], buf.at[i], sems.at[i])
         for i, ref in enumerate((q_ref, k_ref, v_ref))
     ]
+    span = 64 * chunks
+    start = pl.multiple_of(part_ref[0] * span, span)
+    filter_copy = pltpu.make_async_copy(spec_ref.at[:, pl.ds(start, span), :], held_ref, held_sem)
     for copy in copies:
         copy.start()
+    filter_copy.start()
     for i, copy in enumerate(copies):
         copy.wait()
-        out_ref[2 * i : 2 * i + 2] = buf[i, 6:8]
-
-
-def spec_kernel(few, chunks, part_ref, spec_ref, out_ref, buf, sems):
-    blocks = spec_ref.shape[2] // LANES
+        tail_ref[2 * i : 2 * i + 2] = buf[i, 6:8]
+    filter_copy.wait()
+
+
+def spec_kernel(few, spec_ref, out_ref):
     near = LANES // few
-    start = pl.multiple_of(part_ref[0] * (64 * chunks), 64 * chunks)
-    copies = [
-        pltpu.make_async_copy(
-            spec_ref.at[:, pl.ds(start + 64 * m, 64), :], buf.at[m], sems.at[m]
-        )
-        for m in range(chunks)
-    ]
-    for copy in copies:
-        copy.start()
-    for m, copy in enumerate(copies):
-        copy.wait()
-        for i in range(blocks):
-            both = buf[m, :, :, LANES * i : LANES * i + LANES].reshape(LANES, LANES)
+    for m in range(spec_ref.shape[1] // 64):
+        for i in range(spec_ref.shape[2] // LANES):
+            both = spec_ref[:, 64 * m : 64 * m + 64, LANES * i : LANES * i + LANES].reshape(LANES, LANES)
             out_ref[near * i : near * i + near, few * m : few * m + few, :] = both.T.reshape(near, few, LANES)
 
 
@@ -265,27 +259,34 @@
 
     small = pltpu.CompilerParams(vmem_limit_bytes=16 << 20)
     in_hbm = pl.BlockSpec(memory_space=pltpu.HBM)
-    tails = pl.pallas_call(
-        tail_kernel,
-        out_shape=jax.ShapeDtypeStruct((6, channels), F32),
-        in_specs=[in_hbm] * 3,
-        out_specs=whole,
-        compiler_params=small,
-        scratch_shapes=[pltpu.VMEM((3, 8, channels), F32), pltpu.SemaphoreType.DMA((3,))],
-    )(q_proj, k_proj, v_proj)
+    part = lax.axis_index("dp").reshape(1)
+    kept = [pltpu.with_memory_space_constraint(x, pltpu.HBM) for x in (q_proj, k_proj, v_proj, filter_spec)]
+    tails, own_spec = pl.pallas_call(
+        functools.partial(load_kernel, chunks),
+        out_shape=[
+            jax.ShapeDtypeStruct((6, channels), F32),
+            jax.ShapeDtypeStruct((2, 64 * chunks, channels), F32),
+        ],
+        in_specs=[pl.BlockSpec(memory_space=pltpu.SMEM)] + [in_hbm] * 4,
+        out_specs=[whole] * 2,
+        compiler_params=small,
+        scratch_shapes=[
+            pltpu.VMEM((3, 8, channels), F32),
+            pltpu.SemaphoreType.DMA((3,)),
+            pltpu.SemaphoreType.DMA,
+        ],
+    )(part, *kept)
     rim = shifted(tails, "ctx", 1)
 
-    part = lax.axis_index("dp").reshape(1)
     packed = jax.ShapeDtypeStruct((everyone, depth, LANES), F32)
     held = pl.pallas_call(
-        functools.partial(spec_kernel, few, chunks),
+        functools.partial(spec_kernel, few),
         out_shape=packed,
-        in_specs=[pl.BlockSpec(memory_space=pltpu.SMEM), in_hbm],
+        in_specs=[whole],
         out_specs=whole,
-        scratch_shapes=[pltpu.VMEM((chunks, 2, 64, channels), F32), pltpu.SemaphoreType.DMA((chunks,))],
         compiler_params=small,
         cost_estimate=pl.CostEstimate(flops=0, bytes_accessed=1 << 21, transcendentals=0),
-    )(part, filter_spec)
+    )(own_spec)
 
     sent = pl.pallas_call(
         functools.partial(mixed_kernel, few, chunks),

time: 80.6 us -> 78.9 us (0.979)
  local copies, waits for them, and re-layouts: 5.31 us -> 0.08 us
  blocking collectives: 45.4 us -> 47.4 us
  Pallas kernels: 8.92 us -> 9.84 us
    unnamed x34 -> x26, local copies, waits for them, and re-layouts: 5.31 us -> 0.08 us
    all_to_all x1, blocking collectives: 45.4 us -> 47.4 us  [per_device_tiled(): come = lax.all_to_all(sent, ('dp', 'ctx'), 0, 0, tiled=True)]
    pallas_call x2, Pallas kernels: 0.72 us -> 1.63 us  [the longest x1 1.31 us: per_device_tiled(): pl.pallas_call(functools.partial(load_kernel, chunks), out_shape=[jax.Sha...]
  transfers between devices with their start and end apart: 2 -> 2, of which waited for: 1 -> 2; matrix products, arithmetic and copies ran while one was open for 0% -> 0% of each run, Pallas kernels for 1% -> 1%
where the time goes in v3:
time: 78.9 us; the launch traced here: 78.5 us
  blocking collectives  47.4 us (60%)
  waiting for transfers between devices  15.8 us (20%)
  Pallas kernels  9.84 us (12%)
  starting transfers between devices  5.09 us (6%)
    all_to_all x1, blocking collectives, per_device_tiled(): come = lax.all_to_all(sent, ('dp', 'ctx'), 0, 0, tiled=True)  47.4 us
    all_to_all x1, waiting for transfers between devices, per_device_tiled(): back = lax.all_to_all(conv, ('dp', 'ctx'), 0, 0, tiled=True)  15.3 us
    pallas_call x1, Pallas kernels, per_device_tiled(): pl.pallas_call(functools.partial(conv_kernel, parts, few, chunks), out_sh...  6.29 us
    all_to_all x1, starting transfers between devices, per_device_tiled(): back = lax.all_to_all(conv, ('dp', 'ctx'), 0, 0, tiled=True)  2.61 us
    ppermute x1, starting transfers between devices, shifted(): return lax.ppermute(block, axis, route)  2.49 us
  transfers between devices with their start and end apart: 2, of which 2 were waited for; matrix products, arithmetic and copies ran while one was open for 0% of the time, Pallas kernels for 1%

profile of v3, /device:TPU:0, one launch (start us, length us, event | category | flops | bytes accessed | tf_op | source)
XLA Modules:
  0.0 78.5 jit_solution(3310448768725056677)
XLA Ops:
  0.0 1.3 %shard_map.136 = (f32[6,512]{1,0:T(8,128)S(1)}, f32[2,256,512]{2,1,0:T(8,128)S(1)}) custom-call(s32[1]{0:T(128)} %bitcast.part_ref, f32[256,512]{1,0:T(8,128)} %q_ref.3, f32[256,512]{1,0:T(8,128)} %k_ref.5, f32[256,512]{1,0:T(8,128)} %v_ref.5, f32[2,512,512]{2,1,0:T(8,128)} %spec_ref.1), custom_call_target="tpu_custom_call" | custom-call | tf_op jit(solution)/shard_map/pallas_call | solution.py:264
  1.3 0.0 copy-start
  1.3 0.0 copy-start.1
  1.3 0.0 copy-start.7
  1.4 2.5 %collective-permute-start = (f32[6,512]{1,0:T(8,128)S(1)}, f32[6,512]{1,0:T(8,128)S(1)}, u32[]{:S(2)}, u32[]{:S(2)}) collective-permute-start(f32[6,512]{1,0:T(8,128)S(1)} %get-tuple-element.9), channel_id=1, source_target_pairs={{0,1},{1,2},{2,3},{3,4},{4,5},{5,6},{6,7},{7,8},{8,9},{9,10},{10,1... | collective-permute-start | bytes 36872 | tf_op jit(solution)/shard_map/ppermute | solution.py:26
  3.9 0.3 shard_map.137.held_ref
  4.2 0.5 collective-permute-done.rim_ref
  4.7 0.0 copy-done
  4.7 0.0 copy-done.1
  4.7 0.0 copy-done.7
  4.7 0.4 shard_map.138
  5.1 0.0 copy-start.4
  5.1 0.0 copy-start.5
  5.1 0.0 copy-start.6
  5.1 0.0 copy-start.8
  5.1 0.0 copy-start.9
  5.1 0.0 copy-start.10
  5.2 0.0 copy-start.11
  5.2 47.4 %all_to_all.10.in_ref = f32[32,96,128]{2,1,0:T(8,128)S(1)} all-to-all(f32[32,96,128]{2,1,0:T(8,128)S(1)} %shard_map.138), channel_id=1, replica_groups=mesh['dp'=2,'ctx'=16] {'dp','ctx'}, dimensions={0} | all-to-all | bytes 3145728 | tf_op jit(solution)/shard_map/all_to_all | solution.py:301
  52.6 0.0 copy-done.3
  52.6 0.0 copy-done.4
  52.6 0.0 copy-done.5
  52.6 0.0 copy-done.6
  52.6 0.0 copy-done.8
  52.6 0.0 copy-done.9
  52.6 0.0 copy-start.2
  52.6 0.0 copy-start.12
  52.7 6.3 %shard_map.139 = f32[32,16,256]{2,1,0:T(8,128)} custom-call(f32[32,96,128]{2,1,0:T(8,128)S(1)} %all_to_all.10.in_ref, bf16[64,48]{1,0:T(8,128)(2,1)S(1)} %copy-done.10, bf16[16,192]{1,0:T(8,128)(2,1)S(1)} %copy-done.11, f32[32,256]{1,0:T(8,128)S(1)} %copy-done.8, f32[32,256]{1,0:T(8,128)S(1)} %copy-done.9, bf16[512,512]{1,0:T(8,128)(2,1)S(1)} %copy-done.3, ...), custom_call_target="tpu_custom_call" | custom-call | bytes 4194304 | tf_op jit(solution)/shard_map/pallas_call | solution.py:313
  58.9 2.6 %all-to-all-start.1 = ((f32[32,16,256]{2,1,0:T(8,128)}), f32[32,16,256]{2,1,0:T(8,128)S(1)}, u32[]{:S(2)}, u32[]{:S(2)}) async-start(f32[32,16,256]{2,1,0:T(8,128)} %shard_map.139), calls=%async_computation.1 | async-start | bytes 1048576 | tf_op jit(solution)/shard_map/all_to_all | solution.py:323
  61.6 0.5 shard_map.140
  62.1 15.3 %all-to-all-done.1.conv_ref = f32[32,16,256]{2,1,0:T(8,128)S(1)} async-done(((f32[32,16,256]{2,1,0:T(8,128)}), f32[32,16,256]{2,1,0:T(8,128)S(1)}, u32[]{:S(2)}, u32[]{:S(2)}) %all-to-all-start.1) | async-done | bytes 524320 | tf_op jit(solution)/shard_map/all_to_all | solution.py:323
  77.5 1.0 %shard_map.141 = f32[256,512]{1,0:T(8,128)} custom-call(f32[32,16,256]{2,1,0:T(8,128)S(1)} %all-to-all-done.1.conv_ref, f32[256,512]{1,0:T(8,128)S(1)} %get-tuple-element.11.query_ref, f32[256,512]{1,0:T(8,128)S(1)} %get-tuple-element.12.direct_ref), custom_call_target="tpu_custom_call" | custom-call | bytes 2097152 | tf_op jit(solution)/shard_map/pallas_call | solution.py:324
  (5 shorter events, 0.0 us)
Async XLA Ops:
  1.3 3.4 %copy-start = (f32[256,512]{1,0:T(8,128)S(1)}, f32[256,512]{1,0:T(8,128)}, u32[]{:S(2)}) copy-start(f32[256,512]{1,0:T(8,128)} %k_ref.5) | copy-start | bytes 1572868
  1.3 3.3 %copy-start.1 = (f32[256,512]{1,0:T(8,128)S(1)}, f32[256,512]{1,0:T(8,128)}, u32[]{:S(2)}) copy-start(f32[256,512]{1,0:T(8,128)} %v_ref.5) | copy-start | bytes 1572868
  1.3 3.3 %copy-start.7 = (f32[3,3,512]{2,1,0:T(4,128)S(1)}, f32[3,3,512]{2,1,0:T(4,128)}, u32[]{:S(2)}) copy-start(f32[3,3,512]{2,1,0:T(4,128)} %taps_ref.3) | copy-start | bytes 55300
  1.4 3.3 %collective-permute-start = (f32[6,512]{1,0:T(8,128)S(1)}, f32[6,512]{1,0:T(8,128)S(1)}, u32[]{:S(2)}, u32[]{:S(2)}) collective-permute-start(f32[6,512]{1,0:T(8,128)S(1)} %get-tuple-element.9), channel_id=1, source_target_pairs={{0,1},{1,2},{2,3},{3,4},{4,5},{5,6},{6,7},{7,8},{8,9},{9,10},{10,1... | collective-permute-start | bytes 36872 | tf_op jit(solution)/shard_map/ppermute | solution.py:26
  5.1 47.5 %copy-start.3 = (bf16[512,512]{1,0:T(8,128)(2,1)S(1)}, bf16[512,512]{1,0:T(8,128)(2,1)}, u32[]{:S(2)}) copy-start(bf16[512,512]{1,0:T(8,128)(2,1)} %constant.26.clone.fh_ref) | copy-start | bytes 1572868
  5.1 47.5 %copy-start.4 = (bf16[512,512]{1,0:T(8,128)(2,1)S(1)}, bf16[512,512]{1,0:T(8,128)(2,1)}, u32[]{:S(2)}) copy-start(bf16[512,512]{1,0:T(8,128)(2,1)} %constant.27.clone.fl_ref) | copy-start | bytes 1572868
  5.1 47.5 %copy-start.5 = (bf16[512,512]{1,0:T(8,128)(2,1)S(1)}, bf16[512,512]{1,0:T(8,128)(2,1)}, u32[]{:S(2)}) copy-start(bf16[512,512]{1,0:T(8,128)(2,1)} %constant.28.clone.bh_ref) | copy-start | bytes 1572868
  5.1 47.5 %copy-start.6 = (bf16[512,512]{1,0:T(8,128)(2,1)S(1)}, bf16[512,512]{1,0:T(8,128)(2,1)}, u32[]{:S(2)}) copy-start(bf16[512,512]{1,0:T(8,128)(2,1)} %constant.29.clone.bl_ref) | copy-start | bytes 1572868
  5.1 47.5 %copy-start.8 = (f32[32,256]{1,0:T(8,128)S(1)}, f32[32,256]{1,0:T(8,128)}, u32[]{:S(2)}) copy-start(f32[32,256]{1,0:T(8,128)} %constant.24.clone.cos_ref) | copy-start | bytes 98308
  5.1 47.5 %copy-start.9 = (f32[32,256]{1,0:T(8,128)S(1)}, f32[32,256]{1,0:T(8,128)}, u32[]{:S(2)}) copy-start(f32[32,256]{1,0:T(8,128)} %constant.25.clone.sin_ref) | copy-start | bytes 98308
  5.1 47.5 %copy-start.10 = (bf16[64,48]{1,0:T(8,128)(2,1)S(1)}, bf16[64,48]{1,0:T(8,128)(2,1)}, u32[]{:S(2)}) copy-start(bf16[64,48]{1,0:T(8,128)(2,1)} %constant.22.clone.w1_ref) | copy-start | bytes 18436
  5.2 47.5 %copy-start.11 = (bf16[16,192]{1,0:T(8,128)(2,1)S(1)}, bf16[16,192]{1,0:T(8,128)(2,1)}, u32[]{:S(2)}) copy-start(bf16[16,192]{1,0:T(8,128)(2,1)} %constant.23.clone.w2_ref) | copy-start | bytes 18436
  52.6 8.9 %copy-start.2 = (f32[256,512]{1,0:T(8,128)S(1)}, f32[256,512]{1,0:T(8,128)}, u32[]{:S(2)}) copy-start(f32[256,512]{1,0:T(8,128)} %q_ref.3) | copy-start | bytes 1572868
  52.6 8.9 %copy-start.12 = (f32[512]{0:T(512)S(1)}, f32[512]{0:T(512)}, u32[]{:S(2)}) copy-start(f32[512]{0:T(512)} %param.18) | copy-start | bytes 6148
  58.9 18.5 %all-to-all-start.1 = ((f32[32,16,256]{2,1,0:T(8,128)}), f32[32,16,256]{2,1,0:T(8,128)S(1)}, u32[]{:S(2)}, u32[]{:S(2)}) async-start(f32[32,16,256]{2,1,0:T(8,128)} %shard_map.139), calls=%async_computation.1 | async-start | bytes 1048576 | tf_op jit(solution)/shard_map/all_to_all | solution.py:323

commit v4 on v3

--- a/solution.py
+++ b/solution.py
@@ -91,7 +91,6 @@
 def tables(parts, devices, rows):
     outer, seq = 2 * devices, devices * rows
     freq = 2 * seq
-    p, s, r = np.arange(devices), np.arange(outer), np.arange(rows)
     chunks = rows * 2 // parts // 64
     low_bit, chunk, part, dev = np.meshgrid(
         np.arange(2), np.arange(chunks), np.arange(parts), np.arange(devices), indexing="ij"
@@ -101,18 +100,21 @@
     def angle(left, right, period):
         return 2.0 * np.pi * (np.outer(left, right) % period) / period
 
-    first = angle(s, p, outer)
-    w1h, w1l = split_np(np.concatenate([np.cos(first), -np.sin(first)]))
-    w1 = np.concatenate([w1h, w1h, w1l], axis=1)
-    last = np.concatenate([np.cos(first.T), -np.sin(first.T)], axis=1) / freq
-    w2h, w2l = split_np(last)
-    w2 = np.concatenate([w2h, w2h, w2l], axis=1)
+    s, r = np.arange(devices + 1), np.arange(rows)
     twist = angle(s, r, freq)
+    weight = np.where((s % 2 == 1) | (s % devices == 0), 2.0, 1.0)[:, None] / (2 * freq)
+    turns = [np.cos(twist), np.sin(twist), weight * np.cos(twist), weight * np.sin(twist)]
     inner = angle(r, k, rows)
     c, d = np.cos(inner), np.sin(inner)
-    fore = split_np(np.block([[c, -d], [d, c]]))
-    back = split_np(np.block([[c.T, d.T], [-d.T, c.T]]))
-    return (w1, w2, np.cos(twist).astype(np.float32), np.sin(twist).astype(np.float32), *fore, *back)
+
+    def tripled(table):
+        high, low = split_np(table)
+        return np.concatenate([high, high, low])
+
+    fore = tripled(np.block([[c, -d], [d, c]]))
+    back = tripled(np.block([[c.T, d.T], [-d.T, c.T]]))
+    turned = np.eye(LANES)[::-1].astype(BF16)
+    return (np.stack(turns).astype(np.float32), fore, back, turned)
 
 
 def split(x):
@@ -122,6 +124,96 @@
 
 def dot(a, b):
     return jnp.dot(a, b, preferred_element_type=F32)
+
+
+def plus(a, b):
+    return b if a is None else a if b is None else a + b
+
+
+def minus(a, b):
+    return a if b is None else -b if a is None else a - b
+
+
+def times(a, scale):
+    if a is None or abs(scale) < 1e-12:
+        return None
+    return a if scale == 1.0 else -a if scale == -1.0 else a * scale
+
+
+def c_add(a, b):
+    return plus(a[0], b[0]), plus(a[1], b[1])
+
+
+def c_sub(a, b):
+    return minus(a[0], b[0]), minus(a[1], b[1])
+
+
+def c_conj(a):
+    return a[0], None if a[1] is None else -a[1]
+
+
+def c_turn(a, turn):
+    c, d = math.cos(2 * math.pi * turn), math.sin(2 * math.pi * turn)
+    c, d = (float(round(v)) if abs(v - round(v)) < 1e-12 else v for v in (c, d))
+    return minus(times(a[0], c), times(a[1], d)), plus(times(a[0], d), times(a[1], c))
+
+
+def fft_complex(z, sign):
+    n = len(z)
+    if n == 1:
+        return z
+    even, odd = fft_complex(z[::2], sign), fft_complex(z[1::2], sign)
+    odd = [c_turn(v, sign * t / n) for t, v in enumerate(odd)]
+    return [c_add(e, o) for e, o in zip(even, odd)] + [c_sub(e, o) for e, o in zip(even, odd)]
+
+
+def fft_real(x):
+    n = len(x)
+    if n == 1:
+        return [(x[0], None)]
+    half = n // 2
+    even, odd = fft_real(x[::2]), fft_real(x[1::2])
+    out = [None] * (half + 1)
+    for t, (e, o) in enumerate(zip(even, odd)):
+        o = c_turn(o, -t / n)
+        out[half - t] = c_conj(c_sub(e, o))
+        out[t] = c_add(e, o)
+    return out
+
+
+def fft_to_real(z):
+    half = len(z) - 1
+    n = 2 * half
+    if n == 2:
+        return [plus(z[0][0], z[1][0]), minus(z[0][0], z[1][0])]
+    even, odd = [], []
+    for t in range(half // 2 + 1):
+        other = c_conj(z[half - t])
+        even.append(c_add(z[t], other))
+        odd.append(c_turn(c_sub(z[t], other), t / n))
+    out = [None] * n
+    out[::2], out[1::2] = fft_to_real(even), fft_to_real(odd)
+    return out
+
+
+def spread(x):
+    n = len(x)
+    turned = [c_turn((v, None), -p / (2 * n)) for p, v in enumerate(x)]
+    even, odd = fft_complex(turned[::2], -1), fft_complex(turned[1::2], -1)
+    out = [None] * (n + 1)
+    out[::2] = fft_real(x)
+    out[1::2] = [c_add(e, c_turn(o, -t / n)) for t, (e, o) in enumerate(zip(even, odd))]
+    return out
+
+
+def gather(z):
+    n = len(z) - 1
+    ends = [(z[0][0], None), *z[2:n:2], (z[n][0], None)]
+    even = fft_to_real(ends)
+    odd = [None] * n
+    odd[::2] = fft_complex(z[1::2], 1)
+    odd[1::2] = fft_complex([c_turn(v, t / n) for t, v in enumerate(z[1::2])], 1)
+    return [plus(e, c_turn(o, p / (2 * n))[0]) for p, (e, o) in enumerate(zip(even, odd))]
 
 
 def causal(x, rim, taps):
@@ -193,57 +285,84 @@
             out_ref[row, col] = query_ref[row, col] * conv.T + direct_ref[row, col]
 
 
-def conv_kernel(
-    parts, few, chunks, in_ref, w1_ref, w2_ref, cos_ref, sin_ref, fh_ref, fl_ref, bh_ref, bl_ref,
-    out_ref, yh, yl, ph, pq,
-):
+def conv_kernel(parts, few, chunks, in_ref, turn_ref, fore_ref, back_ref, flip_ref, out_ref, spec, triple, undo):
     devices = in_ref.shape[0] // parts
-    outer = 2 * devices
-    rows = out_ref.shape[2]
+    outer, rows = 2 * devices, out_ref.shape[2]
+    kept = devices + 1
     base = few * chunks
-    cosines, sines = cos_ref[...], sin_ref[...]
-
-    def keep(high_ref, low_ref, at, real, imag):
-        for col, x in ((0, real), (rows, imag)):
-            high, low = split(x)
-            high_ref[at : at + outer, col : col + rows] = high
-            low_ref[at : at + outer, col : col + rows] = low
+    wide = 2 * rows
+
+    def keep(at, col, value):
+        high, low = split(value)
+        span = slice(at, at + few)
+        for j, part in enumerate((high, low, high)):
+            triple[span, wide * j + col : wide * j + col + value.shape[1]] = part
+
+    def row_of(s, q):
+        return (s * parts + q) * few
 
     for c in range(few):
-        for q in range(parts):
-            block = slice(q * devices, (q + 1) * devices)
-            x = jnp.concatenate(
-                [in_ref[block, base + few * h + c, :] for h in range(rows // LANES)], axis=1
-            )
-            high, low = split(x)
-            y = dot(w1_ref[...], jnp.concatenate([high, low, high], axis=0))
-            re, im = y[:outer], y[outer:]
-            keep(yh, yl, (c * parts + q) * outer, re * cosines + im * sines, im * cosines - re * sines)
-
-    group = 4
-    step = group * parts * outer
-    for g in range(few // group):
-        span = slice(g * step, (g + 1) * step)
-        spec = dot(yh[span], fh_ref[...]) + dot(yl[span], fh_ref[...]) + dot(yh[span], fl_ref[...])
-        for i in range(group):
-            c = g * group + i
-            resp = jnp.concatenate([in_ref[:, few * m + c, :] for m in range(chunks)], axis=0).T
-            h_re = jnp.concatenate([resp[:outer], resp[outer : 2 * outer]], axis=1)
-            h_im = jnp.concatenate([resp[2 * outer : 3 * outer], resp[3 * outer :]], axis=1)
+        own = jnp.concatenate([in_ref[:, few * m + c, :] for m in range(chunks)], axis=0)
+        spec[:, c, :] = own.T
+
+    for q in range(parts):
+        for h in range(rows // LANES):
+            lane = slice(LANES * h, LANES * h + LANES)
+            at = base + few * h
+            x = [in_ref[q * devices + p, at : at + few, :] for p in range(devices)]
+            for s, (re, im) in enumerate(spread(x)):
+                cosine, sine = turn_ref[0, s : s + 1, lane], turn_ref[1, s : s + 1, lane]
+                if im is None:
+                    turned = re * cosine, -re * sine
+                else:
+                    turned = re * cosine + im * sine, im * cosine - re * sine
+                keep(row_of(s, q), LANES * h, turned[0])
+                keep(row_of(s, q), rows + LANES * h, turned[1])
+
+    other = [[None, None], [None, None]]
+    count = outer - kept
+    for i in range(2):
+        for low_bit in range(2):
+            first = (2 * i + low_bit) * outer + kept
+            high, low = split(spec[first : first + count].reshape(count * few, LANES))
+            other[i][low_bit] = dot(high, flip_ref[...]) + dot(low, flip_ref[...])
+
+    def response(i, s):
+        cols = []
+        for low_bit in range(2):
+            own = spec[(2 * i + low_bit) * outer + s]
+            if 0 < s < devices:
+                at = (outer - s - kept) * few
+                mirror = other[i][1 - low_bit][at : at + few]
+                own = own - mirror if i else own + mirror
+            cols.append(own)
+        return jnp.concatenate(cols, axis=1)
+
+    cuts = (0, kept // 2, kept)
+    for begin, end in zip(cuts[:-1], cuts[1:]):
+        span = slice(row_of(begin, 0), row_of(end, 0))
+        freq = dot(triple[span], fore_ref[...])
+        for s in range(begin, end):
+            h_re, h_im = response(0, s), response(1, s)
             for q in range(parts):
-                at = (i * parts + q) * outer
-                re, im = spec[at : at + outer, :rows], spec[at : at + outer, rows:]
-                keep(ph, pq, g * step + at, re * h_re - im * h_im, re * h_im + im * h_re)
-        undo = dot(ph[span], bh_ref[...]) + dot(pq[span], bh_ref[...]) + dot(ph[span], bl_ref[...])
-        for i in range(group):
-            c = g * group + i
-            for q in range(parts):
-                at = (i * parts + q) * outer
-                re, im = undo[at : at + outer, :rows], undo[at : at + outer, rows:]
-                turned = jnp.concatenate([re * cosines - im * sines, im * cosines + re * sines], axis=0)
-                high, low = split(turned)
-                y = dot(w2_ref[...], jnp.concatenate([high, low, high], axis=0))
-                out_ref[q * devices : (q + 1) * devices, c, :] = y
+                at = row_of(s - begin, q)
+                re, im = freq[at : at + few, :rows], freq[at : at + few, rows:]
+                keep(row_of(s, q), 0, re * h_re - im * h_im)
+                keep(row_of(s, q), rows, re * h_im + im * h_re)
+        undo[span] = dot(triple[span], back_ref[...])
+
+    for q in range(parts):
+        for h in range(rows // LANES):
+            lane = slice(LANES * h, LANES * h + LANES)
+            z = []
+            for s in range(kept):
+                at = row_of(s, q)
+                re = undo[at : at + few, LANES * h : LANES * h + LANES]
+                im = undo[at : at + few, rows + LANES * h : rows + LANES * h + LANES]
+                cosine, sine = turn_ref[2, s : s + 1, lane], turn_ref[3, s : s + 1, lane]
+                z.append((re * cosine - im * sine, im * cosine + re * sine))
+            for p, y in enumerate(gather(z)):
+                out_ref[q * devices + p, :, lane] = y
 
 
 def per_device_tiled(q_proj, k_proj, v_proj, short_filter, skip_gain, filter_spec):
@@ -309,13 +428,17 @@
         cost_estimate=pl.CostEstimate(flops=0, bytes_accessed=5 << 19, transcendentals=0),
     )(q_proj, k_proj, v_proj, rim, short_filter, skip_gain[None, :])
 
-    total = few * parts * outer
+    total = few * parts * (devices + 1)
     conv = pl.pallas_call(
         functools.partial(conv_kernel, parts, few, chunks),
         out_shape=jax.ShapeDtypeStruct((everyone, few, rows), F32),
-        in_specs=[whole] * 9,
+        in_specs=[whole] * 5,
         out_specs=whole,
-        scratch_shapes=[pltpu.VMEM((total, 2 * rows), BF16)] * 4,
+        scratch_shapes=[
+            pltpu.VMEM((4 * outer, few, LANES), F32),
+            pltpu.VMEM((total, 6 * rows), BF16),
+            pltpu.VMEM((total, 2 * rows), F32),
+        ],
         compiler_params=small,
         cost_estimate=pl.CostEstimate(flops=0, bytes_accessed=4 << 20, transcendentals=0),
     )(come, *(jnp.asarray(t) for t in tables(parts, devices, rows)))
@@ -337,8 +460,8 @@
     chunks = 2 * rows // parts // 64
     return (
         rest == 0
-        and few % 8 == 0
-        and 2 * devices == 32
+        and few % 16 == 0
+        and devices == 16
         and rows % LANES == 0
         and parts * devices * chunks == LANES
         and chunks % (rows // LANES) == 0

time: 78.9 us -> 77.5 us (0.982)
  Pallas kernels: 9.84 us -> 8.57 us
    pallas_call x1, Pallas kernels: 6.29 us -> 5.02 us  [per_device_tiled(): pl.pallas_call(functools.partial(conv_kernel, parts, few, chunks), out_sh...]
where the time goes in v4:
time: 77.5 us; the launch traced here: 77.1 us
  blocking collectives  47.4 us (61%)
  waiting for transfers between devices  15.8 us (20%)
  Pallas kernels  8.57 us (11%)
  starting transfers between devices  5.09 us (7%)
    all_to_all x1, blocking collectives, per_device_tiled(): come = lax.all_to_all(sent, ('dp', 'ctx'), 0, 0, tiled=True)  47.4 us
    all_to_all x1, waiting for transfers between devices, per_device_tiled(): back = lax.all_to_all(conv, ('dp', 'ctx'), 0, 0, tiled=True)  15.3 us
    pallas_call x1, Pallas kernels, per_device_tiled(): pl.pallas_call(functools.partial(conv_kernel, parts, few, chunks), out_sh...  5.02 us
    all_to_all x1, starting transfers between devices, per_device_tiled(): back = lax.all_to_all(conv, ('dp', 'ctx'), 0, 0, tiled=True)  2.61 us
    ppermute x1, starting transfers between devices, shifted(): return lax.ppermute(block, axis, route)  2.49 us
  transfers between devices with their start and end apart: 2, of which 2 were waited for; matrix products, arithmetic and copies ran while one was open for 0% of the time, Pallas kernels for 1%

profile of v4, /device:TPU:0, one launch (start us, length us, event | category | flops | bytes accessed | tf_op | source)
XLA Modules:
  0.0 77.1 jit_solution(15771327404468497389)
XLA Ops:
  0.0 1.3 %shard_map.100 = (f32[6,512]{1,0:T(8,128)S(1)}, f32[2,256,512]{2,1,0:T(8,128)S(1)}) custom-call(s32[1]{0:T(128)} %bitcast.part_ref, f32[256,512]{1,0:T(8,128)} %q_ref.3, f32[256,512]{1,0:T(8,128)} %k_ref.5, f32[256,512]{1,0:T(8,128)} %v_ref.5, f32[2,512,512]{2,1,0:T(8,128)} %spec_ref.1), custom_call_target="tpu_custom_call" | custom-call | tf_op jit(solution)/shard_map/pallas_call | solution.py:383
  1.3 0.0 copy-start
  1.3 0.0 copy-start.1
  1.3 0.0 copy-start.5
  1.4 2.5 %collective-permute-start = (f32[6,512]{1,0:T(8,128)S(1)}, f32[6,512]{1,0:T(8,128)S(1)}, u32[]{:S(2)}, u32[]{:S(2)}) collective-permute-start(f32[6,512]{1,0:T(8,128)S(1)} %get-tuple-element.9), channel_id=1, source_target_pairs={{0,1},{1,2},{2,3},{3,4},{4,5},{5,6},{6,7},{7,8},{8,9},{9,10},{10,1... | collective-permute-start | bytes 36872 | tf_op jit(solution)/shard_map/ppermute | solution.py:26
  3.9 0.3 shard_map.101.held_ref
  4.2 0.5 collective-permute-done.rim_ref
  4.7 0.0 copy-done
  4.7 0.0 copy-done.1
  4.7 0.0 copy-done.5
  4.7 0.0 copy-start.6
  4.7 0.0 copy-start.7
  4.7 0.4 shard_map.102
  5.1 0.0 copy-start.3
  5.1 0.0 copy-start.4
  5.1 47.4 %all_to_all.10.in_ref = f32[32,96,128]{2,1,0:T(8,128)S(1)} all-to-all(f32[32,96,128]{2,1,0:T(8,128)S(1)} %shard_map.102), channel_id=1, replica_groups=mesh['dp'=2,'ctx'=16] {'dp','ctx'}, dimensions={0} | all-to-all | bytes 3145728 | tf_op jit(solution)/shard_map/all_to_all | solution.py:420
  52.5 0.0 copy-done.6
  52.5 0.0 copy-done.7
  52.5 0.0 copy-done.3
  52.5 0.0 copy-done.4
  52.5 0.0 copy-start.2
  52.6 0.0 copy-start.8
  52.6 5.0 %shard_map.103 = f32[32,16,256]{2,1,0:T(8,128)} custom-call(f32[32,96,128]{2,1,0:T(8,128)S(1)} %all_to_all.10.in_ref, f32[4,17,256]{2,1,0:T(8,128)S(1)} %copy-done.6, bf16[1536,512]{1,0:T(8,128)(2,1)S(1)} %copy-done.3, bf16[1536,512]{1,0:T(8,128)(2,1)S(1)} %copy-done.4, bf16[128,128]{1,0:T(8,128)(2,1)S(1)} %copy-done.7), custom_call_target="tpu_custom_call" | custom-call | bytes 4194304 | tf_op jit(solution)/shard_map/pallas_call | solution.py:432
  57.6 2.6 %all-to-all-start.1 = ((f32[32,16,256]{2,1,0:T(8,128)}), f32[32,16,256]{2,1,0:T(8,128)S(1)}, u32[]{:S(2)}, u32[]{:S(2)}) async-start(f32[32,16,256]{2,1,0:T(8,128)} %shard_map.103), calls=%async_computation.1 | async-start | bytes 1048576 | tf_op jit(solution)/shard_map/all_to_all | solution.py:446
  60.2 0.0 copy-done.2
  60.2 0.0 copy-done.8
  60.2 0.5 shard_map.104
  60.7 15.3 %all-to-all-done.1.conv_ref = f32[32,16,256]{2,1,0:T(8,128)S(1)} async-done(((f32[32,16,256]{2,1,0:T(8,128)}), f32[32,16,256]{2,1,0:T(8,128)S(1)}, u32[]{:S(2)}, u32[]{:S(2)}) %all-to-all-start.1) | async-done | bytes 524320 | tf_op jit(solution)/shard_map/all_to_all | solution.py:446
  76.1 1.0 %shard_map.105 = f32[256,512]{1,0:T(8,128)} custom-call(f32[32,16,256]{2,1,0:T(8,128)S(1)} %all-to-all-done.1.conv_ref, f32[256,512]{1,0:T(8,128)S(1)} %get-tuple-element.11.query_ref, f32[256,512]{1,0:T(8,128)S(1)} %get-tuple-element.12.direct_ref), custom_call_target="tpu_custom_call" | custom-call | bytes 2097152 | tf_op jit(solution)/shard_map/pallas_call | solution.py:447
Async XLA Ops:
  1.3 3.4 %copy-start = (f32[256,512]{1,0:T(8,128)S(1)}, f32[256,512]{1,0:T(8,128)}, u32[]{:S(2)}) copy-start(f32[256,512]{1,0:T(8,128)} %k_ref.5) | copy-start | bytes 1572868
  1.3 3.3 %copy-start.1 = (f32[256,512]{1,0:T(8,128)S(1)}, f32[256,512]{1,0:T(8,128)}, u32[]{:S(2)}) copy-start(f32[256,512]{1,0:T(8,128)} %v_ref.5) | copy-start | bytes 1572868
  1.3 3.3 %copy-start.5 = (f32[3,3,512]{2,1,0:T(4,128)S(1)}, f32[3,3,512]{2,1,0:T(4,128)}, u32[]{:S(2)}) copy-start(f32[3,3,512]{2,1,0:T(4,128)} %taps_ref.3) | copy-start | bytes 55300
  1.4 3.3 %collective-permute-start = (f32[6,512]{1,0:T(8,128)S(1)}, f32[6,512]{1,0:T(8,128)S(1)}, u32[]{:S(2)}, u32[]{:S(2)}) collective-permute-start(f32[6,512]{1,0:T(8,128)S(1)} %get-tuple-element.9), channel_id=1, source_target_pairs={{0,1},{1,2},{2,3},{3,4},{4,5},{5,6},{6,7},{7,8},{8,9},{9,10},{10,1... | collective-permute-start | bytes 36872 | tf_op jit(solution)/shard_map/ppermute | solution.py:26
  4.7 47.8 %copy-start.6 = (f32[4,17,256]{2,1,0:T(8,128)S(1)}, f32[4,17,256]{2,1,0:T(8,128)}, u32[]{:S(2)}) copy-start(f32[4,17,256]{2,1,0:T(8,128)} %constant.14.clone.turn_ref) | copy-start | bytes 208900
  4.7 47.8 %copy-start.7 = (bf16[128,128]{1,0:T(8,128)(2,1)S(1)}, bf16[128,128]{1,0:T(8,128)(2,1)}, u32[]{:S(2)}) copy-start(bf16[128,128]{1,0:T(8,128)(2,1)} %constant.17.clone.flip_ref) | copy-start | bytes 98308
  5.1 47.4 %copy-start.3 = (bf16[1536,512]{1,0:T(8,128)(2,1)S(1)}, bf16[1536,512]{1,0:T(8,128)(2,1)}, u32[]{:S(2)}) copy-start(bf16[1536,512]{1,0:T(8,128)(2,1)} %constant.15.clone.fore_ref) | copy-start | bytes 4718596
  5.1 47.4 %copy-start.4 = (bf16[1536,512]{1,0:T(8,128)(2,1)S(1)}, bf16[1536,512]{1,0:T(8,128)(2,1)}, u32[]{:S(2)}) copy-start(bf16[1536,512]{1,0:T(8,128)(2,1)} %constant.16.clone.back_ref) | copy-start | bytes 4718596
  52.5 7.7 %copy-start.2 = (f32[256,512]{1,0:T(8,128)S(1)}, f32[256,512]{1,0:T(8,128)}, u32[]{:S(2)}) copy-start(f32[256,512]{1,0:T(8,128)} %q_ref.3) | copy-start | bytes 1572868
  52.6 7.7 %copy-start.8 = (f32[512]{0:T(512)S(1)}, f32[512]{0:T(512)}, u32[]{:S(2)}) copy-start(f32[512]{0:T(512)} %param.14) | copy-start | bytes 6148
  57.6 18.5 %all-to-all-start.1 = ((f32[32,16,256]{2,1,0:T(8,128)}), f32[32,16,256]{2,1,0:T(8,128)S(1)}, u32[]{:S(2)}, u32[]{:S(2)}) async-start(f32[32,16,256]{2,1,0:T(8,128)} %shard_map.103), calls=%async_computation.1 | async-start | bytes 1048576 | tf_op jit(solution)/shard_map/all_to_all | solution.py:446

commit v5 on v4

--- a/solution.py
+++ b/solution.py
@@ -100,11 +100,12 @@
     def angle(left, right, period):
         return 2.0 * np.pi * (np.outer(left, right) % period) / period
 
-    s, r = np.arange(devices + 1), np.arange(rows)
+    s, r, half = np.arange(devices + 1), np.arange(rows), rows // 2
     twist = angle(s, r, freq)
     weight = np.where((s % 2 == 1) | (s % devices == 0), 2.0, 1.0)[:, None] / (2 * freq)
     turns = [np.cos(twist), np.sin(twist), weight * np.cos(twist), weight * np.sin(twist)]
-    inner = angle(r, k, rows)
+    parity = angle([1], r[:half], rows)
+    inner = angle(r[:half], k[:half] // 2, half)
     c, d = np.cos(inner), np.sin(inner)
 
     def tripled(table):
@@ -113,8 +114,10 @@
 
     fore = tripled(np.block([[c, -d], [d, c]]))
     back = tripled(np.block([[c.T, d.T], [-d.T, c.T]]))
-    turned = np.eye(LANES)[::-1].astype(BF16)
-    return (np.stack(turns).astype(np.float32), fore, back, turned)
+    flip = np.concatenate([np.eye(LANES)[::-1]] * 2).astype(BF16)
+    turns = np.stack(turns).astype(np.float32)
+    parity = np.concatenate([np.cos(parity), np.sin(parity)]).astype(np.float32)
+    return turns, parity, fore, back, flip
 
 
 def split(x):
@@ -285,83 +288,90 @@
             out_ref[row, col] = query_ref[row, col] * conv.T + direct_ref[row, col]
 
 
-def conv_kernel(parts, few, chunks, in_ref, turn_ref, fore_ref, back_ref, flip_ref, out_ref, spec, triple, undo):
+def conv_kernel(
+    parts, few, chunks, in_ref, turn_ref, parity_ref, fore_ref, back_ref, flip_ref, out_ref, spec, triple, freq, undo
+):
     devices = in_ref.shape[0] // parts
-    outer, rows = 2 * devices, out_ref.shape[2]
+    outer = 2 * devices
     kept = devices + 1
-    base = few * chunks
-    wide = 2 * rows
-
-    def keep(at, col, value):
-        high, low = split(value)
-        span = slice(at, at + few)
-        for j, part in enumerate((high, low, high)):
-            triple[span, wide * j + col : wide * j + col + value.shape[1]] = part
-
-    def row_of(s, q):
-        return (s * parts + q) * few
+    base, pitch = few * chunks, few + 1
+    left, right = slice(0, LANES), slice(LANES, 2 * LANES)
+    odd_cos, odd_sin = parity_ref[0:1], parity_ref[1:2]
+
+    def row_of(low_bit, s, q):
+        at = ((low_bit * kept + s) * parts + q) * few
+        return slice(at, at + few)
+
+    def keep(span, real, imag):
+        for col, value in ((0, real), (LANES, imag)):
+            high, low = split(value)
+            for j, part in enumerate((high, low, high)):
+                at = 2 * LANES * j + col
+                triple[span, at : at + LANES] = part
+
+    for q in range(parts):
+        tiles = []
+        for h in range(2):
+            at = base + few * h
+            tiles.append(spread([in_ref[q * devices + p, at : at + few, :] for p in range(devices)]))
+        for s in range(kept):
+            turned = []
+            for (re, im), lane in zip((tiles[0][s], tiles[1][s]), (left, right)):
+                cosine, sine = turn_ref[0, s : s + 1, lane], turn_ref[1, s : s + 1, lane]
+                if im is None:
+                    turned.append((re * cosine, -re * sine))
+                else:
+                    turned.append((re * cosine + im * sine, im * cosine - re * sine))
+            keep(row_of(0, s, q), *c_add(*turned))
+            re, im = c_sub(*turned)
+            keep(row_of(1, s, q), re * odd_cos + im * odd_sin, im * odd_cos - re * odd_sin)
+
+    freq[...] = dot(triple[...], fore_ref[...])
 
     for c in range(few):
         own = jnp.concatenate([in_ref[:, few * m + c, :] for m in range(chunks)], axis=0)
-        spec[:, c, :] = own.T
-
-    for q in range(parts):
-        for h in range(rows // LANES):
-            lane = slice(LANES * h, LANES * h + LANES)
-            at = base + few * h
-            x = [in_ref[q * devices + p, at : at + few, :] for p in range(devices)]
-            for s, (re, im) in enumerate(spread(x)):
-                cosine, sine = turn_ref[0, s : s + 1, lane], turn_ref[1, s : s + 1, lane]
-                if im is None:
-                    turned = re * cosine, -re * sine
-                else:
-                    turned = re * cosine + im * sine, im * cosine - re * sine
-                keep(row_of(s, q), LANES * h, turned[0])
-                keep(row_of(s, q), rows + LANES * h, turned[1])
+        spec[pl.ds(c, 4 * outer, stride=pitch), :] = own.T
 
     other = [[None, None], [None, None]]
     count = outer - kept
     for i in range(2):
         for low_bit in range(2):
             first = (2 * i + low_bit) * outer + kept
-            high, low = split(spec[first : first + count].reshape(count * few, LANES))
-            other[i][low_bit] = dot(high, flip_ref[...]) + dot(low, flip_ref[...])
-
-    def response(i, s):
-        cols = []
-        for low_bit in range(2):
-            own = spec[(2 * i + low_bit) * outer + s]
-            if 0 < s < devices:
-                at = (outer - s - kept) * few
-                mirror = other[i][1 - low_bit][at : at + few]
-                own = own - mirror if i else own + mirror
-            cols.append(own)
-        return jnp.concatenate(cols, axis=1)
-
-    cuts = (0, kept // 2, kept)
-    for begin, end in zip(cuts[:-1], cuts[1:]):
-        span = slice(row_of(begin, 0), row_of(end, 0))
-        freq = dot(triple[span], fore_ref[...])
-        for s in range(begin, end):
-            h_re, h_im = response(0, s), response(1, s)
+            pair = split(spec[first * pitch : (first + count) * pitch])
+            other[i][low_bit] = dot(jnp.concatenate(pair, axis=1), flip_ref[...])
+
+    def response(i, low_bit, s):
+        at = ((2 * i + low_bit) * outer + s) * pitch
+        own = spec[at : at + few]
+        if 0 < s < devices:
+            at = (outer - s - kept) * pitch
+            mirror = other[i][1 - low_bit][at : at + few]
+            own = own - mirror if i else own + mirror
+        return own
+
+    for low_bit in range(2):
+        for s in range(kept):
+            h_re, h_im = response(0, low_bit, s), response(1, low_bit, s)
             for q in range(parts):
-                at = row_of(s - begin, q)
-                re, im = freq[at : at + few, :rows], freq[at : at + few, rows:]
-                keep(row_of(s, q), 0, re * h_re - im * h_im)
-                keep(row_of(s, q), rows, re * h_im + im * h_re)
-        undo[span] = dot(triple[span], back_ref[...])
+                span = row_of(low_bit, s, q)
+                re, im = freq[span, left], freq[span, right]
+                keep(span, re * h_re - im * h_im, re * h_im + im * h_re)
+
+    undo[...] = dot(triple[...], back_ref[...])
 
     for q in range(parts):
-        for h in range(rows // LANES):
-            lane = slice(LANES * h, LANES * h + LANES)
-            z = []
-            for s in range(kept):
-                at = row_of(s, q)
-                re = undo[at : at + few, LANES * h : LANES * h + LANES]
-                im = undo[at : at + few, rows + LANES * h : rows + LANES * h + LANES]
+        tiles = [], []
+        for s in range(kept):
+            even, odd = row_of(0, s, q), row_of(1, s, q)
+            base_value = undo[even, left], undo[even, right]
+            re, im = undo[odd, left], undo[odd, right]
+            odd_value = re * odd_cos - im * odd_sin, im * odd_cos + re * odd_sin
+            both = c_add(base_value, odd_value), c_sub(base_value, odd_value)
+            for tile, (re, im), lane in zip(tiles, both, (left, right)):
                 cosine, sine = turn_ref[2, s : s + 1, lane], turn_ref[3, s : s + 1, lane]
-                z.append((re * cosine - im * sine, im * cosine + re * sine))
-            for p, y in enumerate(gather(z)):
+                tile.append((re * cosine - im * sine, im * cosine + re * sine))
+        for tile, lane in zip(tiles, (left, right)):
+            for p, y in enumerate(gather(tile)):
                 out_ref[q * devices + p, :, lane] = y
 
 
@@ -428,16 +438,17 @@
         cost_estimate=pl.CostEstimate(flops=0, bytes_accessed=5 << 19, transcendentals=0),
     )(q_proj, k_proj, v_proj, rim, short_filter, skip_gain[None, :])
 
-    total = few * parts * (devices + 1)
+    total = 2 * few * parts * (devices + 1)
     conv = pl.pallas_call(
         functools.partial(conv_kernel, parts, few, chunks),
         out_shape=jax.ShapeDtypeStruct((everyone, few, rows), F32),
-        in_specs=[whole] * 5,
+        in_specs=[whole] * 6,
         out_specs=whole,
         scratch_shapes=[
-            pltpu.VMEM((4 * outer, few, LANES), F32),
-            pltpu.VMEM((total, 6 * rows), BF16),
-            pltpu.VMEM((total, 2 * rows), F32),
+            pltpu.VMEM((4 * outer * (few + 1), LANES), F32),
+            pltpu.VMEM((total, 6 * LANES), BF16),
+            pltpu.VMEM((total, 2 * LANES), F32),
+            pltpu.VMEM((total, 2 * LANES), F32),
         ],
         compiler_params=small,
         cost_estimate=pl.CostEstimate(flops=0, bytes_accessed=4 << 20, transcendentals=0),
@@ -462,9 +473,9 @@
         rest == 0
         and few % 16 == 0
         and devices == 16
-        and rows % LANES == 0
+        and rows == 2 * LANES
         and parts * devices * chunks == LANES
-        and chunks % (rows // LANES) == 0
+        and chunks % 2 == 0
     )
 
 

time: 77.5 us -> 76.6 us (0.988)
  Pallas kernels: 8.57 us -> 7.71 us
    pallas_call x1, Pallas kernels: 5.02 us -> 4.16 us  [per_device_tiled(): pl.pallas_call(functools.partial(conv_kernel, parts, few, chunks), out_sh...]
where the time goes in v5:
time: 76.6 us; the launch traced here: 76.3 us
  blocking collectives  47.4 us (62%)
  waiting for transfers between devices  15.8 us (21%)
  Pallas kernels  7.71 us (10%)
  starting transfers between devices  5.09 us (7%)
    all_to_all x1, blocking collectives, per_device_tiled(): come = lax.all_to_all(sent, ('dp', 'ctx'), 0, 0, tiled=True)  47.4 us
    all_to_all x1, waiting for transfers between devices, per_device_tiled(): back = lax.all_to_all(conv, ('dp', 'ctx'), 0, 0, tiled=True)  15.3 us
    pallas_call x1, Pallas kernels, per_device_tiled(): pl.pallas_call(functools.partial(conv_kernel, parts, few, chunks), out_sh...  4.16 us
    all_to_all x1, starting transfers between devices, per_device_tiled(): back = lax.all_to_all(conv, ('dp', 'ctx'), 0, 0, tiled=True)  2.61 us
    ppermute x1, starting transfers between devices, shifted(): return lax.ppermute(block, axis, route)  2.49 us
  transfers between devices with their start and end apart: 2, of which 2 were waited for; matrix products, arithmetic and copies ran while one was open for 0% of the time, Pallas kernels for 1%

profile of v5, /device:TPU:0, one launch (start us, length us, event | category | flops | bytes accessed | tf_op | source)
XLA Modules:
  0.0 76.3 jit_solution(8130602705324960256)
XLA Ops:
  0.0 1.3 %shard_map.109 = (f32[6,512]{1,0:T(8,128)S(1)}, f32[2,256,512]{2,1,0:T(8,128)S(1)}) custom-call(s32[1]{0:T(128)} %bitcast.part_ref, f32[256,512]{1,0:T(8,128)} %q_ref.3, f32[256,512]{1,0:T(8,128)} %k_ref.5, f32[256,512]{1,0:T(8,128)} %v_ref.5, f32[2,512,512]{2,1,0:T(8,128)} %spec_ref.1), custom_call_target="tpu_custom_call" | custom-call | tf_op jit(solution)/shard_map/pallas_call | solution.py:393
  1.3 0.0 copy-start
  1.3 0.0 copy-start.1
  1.3 0.0 copy-start.6
  1.4 2.5 %collective-permute-start = (f32[6,512]{1,0:T(8,128)S(1)}, f32[6,512]{1,0:T(8,128)S(1)}, u32[]{:S(2)}, u32[]{:S(2)}) collective-permute-start(f32[6,512]{1,0:T(8,128)S(1)} %get-tuple-element.9), channel_id=1, source_target_pairs={{0,1},{1,2},{2,3},{3,4},{4,5},{5,6},{6,7},{7,8},{8,9},{9,10},{10,1... | collective-permute-start | bytes 36872 | tf_op jit(solution)/shard_map/ppermute | solution.py:26
  3.9 0.3 shard_map.110.held_ref
  4.2 0.5 collective-permute-done.rim_ref
  4.7 0.0 copy-done
  4.7 0.0 copy-done.1
  4.7 0.0 copy-done.6
  4.7 0.4 shard_map.111
  5.1 0.0 copy-start.3
  5.1 0.0 copy-start.4
  5.1 0.0 copy-start.5
  5.1 0.0 copy-start.7
  5.1 0.0 copy-start.9
  5.1 47.4 %all_to_all.10.in_ref = f32[32,96,128]{2,1,0:T(8,128)S(1)} all-to-all(f32[32,96,128]{2,1,0:T(8,128)S(1)} %shard_map.111), channel_id=1, replica_groups=mesh['dp'=2,'ctx'=16] {'dp','ctx'}, dimensions={0} | all-to-all | bytes 3145728 | tf_op jit(solution)/shard_map/all_to_all | solution.py:430
  52.5 0.0 copy-done.3
  52.5 0.0 copy-done.4
  52.5 0.0 copy-done.5
  52.5 0.0 copy-done.7
  52.6 0.0 copy-done.9
  52.6 0.0 copy-start.2
  52.6 0.0 copy-start.8
  52.6 4.2 %shard_map.112 = f32[32,16,256]{2,1,0:T(8,128)} custom-call(f32[32,96,128]{2,1,0:T(8,128)S(1)} %all_to_all.10.in_ref, f32[4,17,256]{2,1,0:T(8,128)S(1)} %copy-done.5, f32[2,128]{1,0:T(2,128)S(1)} %copy-done.9, bf16[768,256]{1,0:T(8,128)(2,1)S(1)} %copy-done.3, bf16[768,256]{1,0:T(8,128)(2,1)S(1)} %copy-done.4, bf16[256,128]{1,0:T(8,128)(2,1)S(1)} %copy-done.7), custom_call_target="tpu_custom_call" | custom-call | bytes 4194304 | tf_op jit(solution)/shard_map/pallas_call | solution.py:442
  56.7 2.6 %all-to-all-start.1 = ((f32[32,16,256]{2,1,0:T(8,128)}), f32[32,16,256]{2,1,0:T(8,128)S(1)}, u32[]{:S(2)}, u32[]{:S(2)}) async-start(f32[32,16,256]{2,1,0:T(8,128)} %shard_map.112), calls=%async_computation.1 | async-start | bytes 1048576 | tf_op jit(solution)/shard_map/all_to_all | solution.py:457
  59.4 0.0 copy-done.2
  59.4 0.0 copy-done.8
  59.4 0.5 shard_map.113
  59.9 15.3 %all-to-all-done.1.conv_ref = f32[32,16,256]{2,1,0:T(8,128)S(1)} async-done(((f32[32,16,256]{2,1,0:T(8,128)}), f32[32,16,256]{2,1,0:T(8,128)S(1)}, u32[]{:S(2)}, u32[]{:S(2)}) %all-to-all-start.1) | async-done | bytes 524320 | tf_op jit(solution)/shard_map/all_to_all | solution.py:457
  75.3 1.0 %shard_map.114 = f32[256,512]{1,0:T(8,128)} custom-call(f32[32,16,256]{2,1,0:T(8,128)S(1)} %all-to-all-done.1.conv_ref, f32[256,512]{1,0:T(8,128)S(1)} %get-tuple-element.11.query_ref, f32[256,512]{1,0:T(8,128)S(1)} %get-tuple-element.12.direct_ref), custom_call_target="tpu_custom_call" | custom-call | bytes 2097152 | tf_op jit(solution)/shard_map/pallas_call | solution.py:458
Async XLA Ops:
  1.3 3.4 %copy-start = (f32[256,512]{1,0:T(8,128)S(1)}, f32[256,512]{1,0:T(8,128)}, u32[]{:S(2)}) copy-start(f32[256,512]{1,0:T(8,128)} %k_ref.5) | copy-start | bytes 1572868
  1.3 3.3 %copy-start.1 = (f32[256,512]{1,0:T(8,128)S(1)}, f32[256,512]{1,0:T(8,128)}, u32[]{:S(2)}) copy-start(f32[256,512]{1,0:T(8,128)} %v_ref.5) | copy-start | bytes 1572868
  1.3 3.3 %copy-start.6 = (f32[3,3,512]{2,1,0:T(4,128)S(1)}, f32[3,3,512]{2,1,0:T(4,128)}, u32[]{:S(2)}) copy-start(f32[3,3,512]{2,1,0:T(4,128)} %taps_ref.3) | copy-start | bytes 55300
  1.4 3.3 %collective-permute-start = (f32[6,512]{1,0:T(8,128)S(1)}, f32[6,512]{1,0:T(8,128)S(1)}, u32[]{:S(2)}, u32[]{:S(2)}) collective-permute-start(f32[6,512]{1,0:T(8,128)S(1)} %get-tuple-element.9), channel_id=1, source_target_pairs={{0,1},{1,2},{2,3},{3,4},{4,5},{5,6},{6,7},{7,8},{8,9},{9,10},{10,1... | collective-permute-start | bytes 36872 | tf_op jit(solution)/shard_map/ppermute | solution.py:26
  5.1 47.5 %copy-start.3 = (bf16[768,256]{1,0:T(8,128)(2,1)S(1)}, bf16[768,256]{1,0:T(8,128)(2,1)}, u32[]{:S(2)}) copy-start(bf16[768,256]{1,0:T(8,128)(2,1)} %constant.18.clone.fore_ref) | copy-start | bytes 1179652
  5.1 47.5 %copy-start.4 = (bf16[768,256]{1,0:T(8,128)(2,1)S(1)}, bf16[768,256]{1,0:T(8,128)(2,1)}, u32[]{:S(2)}) copy-start(bf16[768,256]{1,0:T(8,128)(2,1)} %constant.19.clone.back_ref) | copy-start | bytes 1179652
  5.1 47.4 %copy-start.5 = (f32[4,17,256]{2,1,0:T(8,128)S(1)}, f32[4,17,256]{2,1,0:T(8,128)}, u32[]{:S(2)}) copy-start(f32[4,17,256]{2,1,0:T(8,128)} %constant.16.clone.turn_ref) | copy-start | bytes 208900
  5.1 47.4 %copy-start.7 = (bf16[256,128]{1,0:T(8,128)(2,1)S(1)}, bf16[256,128]{1,0:T(8,128)(2,1)}, u32[]{:S(2)}) copy-start(bf16[256,128]{1,0:T(8,128)(2,1)} %constant.20.clone.flip_ref) | copy-start | bytes 196612
  5.1 47.4 %copy-start.9 = (f32[2,128]{1,0:T(2,128)S(1)}, f32[2,128]{1,0:T(2,128)}, u32[]{:S(2)}) copy-start(f32[2,128]{1,0:T(2,128)} %constant.17.clone.parity_ref) | copy-start | bytes 3076
  52.6 6.8 %copy-start.2 = (f32[256,512]{1,0:T(8,128)S(1)}, f32[256,512]{1,0:T(8,128)}, u32[]{:S(2)}) copy-start(f32[256,512]{1,0:T(8,128)} %q_ref.3) | copy-start | bytes 1572868
  52.6 6.8 %copy-start.8 = (f32[512]{0:T(512)S(1)}, f32[512]{0:T(512)}, u32[]{:S(2)}) copy-start(f32[512]{0:T(512)} %param.15) | copy-start | bytes 6148
  56.7 18.5 %all-to-all-start.1 = ((f32[32,16,256]{2,1,0:T(8,128)}), f32[32,16,256]{2,1,0:T(8,128)S(1)}, u32[]{:S(2)}, u32[]{:S(2)}) async-start(f32[32,16,256]{2,1,0:T(8,128)} %shard_map.112), calls=%async_computation.1 | async-start | bytes 1048576 | tf_op jit(solution)/shard_map/all_to_all | solution.py:457

commit v6 on v5

--- a/solution.py
+++ b/solution.py
@@ -219,62 +219,93 @@
     return [plus(e, c_turn(o, p / (2 * n))[0]) for p, (e, o) in enumerate(zip(even, odd))]
 
 
-def causal(x, rim, taps):
+def causal(x, taps):
+    return taps[0:1] * x + taps[1:2] * pltpu.roll(x, 1, 0) + taps[2:3] * pltpu.roll(x, 2, 0)
+
+
+def block_turn(x, few):
     row = lax.broadcasted_iota(jnp.int32, x.shape, 0)
-    one = jnp.where(row == 0, rim[1:2], pltpu.roll(x, 1, 0))
-    two = jnp.where(row == 0, rim[0:1], jnp.where(row == 1, rim[1:2], pltpu.roll(x, 2, 0)))
-    return taps[0:1] * x + taps[1:2] * one + taps[2:3] * two
-
-
-def load_kernel(chunks, part_ref, q_ref, k_ref, v_ref, spec_ref, tail_ref, held_ref, buf, sems, held_sem):
+    block = lax.broadcasted_iota(jnp.int32, x.shape, 1) // few
+    out = x
+    for d in range(1, 8):
+        moved = pltpu.roll(pltpu.roll(x, LANES - few * d, 1), d, 0)
+        out = jnp.where((row - block + 8) % 8 == d, moved, out)
+    return out
+
+
+def pack_kernel(
+    few, chunks, part_ref, q_ref, k_ref, v_ref, taps_ref, gain_ref, spec_ref,
+    out_ref, ends, keys, values, taps, gain, held, sems, held_sems,
+):
     rows = q_ref.shape[0]
-    copies = [
-        pltpu.make_async_copy(ref.at[rows - 8 : rows], buf.at[i], sems.at[i])
-        for i, ref in enumerate((q_ref, k_ref, v_ref))
+    near = LANES // few
+    start = pl.multiple_of(part_ref[0] * (64 * chunks), 64 * chunks)
+    small = [
+        pltpu.make_async_copy(src, dst, sems.at[i])
+        for i, (src, dst) in enumerate(
+            (
+                (taps_ref, taps),
+                (gain_ref, gain),
+                (q_ref.at[0:8], ends.at[0:8]),
+                (q_ref.at[rows - 8 : rows], ends.at[8:16]),
+                (k_ref, keys),
+                (v_ref, values),
+            )
+        )
     ]
-    span = 64 * chunks
-    start = pl.multiple_of(part_ref[0] * span, span)
-    filter_copy = pltpu.make_async_copy(spec_ref.at[:, pl.ds(start, span), :], held_ref, held_sem)
-    for copy in copies:
+    large = [
+        pltpu.make_async_copy(spec_ref.at[:, pl.ds(start + 64 * m, 64), :], held.at[m], held_sems.at[m])
+        for m in range(chunks)
+    ]
+    for copy in small + large:
         copy.start()
-    filter_copy.start()
-    for i, copy in enumerate(copies):
+    for copy in small:
         copy.wait()
-        tail_ref[2 * i : 2 * i + 2] = buf[i, 6:8]
-    filter_copy.wait()
-
-
-def spec_kernel(few, spec_ref, out_ref):
-    near = LANES // few
-    for m in range(spec_ref.shape[1] // 64):
-        for i in range(spec_ref.shape[2] // LANES):
-            both = spec_ref[:, 64 * m : 64 * m + 64, LANES * i : LANES * i + LANES].reshape(LANES, LANES)
-            out_ref[near * i : near * i + near, few * m : few * m + few, :] = both.T.reshape(near, few, LANES)
-
-
-def mixed_kernel(few, chunks, k_ref, v_ref, rim_ref, taps_ref, held_ref, out_ref):
-    del held_ref
-    near = LANES // few
+    blocks = k_ref.shape[1] // LANES
     base = few * chunks
-    for i in range(k_ref.shape[1] // LANES):
+    for i in range(blocks):
         col = slice(LANES * i, LANES * i + LANES)
-        key_seq = causal(k_ref[:, col], rim_ref[2:4, col], taps_ref[1, :, col])
-        value_seq = causal(v_ref[:, col], rim_ref[4:6, col], taps_ref[2, :, col])
-        mixed_in = key_seq * value_seq
-        for h in range(mixed_in.shape[0] // LANES):
+        dests = slice(near * i, near * i + near)
+        mixed_in = causal(keys[:, col], taps[1, :, col]) * causal(values[:, col], taps[2, :, col])
+        for h in range(rows // LANES):
             turned = mixed_in[LANES * h : LANES * h + LANES].T
             at = base + few * h
-            out_ref[near * i : near * i + near, at : at + few, :] = turned.reshape(near, few, LANES)
-
-
-def local_kernel(q_ref, k_ref, v_ref, rim_ref, taps_ref, gain_ref, query_ref, direct_ref):
+            out_ref[dests, at : at + few, :] = turned.reshape(near, few, LANES)
+
+        def known(first, last, j):
+            t0, t1, t2 = taps[j, 0:1, col], taps[j, 1:2, col], taps[j, 2:3, col]
+            own = t0 * first[0:1], t0 * first[1:2] + t1 * first[0:1]
+            following = t1 * last[1:2] + t2 * last[0:1], t2 * last[1:2]
+            return *own, *following
+
+        k0, k1, next_k0, next_k1 = known(keys[0:2, col], keys[rows - 2 : rows, col], 1)
+        v0, v1, next_v0, next_v1 = known(values[0:2, col], values[rows - 2 : rows, col], 2)
+        q0, q1, next_q0, next_q1 = known(ends[0:2, col], ends[14:16, col], 0)
+        nothing = jnp.zeros_like(q0)
+        at = base + few * (rows // LANES)
+        pairs = jnp.concatenate([k0, v0, k1, v1, next_k0, next_v0, next_k1, next_v1], axis=0)
+        others = [q0, q1, next_q0, next_q1, gain[:, col], nothing, nothing, nothing]
+        out_ref[dests, at, :] = block_turn(pairs, few)
+        out_ref[dests, at + 1, :] = block_turn(jnp.concatenate(others, axis=0), few)
+        for j in range(2, 8):
+            out_ref[dests, at + j, :] = jnp.zeros((near, LANES), F32)
+    for m, copy in enumerate(large):
+        copy.wait()
+        for i in range(blocks):
+            both = held[m, :, :, LANES * i : LANES * i + LANES].reshape(LANES, LANES)
+            out_ref[near * i : near * i + near, few * m : few * m + few, :] = both.T.reshape(near, few, LANES)
+
+
+def local_kernel(q_ref, k_ref, v_ref, taps_ref, gain_ref, query_ref, direct_ref):
     for i in range(q_ref.shape[1] // LANES):
         col = slice(LANES * i, LANES * i + LANES)
-        query_seq = causal(q_ref[:, col], rim_ref[0:2, col], taps_ref[0, :, col])
-        key_seq = causal(k_ref[:, col], rim_ref[2:4, col], taps_ref[1, :, col])
-        value_seq = causal(v_ref[:, col], rim_ref[4:6, col], taps_ref[2, :, col])
-        query_ref[:, col] = query_seq
-        direct_ref[:, col] = query_seq * (gain_ref[:, col] * (key_seq * value_seq))
+        query_seq = causal(q_ref[:, col], taps_ref[0, :, col])
+        key_seq = causal(k_ref[:, col], taps_ref[1, :, col])
+        value_seq = causal(v_ref[:, col], taps_ref[2, :, col])
+        direct = query_seq * (gain_ref[:, col] * (key_seq * value_seq))
+        row = lax.broadcasted_iota(jnp.int32, direct.shape, 0)
+        query_ref[:, col] = jnp.where(row < 2, 1.0, query_seq)
+        direct_ref[:, col] = jnp.where(row < 2, 0.0, direct)
 
 
 def gate_kernel(conv_ref, query_ref, direct_ref, out_ref):
@@ -296,6 +327,29 @@
     kept = devices + 1
     base, pitch = few * chunks, few + 1
     left, right = slice(0, LANES), slice(LANES, 2 * LANES)
+    lane_of = lax.broadcasted_iota(jnp.int32, (few, LANES), 1)
+
+    everyone = in_ref.shape[0]
+    begins = lax.broadcasted_iota(jnp.int32, (everyone, LANES), 0) % devices == 0
+    pairs, others = in_ref[:, base + 2 * few, :], in_ref[:, base + 2 * few + 1, :]
+
+    def before(x, lanes):
+        moved = pltpu.roll(pltpu.roll(x, 1, 0), LANES - lanes, 1)
+        return jnp.where(begins, 0.0, moved)
+
+    pairs = pairs + before(pairs, 4 * few)
+    query = others + before(others, 2 * few)
+    mixed = pairs * pltpu.roll(pairs, LANES - few, 1)
+    gain = pltpu.roll(others, LANES - 4 * few, 1)
+    mixed_second = pltpu.roll(mixed, LANES - 2 * few, 1)
+    query_second = pltpu.roll(query, LANES - few, 1)
+    ends = [mixed, mixed_second, query, query_second, query * gain * mixed, query_second * gain * mixed_second]
+    ends = [x.T[:few] for x in ends]
+
+    def first_lanes(pair, at):
+        first, second = (x[:, at : at + 1] for x in pair)
+        return jnp.where(lane_of == 0, first, second)
+
     odd_cos, odd_sin = parity_ref[0:1], parity_ref[1:2]
 
     def row_of(low_bit, s, q):
@@ -313,7 +367,13 @@
         tiles = []
         for h in range(2):
             at = base + few * h
-            tiles.append(spread([in_ref[q * devices + p, at : at + few, :] for p in range(devices)]))
+            x = [in_ref[q * devices + p, at : at + few, :] for p in range(devices)]
+            if h == 0:
+                x = [
+                    jnp.where(lane_of < 2, first_lanes(ends[:2], q * devices + p), own)
+                    for p, own in enumerate(x)
+                ]
+            tiles.append(spread(x))
         for s in range(kept):
             turned = []
             for (re, im), lane in zip((tiles[0][s], tiles[1][s]), (left, right)):
@@ -372,7 +432,11 @@
                 tile.append((re * cosine - im * sine, im * cosine + re * sine))
         for tile, lane in zip(tiles, (left, right)):
             for p, y in enumerate(gather(tile)):
-                out_ref[q * devices + p, :, lane] = y
+                at = q * devices + p
+                if lane == left:
+                    finished = first_lanes(ends[2:4], at) * y + first_lanes(ends[4:], at)
+                    y = jnp.where(lane_of < 2, finished, y)
+                out_ref[at, :, lane] = y
 
 
 def per_device_tiled(q_proj, k_proj, v_proj, short_filter, skip_gain, filter_spec):
@@ -382,61 +446,44 @@
     few = channels // everyone
     chunks = 2 * rows // parts // 64
     halves = rows // LANES
-    depth = few * (chunks + halves)
+    depth = few * (chunks + halves) + 8
     outer = 2 * devices
     whole = pl.BlockSpec(memory_space=pltpu.VMEM)
-
+    in_hbm = pl.BlockSpec(memory_space=pltpu.HBM)
     small = pltpu.CompilerParams(vmem_limit_bytes=16 << 20)
-    in_hbm = pl.BlockSpec(memory_space=pltpu.HBM)
+    gain_row = skip_gain[None, :]
+
     part = lax.axis_index("dp").reshape(1)
-    kept = [pltpu.with_memory_space_constraint(x, pltpu.HBM) for x in (q_proj, k_proj, v_proj, filter_spec)]
-    tails, own_spec = pl.pallas_call(
-        functools.partial(load_kernel, chunks),
-        out_shape=[
-            jax.ShapeDtypeStruct((6, channels), F32),
-            jax.ShapeDtypeStruct((2, 64 * chunks, channels), F32),
-        ],
-        in_specs=[pl.BlockSpec(memory_space=pltpu.SMEM)] + [in_hbm] * 4,
-        out_specs=[whole] * 2,
+    sources = (q_proj, k_proj, v_proj, short_filter, gain_row, filter_spec)
+    sent = pl.pallas_call(
+        functools.partial(pack_kernel, few, chunks),
+        out_shape=jax.ShapeDtypeStruct((everyone, depth, LANES), F32),
+        in_specs=[pl.BlockSpec(memory_space=pltpu.SMEM)] + [in_hbm] * 6,
+        out_specs=whole,
         compiler_params=small,
         scratch_shapes=[
-            pltpu.VMEM((3, 8, channels), F32),
-            pltpu.SemaphoreType.DMA((3,)),
-            pltpu.SemaphoreType.DMA,
+            pltpu.VMEM((16, channels), F32),
+            pltpu.VMEM((rows, channels), F32),
+            pltpu.VMEM((rows, channels), F32),
+            pltpu.VMEM((3, 3, channels), F32),
+            pltpu.VMEM((1, channels), F32),
+            pltpu.VMEM((chunks, 2, 64, channels), F32),
+            pltpu.SemaphoreType.DMA((6,)),
+            pltpu.SemaphoreType.DMA((chunks,)),
         ],
-    )(part, *kept)
-    rim = shifted(tails, "ctx", 1)
-
-    packed = jax.ShapeDtypeStruct((everyone, depth, LANES), F32)
-    held = pl.pallas_call(
-        functools.partial(spec_kernel, few),
-        out_shape=packed,
-        in_specs=[whole],
-        out_specs=whole,
-        compiler_params=small,
-        cost_estimate=pl.CostEstimate(flops=0, bytes_accessed=1 << 21, transcendentals=0),
-    )(own_spec)
-
-    sent = pl.pallas_call(
-        functools.partial(mixed_kernel, few, chunks),
-        out_shape=packed,
-        in_specs=[whole] * 5,
-        out_specs=whole,
-        input_output_aliases={4: 0},
-        compiler_params=small,
-        cost_estimate=pl.CostEstimate(flops=0, bytes_accessed=3 << 19, transcendentals=0),
-    )(k_proj, v_proj, rim, short_filter, held)
+        cost_estimate=pl.CostEstimate(flops=0, bytes_accessed=1 << 22, transcendentals=0),
+    )(part, *(pltpu.with_memory_space_constraint(x, pltpu.HBM) for x in sources))
 
     come = lax.all_to_all(sent, ("dp", "ctx"), 0, 0, tiled=True)
 
     query_seq, direct = pl.pallas_call(
         local_kernel,
         out_shape=[jax.ShapeDtypeStruct((rows, channels), F32)] * 2,
-        in_specs=[whole] * 6,
+        in_specs=[whole] * 5,
         out_specs=[whole] * 2,
         compiler_params=small,
         cost_estimate=pl.CostEstimate(flops=0, bytes_accessed=5 << 19, transcendentals=0),
-    )(q_proj, k_proj, v_proj, rim, short_filter, skip_gain[None, :])
+    )(q_proj, k_proj, v_proj, short_filter, gain_row)
 
     total = 2 * few * parts * (devices + 1)
     conv = pl.pallas_call(
@@ -471,7 +518,7 @@
     chunks = 2 * rows // parts // 64
     return (
         rest == 0
-        and few % 16 == 0
+        and few == 16
         and devices == 16
         and rows == 2 * LANES
         and parts * devices * chunks == LANES

time: 76.6 us -> 75.5 us (0.986)
  starting transfers between devices: 5.09 us -> 2.61 us
  Pallas kernels: 7.71 us -> 8.77 us
  blocking collectives: 47.4 us -> 48.3 us
    ppermute x1 -> x0, starting transfers between devices: 2.49 us -> none  [shifted(): return lax.ppermute(block, axis, route)]
    all_to_all x1, blocking collectives: 47.4 us -> 48.3 us  [per_device_tiled(): come = lax.all_to_all(sent, ('dp', 'ctx'), 0, 0, tiled=True)]
    pallas_call x3 -> x1, Pallas kernels: 2.03 us -> 2.63 us  [per_device_tiled(): pl.pallas_call(functools.partial(pack_kernel, few, chunks), out_shape=jax...]
  transfers between devices with their start and end apart: 2 -> 1, of which waited for: 2 -> 1; matrix products, arithmetic and copies ran while one was open for 0% -> 0% of each run, Pallas kernels for 1% -> 1%
where the time goes in v6:
time: 75.5 us; the launch traced here: 75.3 us
  blocking collectives  48.3 us (64%)
  waiting for transfers between devices  15.3 us (20%)
  Pallas kernels  8.77 us (12%)
  starting transfers between devices  2.61 us (3%)
    all_to_all x1, blocking collectives, per_device_tiled(): come = lax.all_to_all(sent, ('dp', 'ctx'), 0, 0, tiled=True)  48.3 us
    all_to_all x1, waiting for transfers between devices, per_device_tiled(): back = lax.all_to_all(conv, ('dp', 'ctx'), 0, 0, tiled=True)  15.3 us
    pallas_call x1, Pallas kernels, per_device_tiled(): pl.pallas_call(functools.partial(conv_kernel, parts, few, chunks), out_sh...  4.62 us
    pallas_call x1, Pallas kernels, per_device_tiled(): pl.pallas_call(functools.partial(pack_kernel, few, chunks), out_shape=jax...  2.63 us
    all_to_all x1, starting transfers between devices, per_device_tiled(): back = lax.all_to_all(conv, ('dp', 'ctx'), 0, 0, tiled=True)  2.61 us
  transfers between devices with their start and end apart: 1, of which 1 were waited for; matrix products, arithmetic and copies ran while one was open for 0% of the time, Pallas kernels for 1%

profile of v6, /device:TPU:0, one launch (start us, length us, event | category | flops | bytes accessed | tf_op | source)
XLA Modules:
  0.0 75.3 jit_solution(13595914728923501938)
XLA Ops:
  0.0 2.6 %shard_map.109 = f32[32,104,128]{2,1,0:T(8,128)S(1)} custom-call(s32[1]{0:T(128)} %bitcast.part_ref, f32[256,512]{1,0:T(8,128)} %q_ref.3, f32[256,512]{1,0:T(8,128)} %k_ref.3, f32[256,512]{1,0:T(8,128)} %v_ref.3, f32[3,3,512]{2,1,0:T(4,128)} %taps_ref.3, f32[1,512]{1,0:T(1,128)} %bitcast.2, f32[2,512,512]{2,1,0:T(8,128)} %spec_ref.1), custom_call_target="tpu_custom_call" | custom-call | bytes 4194304 | tf_op jit(solution)/shard_map/pallas_call | solution.py:458
  2.6 0.0 copy-start.3
  2.7 0.0 copy-start.4
  2.7 0.0 copy-start.5
  2.7 0.0 copy-start.7
  2.7 0.0 copy-start.9
  2.7 48.3 %all_to_all.10.in_ref = f32[32,104,128]{2,1,0:T(8,128)S(1)} all-to-all(f32[32,104,128]{2,1,0:T(8,128)S(1)} %shard_map.109), channel_id=1, replica_groups=mesh['dp'=2,'ctx'=16] {'dp','ctx'}, dimensions={0} | all-to-all | bytes 3407872 | tf_op jit(solution)/shard_map/all_to_all | solution.py:477
  51.0 0.0 copy-done.3
  51.0 0.0 copy-done.4
  51.0 0.0 copy-done.5
  51.0 0.0 copy-done.7
  51.1 0.0 copy-done.9
  51.1 0.0 copy-start
  51.1 0.0 copy-start.1
  51.1 0.0 copy-start.2
  51.1 0.0 copy-start.6
  51.1 0.0 copy-start.8
  51.1 4.6 %shard_map.110 = f32[32,16,256]{2,1,0:T(8,128)} custom-call(f32[32,104,128]{2,1,0:T(8,128)S(1)} %all_to_all.10.in_ref, f32[4,17,256]{2,1,0:T(8,128)S(1)} %copy-done.5, f32[2,128]{1,0:T(2,128)S(1)} %copy-done.9, bf16[768,256]{1,0:T(8,128)(2,1)S(1)} %copy-done.3, bf16[768,256]{1,0:T(8,128)(2,1)S(1)} %copy-done.4, bf16[256,128]{1,0:T(8,128)(2,1)S(1)} %copy-done.7), custom_call_target="tpu_custom_call" | custom-call | bytes 4194304 | tf_op jit(solution)/shard_map/pallas_call | solution.py:489
  55.7 2.6 %all-to-all-start.1 = ((f32[32,16,256]{2,1,0:T(8,128)}), f32[32,16,256]{2,1,0:T(8,128)S(1)}, u32[]{:S(2)}, u32[]{:S(2)}) async-start(f32[32,16,256]{2,1,0:T(8,128)} %shard_map.110), calls=%async_computation.1 | async-start | bytes 1048576 | tf_op jit(solution)/shard_map/all_to_all | solution.py:504
  58.4 0.0 copy-done
  58.4 0.0 copy-done.1
  58.4 0.0 copy-done.2
  58.4 0.0 copy-done.6
  58.4 0.0 copy-done.8
  58.4 0.5 shard_map.111
  58.9 15.3 %all-to-all-done.1.conv_ref = f32[32,16,256]{2,1,0:T(8,128)S(1)} async-done(((f32[32,16,256]{2,1,0:T(8,128)}), f32[32,16,256]{2,1,0:T(8,128)S(1)}, u32[]{:S(2)}, u32[]{:S(2)}) %all-to-all-start.1) | async-done | bytes 524320 | tf_op jit(solution)/shard_map/all_to_all | solution.py:504
  74.3 1.0 %shard_map.112 = f32[256,512]{1,0:T(8,128)} custom-call(f32[32,16,256]{2,1,0:T(8,128)S(1)} %all-to-all-done.1.conv_ref, f32[256,512]{1,0:T(8,128)S(1)} %get-tuple-element.7.query_ref, f32[256,512]{1,0:T(8,128)S(1)} %get-tuple-element.8.direct_ref), custom_call_target="tpu_custom_call" | custom-call | bytes 2097152 | tf_op jit(solution)/shard_map/pallas_call | solution.py:505
Async XLA Ops:
  2.6 48.4 %copy-start.3 = (bf16[768,256]{1,0:T(8,128)(2,1)S(1)}, bf16[768,256]{1,0:T(8,128)(2,1)}, u32[]{:S(2)}) copy-start(bf16[768,256]{1,0:T(8,128)(2,1)} %constant.18.clone.fore_ref) | copy-start | bytes 1179652
  2.7 48.4 %copy-start.4 = (bf16[768,256]{1,0:T(8,128)(2,1)S(1)}, bf16[768,256]{1,0:T(8,128)(2,1)}, u32[]{:S(2)}) copy-start(bf16[768,256]{1,0:T(8,128)(2,1)} %constant.19.clone.back_ref) | copy-start | bytes 1179652
  2.7 48.4 %copy-start.5 = (f32[4,17,256]{2,1,0:T(8,128)S(1)}, f32[4,17,256]{2,1,0:T(8,128)}, u32[]{:S(2)}) copy-start(f32[4,17,256]{2,1,0:T(8,128)} %constant.16.clone.turn_ref) | copy-start | bytes 208900
  2.7 48.4 %copy-start.7 = (bf16[256,128]{1,0:T(8,128)(2,1)S(1)}, bf16[256,128]{1,0:T(8,128)(2,1)}, u32[]{:S(2)}) copy-start(bf16[256,128]{1,0:T(8,128)(2,1)} %constant.20.clone.flip_ref) | copy-start | bytes 196612
  2.7 48.4 %copy-start.9 = (f32[2,128]{1,0:T(2,128)S(1)}, f32[2,128]{1,0:T(2,128)}, u32[]{:S(2)}) copy-start(f32[2,128]{1,0:T(2,128)} %constant.17.clone.parity_ref) | copy-start | bytes 3076
  51.1 7.3 %copy-start = (f32[256,512]{1,0:T(8,128)S(1)}, f32[256,512]{1,0:T(8,128)}, u32[]{:S(2)}) copy-start(f32[256,512]{1,0:T(8,128)} %q_ref.3) | copy-start | bytes 1572868
  51.1 7.3 %copy-start.1 = (f32[256,512]{1,0:T(8,128)S(1)}, f32[256,512]{1,0:T(8,128)}, u32[]{:S(2)}) copy-start(f32[256,512]{1,0:T(8,128)} %k_ref.3) | copy-start | bytes 1572868
  51.1 7.3 %copy-start.2 = (f32[256,512]{1,0:T(8,128)S(1)}, f32[256,512]{1,0:T(8,128)}, u32[]{:S(2)}) copy-start(f32[256,512]{1,0:T(8,128)} %v_ref.3) | copy-start | bytes 1572868
  51.1 7.3 %copy-start.6 = (f32[3,3,512]{2,1,0:T(4,128)S(1)}, f32[3,3,512]{2,1,0:T(4,128)}, u32[]{:S(2)}) copy-start(f32[3,3,512]{2,1,0:T(4,128)} %taps_ref.3) | copy-start | bytes 55300
  51.1 7.3 %copy-start.8 = (f32[512]{0:T(512)S(1)}, f32[512]{0:T(512)}, u32[]{:S(2)}) copy-start(f32[512]{0:T(512)} %param.15) | copy-start | bytes 6148
  55.7 18.5 %all-to-all-start.1 = ((f32[32,16,256]{2,1,0:T(8,128)}), f32[32,16,256]{2,1,0:T(8,128)S(1)}, u32[]{:S(2)}, u32[]{:S(2)}) async-start(f32[32,16,256]{2,1,0:T(8,128)} %shard_map.110), calls=%async_computation.1 | async-start | bytes 1048576 | tf_op jit(solution)/shard_map/all_to_all | solution.py:504

commit v7 on v6

--- a/solution.py
+++ b/solution.py
@@ -1,4 +1,5 @@
 import functools
+import itertools
 import math
 
 import jax
@@ -235,36 +236,50 @@
 
 def pack_kernel(
     few, chunks, part_ref, q_ref, k_ref, v_ref, taps_ref, gain_ref, spec_ref,
-    out_ref, ends, keys, values, taps, gain, held, sems, held_sems,
+    out_ref, ends, keys, values, taps, gain, held, sems, held_sems, key_sems,
 ):
     rows = q_ref.shape[0]
     near = LANES // few
     start = pl.multiple_of(part_ref[0] * (64 * chunks), 64 * chunks)
-    small = [
-        pltpu.make_async_copy(src, dst, sems.at[i])
-        for i, (src, dst) in enumerate(
-            (
-                (taps_ref, taps),
-                (gain_ref, gain),
-                (q_ref.at[0:8], ends.at[0:8]),
-                (q_ref.at[rows - 8 : rows], ends.at[8:16]),
-                (k_ref, keys),
-                (v_ref, values),
-            )
-        )
+    blocks = k_ref.shape[1] // LANES
+    base = few * chunks
+
+    def columns(i):
+        return slice(LANES * i, LANES * i + LANES)
+
+    def chunk_rows(m):
+        return spec_ref.at[:, pl.ds(start + 64 * m, 64), :]
+
+    small = [(taps_ref, taps), (gain_ref, gain)]
+    small += [(q_ref.at[0:8], ends.at[0:8]), (q_ref.at[rows - 8 : rows], ends.at[8:16])]
+    small = [pltpu.make_async_copy(*pair, sems.at[i]) for i, pair in enumerate(small)]
+    large = [pltpu.make_async_copy(chunk_rows(m), held.at[m], held_sems.at[m]) for m in range(chunks)]
+    inputs = [
+        [
+            pltpu.make_async_copy(src.at[:, columns(i)], dst.at[:, columns(i)], key_sems.at[j, i])
+            for j, (src, dst) in enumerate(((k_ref, keys), (v_ref, values)))
+        ]
+        for i in range(blocks)
     ]
-    large = [
-        pltpu.make_async_copy(spec_ref.at[:, pl.ds(start + 64 * m, 64), :], held.at[m], held_sems.at[m])
-        for m in range(chunks)
-    ]
-    for copy in small + large:
+    for copy in (large[0], *small, *inputs[0], *large[1:], *sum(inputs[1:], [])):
         copy.start()
+
+    def turn_chunk(m):
+        large[m].wait()
+        for i in range(blocks):
+            both = held[m, :, :, columns(i)].reshape(LANES, LANES)
+            out_ref[near * i : near * i + near, few * m : few * m + few, :] = both.T.reshape(near, few, LANES)
+
+    turn_chunk(0)
     for copy in small:
         copy.wait()
-    blocks = k_ref.shape[1] // LANES
-    base = few * chunks
     for i in range(blocks):
-        col = slice(LANES * i, LANES * i + LANES)
+        if i == 1:
+            for m in range(1, chunks):
+                turn_chunk(m)
+        for copy in inputs[i]:
+            copy.wait()
+        col = columns(i)
         dests = slice(near * i, near * i + near)
         mixed_in = causal(keys[:, col], taps[1, :, col]) * causal(values[:, col], taps[2, :, col])
         for h in range(rows // LANES):
@@ -289,11 +304,6 @@
         out_ref[dests, at + 1, :] = block_turn(jnp.concatenate(others, axis=0), few)
         for j in range(2, 8):
             out_ref[dests, at + j, :] = jnp.zeros((near, LANES), F32)
-    for m, copy in enumerate(large):
-        copy.wait()
-        for i in range(blocks):
-            both = held[m, :, :, LANES * i : LANES * i + LANES].reshape(LANES, LANES)
-            out_ref[near * i : near * i + near, few * m : few * m + few, :] = both.T.reshape(near, few, LANES)
 
 
 def local_kernel(q_ref, k_ref, v_ref, taps_ref, gain_ref, query_ref, direct_ref):
@@ -308,19 +318,24 @@
         direct_ref[:, col] = jnp.where(row < 2, 0.0, direct)
 
 
-def gate_kernel(conv_ref, query_ref, direct_ref, out_ref):
+def gate_kernel(conv_ref, query_ref, direct_ref, out_ref, gated, sems):
     few = conv_ref.shape[1]
     near = LANES // few
-    for i in range(conv_ref.shape[0] // near):
-        col = slice(LANES * i, LANES * i + LANES)
-        for h in range(conv_ref.shape[2] // LANES):
-            row = slice(LANES * h, LANES * h + LANES)
+    leaving = []
+    for h in range(conv_ref.shape[2] // LANES):
+        row = slice(LANES * h, LANES * h + LANES)
+        for i in range(conv_ref.shape[0] // near):
+            col = slice(LANES * i, LANES * i + LANES)
             conv = conv_ref[near * i : near * i + near, :, row].reshape(LANES, LANES)
-            out_ref[row, col] = query_ref[row, col] * conv.T + direct_ref[row, col]
+            gated[row, col] = query_ref[row, col] * conv.T + direct_ref[row, col]
+        leaving.append(pltpu.make_async_copy(gated.at[row], out_ref.at[row], sems.at[h]))
+        leaving[h].start()
+    for copy in leaving:
+        copy.wait()
 
 
 def conv_kernel(
-    parts, few, chunks, in_ref, turn_ref, parity_ref, fore_ref, back_ref, flip_ref, out_ref, spec, triple, freq, undo
+    parts, few, chunks, in_ref, turn_ref, parity_ref, fore_ref, back_ref, flip_ref, out_ref, spec, triple, freq, undo, ends
 ):
     devices = in_ref.shape[0] // parts
     outer = 2 * devices
@@ -343,12 +358,15 @@
     gain = pltpu.roll(others, LANES - 4 * few, 1)
     mixed_second = pltpu.roll(mixed, LANES - 2 * few, 1)
     query_second = pltpu.roll(query, LANES - few, 1)
-    ends = [mixed, mixed_second, query, query_second, query * gain * mixed, query_second * gain * mixed_second]
-    ends = [x.T[:few] for x in ends]
-
-    def first_lanes(pair, at):
-        first, second = (x[:, at : at + 1] for x in pair)
-        return jnp.where(lane_of == 0, first, second)
+    direct = query * gain * mixed, query_second * gain * mixed_second
+    for r, group in enumerate(((mixed, query, direct[0]), (mixed_second, query_second, direct[1]))):
+        for j, x in enumerate(group):
+            ends[pl.ds(2 * everyone * j + r, everyone, stride=2), :] = x
+    ends_of = [ends[2 * everyone * j : 2 * everyone * (j + 1)].T[:few] for j in range(3)]
+
+    def first_lanes(j, at):
+        wide = jnp.concatenate([ends_of[j]] * (LANES // (2 * everyone)), axis=1)
+        return pltpu.roll(wide, (LANES - 2 * at) % LANES, 1) if at else wide
 
     odd_cos, odd_sin = parity_ref[0:1], parity_ref[1:2]
 
@@ -370,7 +388,7 @@
             x = [in_ref[q * devices + p, at : at + few, :] for p in range(devices)]
             if h == 0:
                 x = [
-                    jnp.where(lane_of < 2, first_lanes(ends[:2], q * devices + p), own)
+                    jnp.where(lane_of < 2, first_lanes(0, q * devices + p), own)
                     for p, own in enumerate(x)
                 ]
             tiles.append(spread(x))
@@ -386,11 +404,14 @@
             re, im = c_sub(*turned)
             keep(row_of(1, s, q), re * odd_cos + im * odd_sin, im * odd_cos - re * odd_sin)
 
-    freq[...] = dot(triple[...], fore_ref[...])
-
-    for c in range(few):
-        own = jnp.concatenate([in_ref[:, few * m + c, :] for m in range(chunks)], axis=0)
-        spec[pl.ds(c, 4 * outer, stride=pitch), :] = own.T
+    pieces = 4
+    size = freq.shape[0] // pieces
+    for j in range(pieces):
+        span = slice(j * size, (j + 1) * size)
+        freq[span] = dot(triple[span], fore_ref[...])
+        for c in range(j * few // pieces, (j + 1) * few // pieces):
+            own = jnp.concatenate([in_ref[:, few * m + c, :] for m in range(chunks)], axis=0)
+            spec[pl.ds(c, 4 * outer, stride=pitch), :] = own.T
 
     other = [[None, None], [None, None]]
     count = outer - kept
@@ -409,15 +430,16 @@
             own = own - mirror if i else own + mirror
         return own
 
-    for low_bit in range(2):
-        for s in range(kept):
+    cuts = (0, kept // 2, kept)
+    for low_bit, (begin, end) in itertools.product(range(2), zip(cuts[:-1], cuts[1:])):
+        for s in range(begin, end):
             h_re, h_im = response(0, low_bit, s), response(1, low_bit, s)
             for q in range(parts):
                 span = row_of(low_bit, s, q)
                 re, im = freq[span, left], freq[span, right]
                 keep(span, re * h_re - im * h_im, re * h_im + im * h_re)
-
-    undo[...] = dot(triple[...], back_ref[...])
+        span = slice(row_of(low_bit, begin, 0).start, row_of(low_bit, end, 0).start)
+        undo[span] = dot(triple[span], back_ref[...])
 
     for q in range(parts):
         tiles = [], []
@@ -434,7 +456,7 @@
             for p, y in enumerate(gather(tile)):
                 at = q * devices + p
                 if lane == left:
-                    finished = first_lanes(ends[2:4], at) * y + first_lanes(ends[4:], at)
+                    finished = first_lanes(1, at) * y + first_lanes(2, at)
                     y = jnp.where(lane_of < 2, finished, y)
                 out_ref[at, :, lane] = y
 
@@ -468,8 +490,9 @@
             pltpu.VMEM((3, 3, channels), F32),
             pltpu.VMEM((1, channels), F32),
             pltpu.VMEM((chunks, 2, 64, channels), F32),
-            pltpu.SemaphoreType.DMA((6,)),
+            pltpu.SemaphoreType.DMA((4,)),
             pltpu.SemaphoreType.DMA((chunks,)),
+            pltpu.SemaphoreType.DMA((2, channels // LANES)),
         ],
         cost_estimate=pl.CostEstimate(flops=0, bytes_accessed=1 << 22, transcendentals=0),
     )(part, *(pltpu.with_memory_space_constraint(x, pltpu.HBM) for x in sources))
@@ -496,6 +519,7 @@
             pltpu.VMEM((total, 6 * LANES), BF16),
             pltpu.VMEM((total, 2 * LANES), F32),
             pltpu.VMEM((total, 2 * LANES), F32),
+            pltpu.VMEM((6 * everyone, LANES), F32),
         ],
         compiler_params=small,
         cost_estimate=pl.CostEstimate(flops=0, bytes_accessed=4 << 20, transcendentals=0),
@@ -506,7 +530,8 @@
         gate_kernel,
         out_shape=jax.ShapeDtypeStruct((rows, channels), F32),
         in_specs=[whole] * 3,
-        out_specs=whole,
+        out_specs=in_hbm,
+        scratch_shapes=[pltpu.VMEM((rows, channels), F32), pltpu.SemaphoreType.DMA((halves,))],
         compiler_params=small,
         cost_estimate=pl.CostEstimate(flops=0, bytes_accessed=1 << 21, transcendentals=0),
     )(back, query_seq, direct)

time: 75.5 us -> 75.1 us (level)
  no operation moved by 1% of the time
where the time goes in v7:
time: 75.1 us; the launch traced here: 74.8 us
  blocking collectives  48.3 us (64%)
  waiting for transfers between devices  15.3 us (20%)
  Pallas kernels  8.31 us (11%)
  starting transfers between devices  2.61 us (3%)
    all_to_all x1, blocking collectives, per_device_tiled(): come = lax.all_to_all(sent, ('dp', 'ctx'), 0, 0, tiled=True)  48.3 us
    all_to_all x1, waiting for transfers between devices, per_device_tiled(): back = lax.all_to_all(conv, ('dp', 'ctx'), 0, 0, tiled=True)  15.3 us
    pallas_call x1, Pallas kernels, per_device_tiled(): pl.pallas_call(functools.partial(conv_kernel, parts, few, chunks), out_sh...  4.23 us
    pallas_call x1, Pallas kernels, per_device_tiled(): pl.pallas_call(functools.partial(pack_kernel, few, chunks), out_shape=jax...  2.62 us
    all_to_all x1, starting transfers between devices, per_device_tiled(): back = lax.all_to_all(conv, ('dp', 'ctx'), 0, 0, tiled=True)  2.61 us
  transfers between devices with their start and end apart: 1, of which 1 were waited for; matrix products, arithmetic and copies ran while one was open for 0% of the time, Pallas kernels for 1%

profile of v7, /device:TPU:0, one launch (start us, length us, event | category | flops | bytes accessed | tf_op | source)
XLA Modules:
  0.0 74.8 jit_solution(1870718639536751763)
XLA Ops:
  0.0 2.6 %shard_map.109 = f32[32,104,128]{2,1,0:T(8,128)S(1)} custom-call(s32[1]{0:T(128)} %bitcast.part_ref, f32[256,512]{1,0:T(8,128)} %q_ref.3, f32[256,512]{1,0:T(8,128)} %k_ref.3, f32[256,512]{1,0:T(8,128)} %v_ref.3, f32[3,3,512]{2,1,0:T(4,128)} %taps_ref.3, f32[1,512]{1,0:T(1,128)} %bitcast.2, f32[2,512,512]{2,1,0:T(8,128)} %spec_ref.1), custom_call_target="tpu_custom_call" | custom-call | bytes 4194304 | tf_op jit(solution)/shard_map/pallas_call | solution.py:480
  2.6 0.0 copy-start.3
  2.6 0.0 copy-start.4
  2.7 0.0 copy-start.5
  2.7 0.0 copy-start.7
  2.7 0.0 copy-start.9
  2.7 48.3 %all_to_all.10.in_ref = f32[32,104,128]{2,1,0:T(8,128)S(1)} all-to-all(f32[32,104,128]{2,1,0:T(8,128)S(1)} %shard_map.109), channel_id=1, replica_groups=mesh['dp'=2,'ctx'=16] {'dp','ctx'}, dimensions={0} | all-to-all | bytes 3407872 | tf_op jit(solution)/shard_map/all_to_all | solution.py:500
  51.0 0.0 copy-done.3
  51.0 0.0 copy-done.4
  51.0 0.0 copy-done.5
  51.0 0.0 copy-done.7
  51.0 0.0 copy-done.9
  51.1 0.0 copy-start
  51.1 0.0 copy-start.1
  51.1 0.0 copy-start.2
  51.1 0.0 copy-start.6
  51.1 0.0 copy-start.8
  51.1 4.2 %shard_map.110 = f32[32,16,256]{2,1,0:T(8,128)} custom-call(f32[32,104,128]{2,1,0:T(8,128)S(1)} %all_to_all.10.in_ref, f32[4,17,256]{2,1,0:T(8,128)S(1)} %copy-done.5, f32[2,128]{1,0:T(2,128)S(1)} %copy-done.9, bf16[768,256]{1,0:T(8,128)(2,1)S(1)} %copy-done.3, bf16[768,256]{1,0:T(8,128)(2,1)S(1)} %copy-done.4, bf16[256,128]{1,0:T(8,128)(2,1)S(1)} %copy-done.7), custom_call_target="tpu_custom_call" | custom-call | bytes 4194304 | tf_op jit(solution)/shard_map/pallas_call | solution.py:512
  55.3 2.6 %all-to-all-start.1 = ((f32[32,16,256]{2,1,0:T(8,128)}), f32[32,16,256]{2,1,0:T(8,128)S(1)}, u32[]{:S(2)}, u32[]{:S(2)}) async-start(f32[32,16,256]{2,1,0:T(8,128)} %shard_map.110), calls=%async_computation.1 | async-start | bytes 1048576 | tf_op jit(solution)/shard_map/all_to_all | solution.py:528
  58.0 0.0 copy-done
  58.0 0.0 copy-done.1
  58.0 0.0 copy-done.2
  58.0 0.0 copy-done.6
  58.0 0.0 copy-done.8
  58.0 0.5 shard_map.111
  58.5 15.3 %all-to-all-done.1.conv_ref = f32[32,16,256]{2,1,0:T(8,128)S(1)} async-done(((f32[32,16,256]{2,1,0:T(8,128)}), f32[32,16,256]{2,1,0:T(8,128)S(1)}, u32[]{:S(2)}, u32[]{:S(2)}) %all-to-all-start.1) | async-done | bytes 524320 | tf_op jit(solution)/shard_map/all_to_all | solution.py:528
  73.9 0.9 %shard_map.112 = f32[256,512]{1,0:T(8,128)} custom-call(f32[32,16,256]{2,1,0:T(8,128)S(1)} %all-to-all-done.1.conv_ref, f32[256,512]{1,0:T(8,128)S(1)} %get-tuple-element.7.query_ref, f32[256,512]{1,0:T(8,128)S(1)} %get-tuple-element.8.direct_ref), custom_call_target="tpu_custom_call" | custom-call | bytes 2097152 | tf_op jit(solution)/shard_map/pallas_call | solution.py:529
Async XLA Ops:
  2.6 48.4 %copy-start.3 = (bf16[768,256]{1,0:T(8,128)(2,1)S(1)}, bf16[768,256]{1,0:T(8,128)(2,1)}, u32[]{:S(2)}) copy-start(bf16[768,256]{1,0:T(8,128)(2,1)} %constant.18.clone.fore_ref) | copy-start | bytes 1179652
  2.6 48.4 %copy-start.4 = (bf16[768,256]{1,0:T(8,128)(2,1)S(1)}, bf16[768,256]{1,0:T(8,128)(2,1)}, u32[]{:S(2)}) copy-start(bf16[768,256]{1,0:T(8,128)(2,1)} %constant.19.clone.back_ref) | copy-start | bytes 1179652
  2.7 48.4 %copy-start.5 = (f32[4,17,256]{2,1,0:T(8,128)S(1)}, f32[4,17,256]{2,1,0:T(8,128)}, u32[]{:S(2)}) copy-start(f32[4,17,256]{2,1,0:T(8,128)} %constant.16.clone.turn_ref) | copy-start | bytes 208900
  2.7 48.4 %copy-start.7 = (bf16[256,128]{1,0:T(8,128)(2,1)S(1)}, bf16[256,128]{1,0:T(8,128)(2,1)}, u32[]{:S(2)}) copy-start(bf16[256,128]{1,0:T(8,128)(2,1)} %constant.20.clone.flip_ref) | copy-start | bytes 196612
  2.7 48.4 %copy-start.9 = (f32[2,128]{1,0:T(2,128)S(1)}, f32[2,128]{1,0:T(2,128)}, u32[]{:S(2)}) copy-start(f32[2,128]{1,0:T(2,128)} %constant.17.clone.parity_ref) | copy-start | bytes 3076
  51.1 6.9 %copy-start = (f32[256,512]{1,0:T(8,128)S(1)}, f32[256,512]{1,0:T(8,128)}, u32[]{:S(2)}) copy-start(f32[256,512]{1,0:T(8,128)} %q_ref.3) | copy-start | bytes 1572868
  51.1 6.9 %copy-start.1 = (f32[256,512]{1,0:T(8,128)S(1)}, f32[256,512]{1,0:T(8,128)}, u32[]{:S(2)}) copy-start(f32[256,512]{1,0:T(8,128)} %k_ref.3) | copy-start | bytes 1572868
  51.1 6.9 %copy-start.2 = (f32[256,512]{1,0:T(8,128)S(1)}, f32[256,512]{1,0:T(8,128)}, u32[]{:S(2)}) copy-start(f32[256,512]{1,0:T(8,128)} %v_ref.3) | copy-start | bytes 1572868
  51.1 6.9 %copy-start.6 = (f32[3,3,512]{2,1,0:T(4,128)S(1)}, f32[3,3,512]{2,1,0:T(4,128)}, u32[]{:S(2)}) copy-start(f32[3,3,512]{2,1,0:T(4,128)} %taps_ref.3) | copy-start | bytes 55300
  51.1 6.9 %copy-start.8 = (f32[512]{0:T(512)S(1)}, f32[512]{0:T(512)}, u32[]{:S(2)}) copy-start(f32[512]{0:T(512)} %param.15) | copy-start | bytes 6148
  55.3 18.5 %all-to-all-start.1 = ((f32[32,16,256]{2,1,0:T(8,128)}), f32[32,16,256]{2,1,0:T(8,128)S(1)}, u32[]{:S(2)}, u32[]{:S(2)}) async-start(f32[32,16,256]{2,1,0:T(8,128)} %shard_map.110), calls=%async_computation.1 | async-start | bytes 1048576 | tf_op jit(solution)/shard_map/all_to_all | solution.py:528

commit v8 on v7

--- a/solution.py
+++ b/solution.py
@@ -93,8 +93,8 @@
     outer, seq = 2 * devices, devices * rows
     freq = 2 * seq
     chunks = rows * 2 // parts // 64
-    low_bit, chunk, part, dev = np.meshgrid(
-        np.arange(2), np.arange(chunks), np.arange(parts), np.arange(devices), indexing="ij"
+    low_bit, chunk, dev, part = np.meshgrid(
+        np.arange(2), np.arange(chunks), np.arange(devices), np.arange(parts), indexing="ij"
     )
     k = (dev * (2 * rows // outer) + part * (2 * rows // parts // outer) + 2 * chunk + low_bit).ravel()
 
@@ -345,11 +345,11 @@
     lane_of = lax.broadcasted_iota(jnp.int32, (few, LANES), 1)
 
     everyone = in_ref.shape[0]
-    begins = lax.broadcasted_iota(jnp.int32, (everyone, LANES), 0) % devices == 0
+    begins = lax.broadcasted_iota(jnp.int32, (everyone, LANES), 0) < parts
     pairs, others = in_ref[:, base + 2 * few, :], in_ref[:, base + 2 * few + 1, :]
 
     def before(x, lanes):
-        moved = pltpu.roll(pltpu.roll(x, 1, 0), LANES - lanes, 1)
+        moved = pltpu.roll(pltpu.roll(x, parts, 0), LANES - lanes, 1)
         return jnp.where(begins, 0.0, moved)
 
     pairs = pairs + before(pairs, 4 * few)
@@ -385,10 +385,10 @@
         tiles = []
         for h in range(2):
             at = base + few * h
-            x = [in_ref[q * devices + p, at : at + few, :] for p in range(devices)]
+            x = [in_ref[p * parts + q, at : at + few, :] for p in range(devices)]
             if h == 0:
                 x = [
-                    jnp.where(lane_of < 2, first_lanes(0, q * devices + p), own)
+                    jnp.where(lane_of < 2, first_lanes(0, p * parts + q), own)
                     for p, own in enumerate(x)
                 ]
             tiles.append(spread(x))
@@ -454,7 +454,7 @@
                 tile.append((re * cosine - im * sine, im * cosine + re * sine))
         for tile, lane in zip(tiles, (left, right)):
             for p, y in enumerate(gather(tile)):
-                at = q * devices + p
+                at = p * parts + q
                 if lane == left:
                     finished = first_lanes(1, at) * y + first_lanes(2, at)
                     y = jnp.where(lane_of < 2, finished, y)
@@ -497,7 +497,7 @@
         cost_estimate=pl.CostEstimate(flops=0, bytes_accessed=1 << 22, transcendentals=0),
     )(part, *(pltpu.with_memory_space_constraint(x, pltpu.HBM) for x in sources))
 
-    come = lax.all_to_all(sent, ("dp", "ctx"), 0, 0, tiled=True)
+    come = lax.all_to_all(sent, ("ctx", "dp"), 0, 0, tiled=True)
 
     query_seq, direct = pl.pallas_call(
         local_kernel,
@@ -525,7 +525,7 @@
         cost_estimate=pl.CostEstimate(flops=0, bytes_accessed=4 << 20, transcendentals=0),
     )(come, *(jnp.asarray(t) for t in tables(parts, devices, rows)))
 
-    back = lax.all_to_all(conv, ("dp", "ctx"), 0, 0, tiled=True)
+    back = lax.all_to_all(conv, ("ctx", "dp"), 0, 0, tiled=True)
     return pl.pallas_call(
         gate_kernel,
         out_shape=jax.ShapeDtypeStruct((rows, channels), F32),

time: 75.1 us -> 74.9 us (level)
  starting transfers between devices: 2.61 us -> 3.67 us
  waiting for transfers between devices: 15.3 us -> 14.4 us
  blocking collectives: 48.3 us -> 47.4 us
    all_to_all x1, starting transfers between devices: 2.61 us -> 3.67 us  [per_device_tiled(): back = lax.all_to_all(conv, ('ctx', 'dp'), 0, 0, tiled=True)]
    all_to_all x1, blocking collectives: 48.3 us -> 47.4 us  [per_device_tiled(): come = lax.all_to_all(sent, ('ctx', 'dp'), 0, 0, tiled=True)]
    all_to_all x1, waiting for transfers between devices: 15.3 us -> 14.4 us  [per_device_tiled(): back = lax.all_to_all(conv, ('ctx', 'dp'), 0, 0, tiled=True)]
where the time goes in v8:
time: 74.9 us; the launch traced here: 74 us
  blocking collectives  47.4 us (63%)
  waiting for transfers between devices  14.4 us (19%)
  Pallas kernels  8.31 us (11%)
  starting transfers between devices  3.67 us (5%)
    all_to_all x1, blocking collectives, per_device_tiled(): come = lax.all_to_all(sent, ('ctx', 'dp'), 0, 0, tiled=True)  47.4 us
    all_to_all x1, waiting for transfers between devices, per_device_tiled(): back = lax.all_to_all(conv, ('ctx', 'dp'), 0, 0, tiled=True)  14.4 us
    pallas_call x1, Pallas kernels, per_device_tiled(): pl.pallas_call(functools.partial(conv_kernel, parts, few, chunks), out_sh...  4.23 us
    all_to_all x1, starting transfers between devices, per_device_tiled(): back = lax.all_to_all(conv, ('ctx', 'dp'), 0, 0, tiled=True)  3.67 us
    pallas_call x1, Pallas kernels, per_device_tiled(): pl.pallas_call(functools.partial(pack_kernel, few, chunks), out_shape=jax...  2.62 us
  transfers between devices with their start and end apart: 1, of which 1 were waited for; matrix products, arithmetic and copies ran while one was open for 0% of the time, Pallas kernels for 1%

profile of v8, /device:TPU:0, one launch (start us, length us, event | category | flops | bytes accessed | tf_op | source)
XLA Modules:
  0.0 74.0 jit_solution(6434542335302850533)
XLA Ops:
  0.0 2.6 %shard_map.109 = f32[32,104,128]{2,1,0:T(8,128)S(1)} custom-call(s32[1]{0:T(128)} %bitcast.part_ref, f32[256,512]{1,0:T(8,128)} %q_ref.3, f32[256,512]{1,0:T(8,128)} %k_ref.3, f32[256,512]{1,0:T(8,128)} %v_ref.3, f32[3,3,512]{2,1,0:T(4,128)} %taps_ref.3, f32[1,512]{1,0:T(1,128)} %bitcast.2, f32[2,512,512]{2,1,0:T(8,128)} %spec_ref.1), custom_call_target="tpu_custom_call" | custom-call | bytes 4194304 | tf_op jit(solution)/shard_map/pallas_call | solution.py:480
  2.6 0.0 copy-start.3
  2.6 0.0 copy-start.4
  2.7 0.0 copy-start.5
  2.7 0.0 copy-start.7
  2.7 0.0 copy-start.9
  2.7 47.4 %all_to_all.10.in_ref = f32[32,104,128]{2,1,0:T(8,128)S(1)} all-to-all(f32[32,104,128]{2,1,0:T(8,128)S(1)} %shard_map.109), channel_id=1, replica_groups=mesh['dp'=2,'ctx'=16] {'ctx','dp'}, dimensions={0} | all-to-all | bytes 3407872 | tf_op jit(solution)/shard_map/all_to_all | solution.py:500
  50.1 0.0 copy-done.3
  50.1 0.0 copy-done.4
  50.1 0.0 copy-done.5
  50.1 0.0 copy-done.7
  50.1 0.0 copy-done.9
  50.1 0.0 copy-start
  50.1 0.0 copy-start.1
  50.1 0.0 copy-start.2
  50.1 0.0 copy-start.6
  50.2 0.0 copy-start.8
  50.2 4.2 %shard_map.110 = f32[32,16,256]{2,1,0:T(8,128)} custom-call(f32[32,104,128]{2,1,0:T(8,128)S(1)} %all_to_all.10.in_ref, f32[4,17,256]{2,1,0:T(8,128)S(1)} %copy-done.5, f32[2,128]{1,0:T(2,128)S(1)} %copy-done.9, bf16[768,256]{1,0:T(8,128)(2,1)S(1)} %copy-done.3, bf16[768,256]{1,0:T(8,128)(2,1)S(1)} %copy-done.4, bf16[256,128]{1,0:T(8,128)(2,1)S(1)} %copy-done.7), custom_call_target="tpu_custom_call" | custom-call | bytes 4194304 | tf_op jit(solution)/shard_map/pallas_call | solution.py:512
  54.4 3.7 %all-to-all-start.1 = ((f32[32,16,256]{2,1,0:T(8,128)}), f32[32,16,256]{2,1,0:T(8,128)S(1)}, u32[]{:S(2)}, u32[]{:S(2)}) async-start(f32[32,16,256]{2,1,0:T(8,128)} %shard_map.110), calls=%async_computation.1 | async-start | bytes 1048576 | tf_op jit(solution)/shard_map/all_to_all | solution.py:528
  58.1 0.0 copy-done
  58.1 0.0 copy-done.1
  58.1 0.0 copy-done.2
  58.1 0.0 copy-done.6
  58.1 0.0 copy-done.8
  58.1 0.5 shard_map.111
  58.6 14.4 %all-to-all-done.1.conv_ref = f32[32,16,256]{2,1,0:T(8,128)S(1)} async-done(((f32[32,16,256]{2,1,0:T(8,128)}), f32[32,16,256]{2,1,0:T(8,128)S(1)}, u32[]{:S(2)}, u32[]{:S(2)}) %all-to-all-start.1) | async-done | bytes 524320 | tf_op jit(solution)/shard_map/all_to_all | solution.py:528
  73.1 0.9 %shard_map.112 = f32[256,512]{1,0:T(8,128)} custom-call(f32[32,16,256]{2,1,0:T(8,128)S(1)} %all-to-all-done.1.conv_ref, f32[256,512]{1,0:T(8,128)S(1)} %get-tuple-element.7.query_ref, f32[256,512]{1,0:T(8,128)S(1)} %get-tuple-element.8.direct_ref), custom_call_target="tpu_custom_call" | custom-call | bytes 2097152 | tf_op jit(solution)/shard_map/pallas_call | solution.py:529
Async XLA Ops:
  2.6 47.5 %copy-start.3 = (bf16[768,256]{1,0:T(8,128)(2,1)S(1)}, bf16[768,256]{1,0:T(8,128)(2,1)}, u32[]{:S(2)}) copy-start(bf16[768,256]{1,0:T(8,128)(2,1)} %constant.18.clone.fore_ref) | copy-start | bytes 1179652
  2.6 47.4 %copy-start.4 = (bf16[768,256]{1,0:T(8,128)(2,1)S(1)}, bf16[768,256]{1,0:T(8,128)(2,1)}, u32[]{:S(2)}) copy-start(bf16[768,256]{1,0:T(8,128)(2,1)} %constant.19.clone.back_ref) | copy-start | bytes 1179652
  2.7 47.4 %copy-start.5 = (f32[4,17,256]{2,1,0:T(8,128)S(1)}, f32[4,17,256]{2,1,0:T(8,128)}, u32[]{:S(2)}) copy-start(f32[4,17,256]{2,1,0:T(8,128)} %constant.16.clone.turn_ref) | copy-start | bytes 208900
  2.7 47.4 %copy-start.7 = (bf16[256,128]{1,0:T(8,128)(2,1)S(1)}, bf16[256,128]{1,0:T(8,128)(2,1)}, u32[]{:S(2)}) copy-start(bf16[256,128]{1,0:T(8,128)(2,1)} %constant.20.clone.flip_ref) | copy-start | bytes 196612
  2.7 47.4 %copy-start.9 = (f32[2,128]{1,0:T(2,128)S(1)}, f32[2,128]{1,0:T(2,128)}, u32[]{:S(2)}) copy-start(f32[2,128]{1,0:T(2,128)} %constant.17.clone.parity_ref) | copy-start | bytes 3076
  50.1 8.0 %copy-start = (f32[256,512]{1,0:T(8,128)S(1)}, f32[256,512]{1,0:T(8,128)}, u32[]{:S(2)}) copy-start(f32[256,512]{1,0:T(8,128)} %q_ref.3) | copy-start | bytes 1572868
  50.1 8.0 %copy-start.1 = (f32[256,512]{1,0:T(8,128)S(1)}, f32[256,512]{1,0:T(8,128)}, u32[]{:S(2)}) copy-start(f32[256,512]{1,0:T(8,128)} %k_ref.3) | copy-start | bytes 1572868
  50.1 8.0 %copy-start.2 = (f32[256,512]{1,0:T(8,128)S(1)}, f32[256,512]{1,0:T(8,128)}, u32[]{:S(2)}) copy-start(f32[256,512]{1,0:T(8,128)} %v_ref.3) | copy-start | bytes 1572868
  50.1 8.0 %copy-start.6 = (f32[3,3,512]{2,1,0:T(4,128)S(1)}, f32[3,3,512]{2,1,0:T(4,128)}, u32[]{:S(2)}) copy-start(f32[3,3,512]{2,1,0:T(4,128)} %taps_ref.3) | copy-start | bytes 55300
  50.2 8.0 %copy-start.8 = (f32[512]{0:T(512)S(1)}, f32[512]{0:T(512)}, u32[]{:S(2)}) copy-start(f32[512]{0:T(512)} %param.15) | copy-start | bytes 6148
  54.4 18.7 %all-to-all-start.1 = ((f32[32,16,256]{2,1,0:T(8,128)}), f32[32,16,256]{2,1,0:T(8,128)S(1)}, u32[]{:S(2)}, u32[]{:S(2)}) async-start(f32[32,16,256]{2,1,0:T(8,128)} %shard_map.110), calls=%async_computation.1 | async-start | bytes 1048576 | tf_op jit(solution)/shard_map/all_to_all | solution.py:528

commit v9 on v8

--- a/solution.py
+++ b/solution.py
@@ -234,6 +234,12 @@
     return out
 
 
+def place(out_ref, near, i, at, value):
+    few = value.shape[0] // near
+    rows = slice(at // 2, (at + few) // 2)
+    out_ref[near * i : near * i + near, rows] = value.reshape(near, few // 2, 2, LANES)
+
+
 def pack_kernel(
     few, chunks, part_ref, q_ref, k_ref, v_ref, taps_ref, gain_ref, spec_ref,
     out_ref, ends, keys, values, taps, gain, held, sems, held_sems, key_sems,
@@ -268,7 +274,7 @@
         large[m].wait()
         for i in range(blocks):
             both = held[m, :, :, columns(i)].reshape(LANES, LANES)
-            out_ref[near * i : near * i + near, few * m : few * m + few, :] = both.T.reshape(near, few, LANES)
+            place(out_ref, near, i, few * m, both.T)
 
     turn_chunk(0)
     for copy in small:
@@ -285,7 +291,7 @@
         for h in range(rows // LANES):
             turned = mixed_in[LANES * h : LANES * h + LANES].T
             at = base + few * h
-            out_ref[dests, at : at + few, :] = turned.reshape(near, few, LANES)
+            place(out_ref, near, i, at, turned)
 
         def known(first, last, j):
             t0, t1, t2 = taps[j, 0:1, col], taps[j, 1:2, col], taps[j, 2:3, col]
@@ -300,10 +306,8 @@
         at = base + few * (rows // LANES)
         pairs = jnp.concatenate([k0, v0, k1, v1, next_k0, next_v0, next_k1, next_v1], axis=0)
         others = [q0, q1, next_q0, next_q1, gain[:, col], nothing, nothing, nothing]
-        out_ref[dests, at, :] = block_turn(pairs, few)
-        out_ref[dests, at + 1, :] = block_turn(jnp.concatenate(others, axis=0), few)
-        for j in range(2, 8):
-            out_ref[dests, at + j, :] = jnp.zeros((near, LANES), F32)
+        out_ref[dests, at // 2, 0, :] = block_turn(pairs, few)
+        out_ref[dests, at // 2, 1, :] = block_turn(jnp.concatenate(others, axis=0), few)
 
 
 def local_kernel(q_ref, k_ref, v_ref, taps_ref, gain_ref, query_ref, direct_ref):
@@ -346,7 +350,7 @@
 
     everyone = in_ref.shape[0]
     begins = lax.broadcasted_iota(jnp.int32, (everyone, LANES), 0) < parts
-    pairs, others = in_ref[:, base + 2 * few, :], in_ref[:, base + 2 * few + 1, :]
+    pairs, others = in_ref[:, base // 2 + few, 0, :], in_ref[:, base // 2 + few, 1, :]
 
     def before(x, lanes):
         moved = pltpu.roll(pltpu.roll(x, parts, 0), LANES - lanes, 1)
@@ -385,7 +389,10 @@
         tiles = []
         for h in range(2):
             at = base + few * h
-            x = [in_ref[p * parts + q, at : at + few, :] for p in range(devices)]
+            x = [
+                in_ref[p * parts + q, at // 2 : (at + few) // 2].reshape(few, LANES)
+                for p in range(devices)
+            ]
             if h == 0:
                 x = [
                     jnp.where(lane_of < 2, first_lanes(0, p * parts + q), own)
@@ -410,7 +417,7 @@
         span = slice(j * size, (j + 1) * size)
         freq[span] = dot(triple[span], fore_ref[...])
         for c in range(j * few // pieces, (j + 1) * few // pieces):
-            own = jnp.concatenate([in_ref[:, few * m + c, :] for m in range(chunks)], axis=0)
+            own = jnp.concatenate([in_ref[:, (few * m + c) // 2, c % 2, :] for m in range(chunks)], axis=0)
             spec[pl.ds(c, 4 * outer, stride=pitch), :] = own.T
 
     other = [[None, None], [None, None]]
@@ -468,7 +475,7 @@
     few = channels // everyone
     chunks = 2 * rows // parts // 64
     halves = rows // LANES
-    depth = few * (chunks + halves) + 8
+    depth = few * (chunks + halves) + 2
     outer = 2 * devices
     whole = pl.BlockSpec(memory_space=pltpu.VMEM)
     in_hbm = pl.BlockSpec(memory_space=pltpu.HBM)
@@ -479,7 +486,7 @@
     sources = (q_proj, k_proj, v_proj, short_filter, gain_row, filter_spec)
     sent = pl.pallas_call(
         functools.partial(pack_kernel, few, chunks),
-        out_shape=jax.ShapeDtypeStruct((everyone, depth, LANES), F32),
+        out_shape=jax.ShapeDtypeStruct((everyone, depth // 2, 2, LANES), F32),
         in_specs=[pl.BlockSpec(memory_space=pltpu.SMEM)] + [in_hbm] * 6,
         out_specs=whole,
         compiler_params=small,

time: 74.9 us -> 73.8 us (0.985)
  blocking collectives: 47.4 us -> 45.3 us
  Pallas kernels: 8.31 us -> 9.32 us
    all_to_all x1, blocking collectives: 47.4 us -> 45.3 us  [per_device_tiled(): come = lax.all_to_all(sent, ('ctx', 'dp'), 0, 0, tiled=True)]
    pallas_call x1, Pallas kernels: 4.23 us -> 5.26 us  [per_device_tiled(): pl.pallas_call(functools.partial(conv_kernel, parts, few, chunks), out_sh...]
where the time goes in v9:
time: 73.8 us; the launch traced here: 72.9 us
  blocking collectives  45.3 us (61%)
  waiting for transfers between devices  14.4 us (20%)
  Pallas kernels  9.32 us (13%)
  starting transfers between devices  3.67 us (5%)
    all_to_all x1, blocking collectives, per_device_tiled(): come = lax.all_to_all(sent, ('ctx', 'dp'), 0, 0, tiled=True)  45.3 us
    all_to_all x1, waiting for transfers between devices, per_device_tiled(): back = lax.all_to_all(conv, ('ctx', 'dp'), 0, 0, tiled=True)  14.4 us
    pallas_call x1, Pallas kernels, per_device_tiled(): pl.pallas_call(functools.partial(conv_kernel, parts, few, chunks), out_sh...  5.26 us
    all_to_all x1, starting transfers between devices, per_device_tiled(): back = lax.all_to_all(conv, ('ctx', 'dp'), 0, 0, tiled=True)  3.67 us
    pallas_call x1, Pallas kernels, per_device_tiled(): pl.pallas_call(functools.partial(pack_kernel, few, chunks), out_shape=jax...  2.61 us
  transfers between devices with their start and end apart: 1, of which 1 were waited for; matrix products, arithmetic and copies ran while one was open for 0% of the time, Pallas kernels for 1%

profile of v9, /device:TPU:0, one launch (start us, length us, event | category | flops | bytes accessed | tf_op | source)
XLA Modules:
  0.0 72.9 jit_solution(6199856524248947168)
XLA Ops:
  0.0 2.6 %shard_map.109 = f32[32,49,2,128]{3,2,1,0:T(2,128)S(1)} custom-call(s32[1]{0:T(128)} %bitcast.part_ref, f32[256,512]{1,0:T(8,128)} %q_ref.3, f32[256,512]{1,0:T(8,128)} %k_ref.3, f32[256,512]{1,0:T(8,128)} %v_ref.3, f32[3,3,512]{2,1,0:T(4,128)} %taps_ref.3, f32[1,512]{1,0:T(1,128)} %bitcast.2, f32[2,512,512]{2,1,0:T(8,128)} %spec_ref.1), custom_call_target="tpu_custom_call" | custom-call | bytes 4194304 | tf_op jit(solution)/shard_map/pallas_call | solution.py:487
  2.6 0.0 copy-start.3
  2.6 0.0 copy-start.4
  2.6 0.0 copy-start.5
  2.7 0.0 copy-start.7
  2.7 0.0 copy-start.9
  2.7 45.3 %all_to_all.10.in_ref = f32[32,49,2,128]{3,2,1,0:T(2,128)S(1)} all-to-all(f32[32,49,2,128]{3,2,1,0:T(2,128)S(1)} %shard_map.109), channel_id=1, replica_groups=mesh['dp'=2,'ctx'=16] {'ctx','dp'}, dimensions={0} | all-to-all | bytes 3211264 | tf_op jit(solution)/shard_map/all_to_all | solution.py:507
  48.0 0.0 copy-done.3
  48.0 0.0 copy-done.4
  48.0 0.0 copy-done.5
  48.0 0.0 copy-done.7
  48.0 0.0 copy-done.9
  48.0 0.0 copy-start
  48.0 0.0 copy-start.1
  48.0 0.0 copy-start.2
  48.0 0.0 copy-start.6
  48.0 0.0 copy-start.8
  48.0 5.3 %shard_map.110 = f32[32,16,256]{2,1,0:T(8,128)} custom-call(f32[32,49,2,128]{3,2,1,0:T(2,128)S(1)} %all_to_all.10.in_ref, f32[4,17,256]{2,1,0:T(8,128)S(1)} %copy-done.5, f32[2,128]{1,0:T(2,128)S(1)} %copy-done.9, bf16[768,256]{1,0:T(8,128)(2,1)S(1)} %copy-done.3, bf16[768,256]{1,0:T(8,128)(2,1)S(1)} %copy-done.4, bf16[256,128]{1,0:T(8,128)(2,1)S(1)} %copy-done.7), custom_call_target="tpu_custom_call" | custom-call | bytes 4194304 | tf_op jit(solution)/shard_map/pallas_call | solution.py:519
  53.3 3.7 %all-to-all-start.1 = ((f32[32,16,256]{2,1,0:T(8,128)}), f32[32,16,256]{2,1,0:T(8,128)S(1)}, u32[]{:S(2)}, u32[]{:S(2)}) async-start(f32[32,16,256]{2,1,0:T(8,128)} %shard_map.110), calls=%async_computation.1 | async-start | bytes 1048576 | tf_op jit(solution)/shard_map/all_to_all | solution.py:535
  57.0 0.0 copy-done
  57.0 0.0 copy-done.1
  57.0 0.0 copy-done.2
  57.0 0.0 copy-done.6
  57.0 0.0 copy-done.8
  57.0 0.5 shard_map.111
  57.6 14.4 %all-to-all-done.1.conv_ref = f32[32,16,256]{2,1,0:T(8,128)S(1)} async-done(((f32[32,16,256]{2,1,0:T(8,128)}), f32[32,16,256]{2,1,0:T(8,128)S(1)}, u32[]{:S(2)}, u32[]{:S(2)}) %all-to-all-start.1) | async-done | bytes 524320 | tf_op jit(solution)/shard_map/all_to_all | solution.py:535
  72.0 0.9 %shard_map.112 = f32[256,512]{1,0:T(8,128)} custom-call(f32[32,16,256]{2,1,0:T(8,128)S(1)} %all-to-all-done.1.conv_ref, f32[256,512]{1,0:T(8,128)S(1)} %get-tuple-element.7.query_ref, f32[256,512]{1,0:T(8,128)S(1)} %get-tuple-element.8.direct_ref), custom_call_target="tpu_custom_call" | custom-call | bytes 2097152 | tf_op jit(solution)/shard_map/pallas_call | solution.py:536
Async XLA Ops:
  2.6 45.3 %copy-start.3 = (bf16[768,256]{1,0:T(8,128)(2,1)S(1)}, bf16[768,256]{1,0:T(8,128)(2,1)}, u32[]{:S(2)}) copy-start(bf16[768,256]{1,0:T(8,128)(2,1)} %constant.18.clone.fore_ref) | copy-start | bytes 1179652
  2.6 45.3 %copy-start.4 = (bf16[768,256]{1,0:T(8,128)(2,1)S(1)}, bf16[768,256]{1,0:T(8,128)(2,1)}, u32[]{:S(2)}) copy-start(bf16[768,256]{1,0:T(8,128)(2,1)} %constant.19.clone.back_ref) | copy-start | bytes 1179652
  2.6 45.3 %copy-start.5 = (f32[4,17,256]{2,1,0:T(8,128)S(1)}, f32[4,17,256]{2,1,0:T(8,128)}, u32[]{:S(2)}) copy-start(f32[4,17,256]{2,1,0:T(8,128)} %constant.16.clone.turn_ref) | copy-start | bytes 208900
  2.7 45.3 %copy-start.7 = (bf16[256,128]{1,0:T(8,128)(2,1)S(1)}, bf16[256,128]{1,0:T(8,128)(2,1)}, u32[]{:S(2)}) copy-start(bf16[256,128]{1,0:T(8,128)(2,1)} %constant.20.clone.flip_ref) | copy-start | bytes 196612
  2.7 45.3 %copy-start.9 = (f32[2,128]{1,0:T(2,128)S(1)}, f32[2,128]{1,0:T(2,128)}, u32[]{:S(2)}) copy-start(f32[2,128]{1,0:T(2,128)} %constant.17.clone.parity_ref) | copy-start | bytes 3076
  48.0 9.0 %copy-start = (f32[256,512]{1,0:T(8,128)S(1)}, f32[256,512]{1,0:T(8,128)}, u32[]{:S(2)}) copy-start(f32[256,512]{1,0:T(8,128)} %q_ref.3) | copy-start | bytes 1572868
  48.0 9.0 %copy-start.1 = (f32[256,512]{1,0:T(8,128)S(1)}, f32[256,512]{1,0:T(8,128)}, u32[]{:S(2)}) copy-start(f32[256,512]{1,0:T(8,128)} %k_ref.3) | copy-start | bytes 1572868
  48.0 9.0 %copy-start.2 = (f32[256,512]{1,0:T(8,128)S(1)}, f32[256,512]{1,0:T(8,128)}, u32[]{:S(2)}) copy-start(f32[256,512]{1,0:T(8,128)} %v_ref.3) | copy-start | bytes 1572868
  48.0 9.0 %copy-start.6 = (f32[3,3,512]{2,1,0:T(4,128)S(1)}, f32[3,3,512]{2,1,0:T(4,128)}, u32[]{:S(2)}) copy-start(f32[3,3,512]{2,1,0:T(4,128)} %taps_ref.3) | copy-start | bytes 55300
  48.0 9.0 %copy-start.8 = (f32[512]{0:T(512)S(1)}, f32[512]{0:T(512)}, u32[]{:S(2)}) copy-start(f32[512]{0:T(512)} %param.15) | copy-start | bytes 6148
  53.3 18.7 %all-to-all-start.1 = ((f32[32,16,256]{2,1,0:T(8,128)}), f32[32,16,256]{2,1,0:T(8,128)S(1)}, u32[]{:S(2)}, u32[]{:S(2)}) async-start(f32[32,16,256]{2,1,0:T(8,128)} %shard_map.110), calls=%async_computation.1 | async-start | bytes 1048576 | tf_op jit(solution)/shard_map/all_to_all | solution.py:535

commit v10 on v9

--- a/solution.py
+++ b/solution.py
@@ -339,7 +339,7 @@
 
 
 def conv_kernel(
-    parts, few, chunks, in_ref, turn_ref, parity_ref, fore_ref, back_ref, flip_ref, out_ref, spec, triple, freq, undo, ends
+    parts, few, chunks, in_ref, turn_ref, parity_ref, fore_ref, back_ref, flip_ref, out_ref, spec, triple, freq, undo, ends, blocks
 ):
     devices = in_ref.shape[0] // parts
     outer = 2 * devices
@@ -385,14 +385,16 @@
                 at = 2 * LANES * j + col
                 triple[span, at : at + LANES] = part
 
+    for j in range(2 * few):
+        h, c = divmod(j, few)
+        span = pl.ds(h * everyone * pitch + c, everyone, stride=pitch)
+        blocks[span, :] = in_ref[:, (base + j) // 2, j % 2, :]
+
     for q in range(parts):
         tiles = []
         for h in range(2):
-            at = base + few * h
-            x = [
-                in_ref[p * parts + q, at // 2 : (at + few) // 2].reshape(few, LANES)
-                for p in range(devices)
-            ]
+            first = [(h * everyone + p * parts + q) * pitch for p in range(devices)]
+            x = [blocks[at : at + few] for at in first]
             if h == 0:
                 x = [
                     jnp.where(lane_of < 2, first_lanes(0, p * parts + q), own)
@@ -527,6 +529,7 @@
             pltpu.VMEM((total, 2 * LANES), F32),
             pltpu.VMEM((total, 2 * LANES), F32),
             pltpu.VMEM((6 * everyone, LANES), F32),
+            pltpu.VMEM((2 * everyone * (few + 1), LANES), F32),
         ],
         compiler_params=small,
         cost_estimate=pl.CostEstimate(flops=0, bytes_accessed=4 << 20, transcendentals=0),

time: 73.8 us -> 73.1 us (level)
  Pallas kernels: 9.32 us -> 8.57 us
    pallas_call x1, Pallas kernels: 5.26 us -> 4.5 us  [per_device_tiled(): pl.pallas_call(functools.partial(conv_kernel, parts, few, chunks), out_sh...]
where the time goes in v10:
time: 73.1 us; the launch traced here: 72.2 us
  blocking collectives  45.3 us (62%)
  waiting for transfers between devices  14.4 us (20%)
  Pallas kernels  8.57 us (12%)
  starting transfers between devices  3.67 us (5%)
    all_to_all x1, blocking collectives, per_device_tiled(): come = lax.all_to_all(sent, ('ctx', 'dp'), 0, 0, tiled=True)  45.3 us
    all_to_all x1, waiting for transfers between devices, per_device_tiled(): back = lax.all_to_all(conv, ('ctx', 'dp'), 0, 0, tiled=True)  14.4 us
    pallas_call x1, Pallas kernels, per_device_tiled(): pl.pallas_call(functools.partial(conv_kernel, parts, few, chunks), out_sh...  4.5 us
    all_to_all x1, starting transfers between devices, per_device_tiled(): back = lax.all_to_all(conv, ('ctx', 'dp'), 0, 0, tiled=True)  3.67 us
    pallas_call x1, Pallas kernels, per_device_tiled(): pl.pallas_call(functools.partial(pack_kernel, few, chunks), out_shape=jax...  2.61 us
  transfers between devices with their start and end apart: 1, of which 1 were waited for; matrix products, arithmetic and copies ran while one was open for 0% of the time, Pallas kernels for 1%

profile of v10, /device:TPU:0, one launch (start us, length us, event | category | flops | bytes accessed | tf_op | source)
XLA Modules:
  0.0 72.2 jit_solution(12028630848103164535)
XLA Ops:
  0.0 2.6 %shard_map.109 = f32[32,49,2,128]{3,2,1,0:T(2,128)S(1)} custom-call(s32[1]{0:T(128)} %bitcast.part_ref, f32[256,512]{1,0:T(8,128)} %q_ref.3, f32[256,512]{1,0:T(8,128)} %k_ref.3, f32[256,512]{1,0:T(8,128)} %v_ref.3, f32[3,3,512]{2,1,0:T(4,128)} %taps_ref.3, f32[1,512]{1,0:T(1,128)} %bitcast.2, f32[2,512,512]{2,1,0:T(8,128)} %spec_ref.1), custom_call_target="tpu_custom_call" | custom-call | bytes 4194304 | tf_op jit(solution)/shard_map/pallas_call | solution.py:489
  2.6 0.0 copy-start.3
  2.6 0.0 copy-start.4
  2.6 0.0 copy-start.5
  2.7 0.0 copy-start.7
  2.7 0.0 copy-start.9
  2.7 45.3 %all_to_all.10.in_ref = f32[32,49,2,128]{3,2,1,0:T(2,128)S(1)} all-to-all(f32[32,49,2,128]{3,2,1,0:T(2,128)S(1)} %shard_map.109), channel_id=1, replica_groups=mesh['dp'=2,'ctx'=16] {'ctx','dp'}, dimensions={0} | all-to-all | bytes 3211264 | tf_op jit(solution)/shard_map/all_to_all | solution.py:509
  48.0 0.0 copy-done.3
  48.0 0.0 copy-done.4
  48.0 0.0 copy-done.5
  48.0 0.0 copy-done.7
  48.0 0.0 copy-done.9
  48.0 0.0 copy-start
  48.0 0.0 copy-start.1
  48.0 0.0 copy-start.2
  48.0 0.0 copy-start.6
  48.0 0.0 copy-start.8
  48.0 4.5 %shard_map.110 = f32[32,16,256]{2,1,0:T(8,128)} custom-call(f32[32,49,2,128]{3,2,1,0:T(2,128)S(1)} %all_to_all.10.in_ref, f32[4,17,256]{2,1,0:T(8,128)S(1)} %copy-done.5, f32[2,128]{1,0:T(2,128)S(1)} %copy-done.9, bf16[768,256]{1,0:T(8,128)(2,1)S(1)} %copy-done.3, bf16[768,256]{1,0:T(8,128)(2,1)S(1)} %copy-done.4, bf16[256,128]{1,0:T(8,128)(2,1)S(1)} %copy-done.7), custom_call_target="tpu_custom_call" | custom-call | bytes 4194304 | tf_op jit(solution)/shard_map/pallas_call | solution.py:521
  52.6 3.7 %all-to-all-start.1 = ((f32[32,16,256]{2,1,0:T(8,128)}), f32[32,16,256]{2,1,0:T(8,128)S(1)}, u32[]{:S(2)}, u32[]{:S(2)}) async-start(f32[32,16,256]{2,1,0:T(8,128)} %shard_map.110), calls=%async_computation.1 | async-start | bytes 1048576 | tf_op jit(solution)/shard_map/all_to_all | solution.py:538
  56.2 0.0 copy-done
  56.2 0.0 copy-done.1
  56.2 0.0 copy-done.2
  56.3 0.0 copy-done.6
  56.3 0.0 copy-done.8
  56.3 0.5 shard_map.111
  56.8 14.4 %all-to-all-done.1.conv_ref = f32[32,16,256]{2,1,0:T(8,128)S(1)} async-done(((f32[32,16,256]{2,1,0:T(8,128)}), f32[32,16,256]{2,1,0:T(8,128)S(1)}, u32[]{:S(2)}, u32[]{:S(2)}) %all-to-all-start.1) | async-done | bytes 524320 | tf_op jit(solution)/shard_map/all_to_all | solution.py:538
  71.2 0.9 %shard_map.112 = f32[256,512]{1,0:T(8,128)} custom-call(f32[32,16,256]{2,1,0:T(8,128)S(1)} %all-to-all-done.1.conv_ref, f32[256,512]{1,0:T(8,128)S(1)} %get-tuple-element.7.query_ref, f32[256,512]{1,0:T(8,128)S(1)} %get-tuple-element.8.direct_ref), custom_call_target="tpu_custom_call" | custom-call | bytes 2097152 | tf_op jit(solution)/shard_map/pallas_call | solution.py:539
Async XLA Ops:
  2.6 45.3 %copy-start.3 = (bf16[768,256]{1,0:T(8,128)(2,1)S(1)}, bf16[768,256]{1,0:T(8,128)(2,1)}, u32[]{:S(2)}) copy-start(bf16[768,256]{1,0:T(8,128)(2,1)} %constant.18.clone.fore_ref) | copy-start | bytes 1179652
  2.6 45.3 %copy-start.4 = (bf16[768,256]{1,0:T(8,128)(2,1)S(1)}, bf16[768,256]{1,0:T(8,128)(2,1)}, u32[]{:S(2)}) copy-start(bf16[768,256]{1,0:T(8,128)(2,1)} %constant.19.clone.back_ref) | copy-start | bytes 1179652
  2.6 45.3 %copy-start.5 = (f32[4,17,256]{2,1,0:T(8,128)S(1)}, f32[4,17,256]{2,1,0:T(8,128)}, u32[]{:S(2)}) copy-start(f32[4,17,256]{2,1,0:T(8,128)} %constant.16.clone.turn_ref) | copy-start | bytes 208900
  2.7 45.3 %copy-start.7 = (bf16[256,128]{1,0:T(8,128)(2,1)S(1)}, bf16[256,128]{1,0:T(8,128)(2,1)}, u32[]{:S(2)}) copy-start(bf16[256,128]{1,0:T(8,128)(2,1)} %constant.20.clone.flip_ref) | copy-start | bytes 196612
  2.7 45.3 %copy-start.9 = (f32[2,128]{1,0:T(2,128)S(1)}, f32[2,128]{1,0:T(2,128)}, u32[]{:S(2)}) copy-start(f32[2,128]{1,0:T(2,128)} %constant.17.clone.parity_ref) | copy-start | bytes 3076
  48.0 8.2 %copy-start = (f32[256,512]{1,0:T(8,128)S(1)}, f32[256,512]{1,0:T(8,128)}, u32[]{:S(2)}) copy-start(f32[256,512]{1,0:T(8,128)} %q_ref.3) | copy-start | bytes 1572868
  48.0 8.2 %copy-start.1 = (f32[256,512]{1,0:T(8,128)S(1)}, f32[256,512]{1,0:T(8,128)}, u32[]{:S(2)}) copy-start(f32[256,512]{1,0:T(8,128)} %k_ref.3) | copy-start | bytes 1572868
  48.0 8.2 %copy-start.2 = (f32[256,512]{1,0:T(8,128)S(1)}, f32[256,512]{1,0:T(8,128)}, u32[]{:S(2)}) copy-start(f32[256,512]{1,0:T(8,128)} %v_ref.3) | copy-start | bytes 1572868
  48.0 8.2 %copy-start.6 = (f32[3,3,512]{2,1,0:T(4,128)S(1)}, f32[3,3,512]{2,1,0:T(4,128)}, u32[]{:S(2)}) copy-start(f32[3,3,512]{2,1,0:T(4,128)} %taps_ref.3) | copy-start | bytes 55300
  48.0 8.2 %copy-start.8 = (f32[512]{0:T(512)S(1)}, f32[512]{0:T(512)}, u32[]{:S(2)}) copy-start(f32[512]{0:T(512)} %param.15) | copy-start | bytes 6148
  52.6 18.7 %all-to-all-start.1 = ((f32[32,16,256]{2,1,0:T(8,128)}), f32[32,16,256]{2,1,0:T(8,128)S(1)}, u32[]{:S(2)}, u32[]{:S(2)}) async-start(f32[32,16,256]{2,1,0:T(8,128)} %shard_map.110), calls=%async_computation.1 | async-start | bytes 1048576 | tf_op jit(solution)/shard_map/all_to_all | solution.py:538

commit v11 on v10

--- a/solution.py
+++ b/solution.py
@@ -261,30 +261,24 @@
     small = [pltpu.make_async_copy(*pair, sems.at[i]) for i, pair in enumerate(small)]
     large = [pltpu.make_async_copy(chunk_rows(m), held.at[m], held_sems.at[m]) for m in range(chunks)]
     inputs = [
-        [
-            pltpu.make_async_copy(src.at[:, columns(i)], dst.at[:, columns(i)], key_sems.at[j, i])
-            for j, (src, dst) in enumerate(((k_ref, keys), (v_ref, values)))
-        ]
-        for i in range(blocks)
+        pltpu.make_async_copy(src, dst, key_sems.at[j])
+        for j, (src, dst) in enumerate(((k_ref, keys), (v_ref, values)))
     ]
-    for copy in (large[0], *small, *inputs[0], *large[1:], *sum(inputs[1:], [])):
+    for copy in (*large, *small, *inputs):
         copy.start()
 
     def turn_chunk(m):
-        large[m].wait()
         for i in range(blocks):
             both = held[m, :, :, columns(i)].reshape(LANES, LANES)
             place(out_ref, near, i, few * m, both.T)
 
-    turn_chunk(0)
-    for copy in small:
+    for copy in large:
+        copy.wait()
+    for m in range(chunks):
+        turn_chunk(m)
+    for copy in (*small, *inputs):
         copy.wait()
     for i in range(blocks):
-        if i == 1:
-            for m in range(1, chunks):
-                turn_chunk(m)
-        for copy in inputs[i]:
-            copy.wait()
         col = columns(i)
         dests = slice(near * i, near * i + near)
         mixed_in = causal(keys[:, col], taps[1, :, col]) * causal(values[:, col], taps[2, :, col])
@@ -339,7 +333,7 @@
 
 
 def conv_kernel(
-    parts, few, chunks, in_ref, turn_ref, parity_ref, fore_ref, back_ref, flip_ref, out_ref, spec, triple, freq, undo, ends, blocks
+    parts, few, chunks, in_ref, turn_ref, parity_ref, fore_ref, back_ref, flip_ref, out_ref, spec, triple, freq, undo, ends, blocks, leaving, sems
 ):
     devices = in_ref.shape[0] // parts
     outer = 2 * devices
@@ -450,6 +444,7 @@
         span = slice(row_of(low_bit, begin, 0).start, row_of(low_bit, end, 0).start)
         undo[span] = dot(triple[span], back_ref[...])
 
+    copies = []
     for q in range(parts):
         tiles = [], []
         for s in range(kept):
@@ -467,7 +462,11 @@
                 if lane == left:
                     finished = first_lanes(1, at) * y + first_lanes(2, at)
                     y = jnp.where(lane_of < 2, finished, y)
-                out_ref[at, :, lane] = y
+                leaving[p, q, :, lane] = y
+        copies.append(pltpu.make_async_copy(leaving.at[:, q], out_ref.at[:, q], sems.at[q]))
+        copies[q].start()
+    for copy in copies:
+        copy.wait()
 
 
 def per_device_tiled(q_proj, k_proj, v_proj, short_filter, skip_gain, filter_spec):
@@ -501,7 +500,7 @@
             pltpu.VMEM((chunks, 2, 64, channels), F32),
             pltpu.SemaphoreType.DMA((4,)),
             pltpu.SemaphoreType.DMA((chunks,)),
-            pltpu.SemaphoreType.DMA((2, channels // LANES)),
+            pltpu.SemaphoreType.DMA((2,)),
         ],
         cost_estimate=pl.CostEstimate(flops=0, bytes_accessed=1 << 22, transcendentals=0),
     )(part, *(pltpu.with_memory_space_constraint(x, pltpu.HBM) for x in sources))
@@ -520,9 +519,9 @@
     total = 2 * few * parts * (devices + 1)
     conv = pl.pallas_call(
         functools.partial(conv_kernel, parts, few, chunks),
-        out_shape=jax.ShapeDtypeStruct((everyone, few, rows), F32),
+        out_shape=jax.ShapeDtypeStruct((devices, parts, few, rows), F32),
         in_specs=[whole] * 6,
-        out_specs=whole,
+        out_specs=in_hbm,
         scratch_shapes=[
             pltpu.VMEM((4 * outer * (few + 1), LANES), F32),
             pltpu.VMEM((total, 6 * LANES), BF16),
@@ -530,12 +529,14 @@
             pltpu.VMEM((total, 2 * LANES), F32),
             pltpu.VMEM((6 * everyone, LANES), F32),
             pltpu.VMEM((2 * everyone * (few + 1), LANES), F32),
+            pltpu.VMEM((devices, parts, few, rows), F32),
+            pltpu.SemaphoreType.DMA((parts,)),
         ],
         compiler_params=small,
         cost_estimate=pl.CostEstimate(flops=0, bytes_accessed=4 << 20, transcendentals=0),
     )(come, *(jnp.asarray(t) for t in tables(parts, devices, rows)))
 
-    back = lax.all_to_all(conv, ("ctx", "dp"), 0, 0, tiled=True)
+    back = lax.all_to_all(conv.reshape(everyone, few, rows), ("ctx", "dp"), 0, 0, tiled=True)
     return pl.pallas_call(
         gate_kernel,
         out_shape=jax.ShapeDtypeStruct((rows, channels), F32),

time: 73.1 us -> 72.8 us (level)
  no operation moved by 1% of the time
where the time goes in v11:
time: 72.8 us; the launch traced here: 71.9 us
  blocking collectives  45.3 us (62%)
  waiting for transfers between devices  14.4 us (20%)
  Pallas kernels  8.26 us (11%)
  starting transfers between devices  3.67 us (5%)
    all_to_all x1, blocking collectives, per_device_tiled(): come = lax.all_to_all(sent, ('ctx', 'dp'), 0, 0, tiled=True)  45.3 us
    all_to_all x1, waiting for transfers between devices, per_device_tiled(): lax.all_to_all(conv.reshape(everyone, few, rows), ('ctx', 'dp'), 0, 0, ti...  14.4 us
    pallas_call x1, Pallas kernels, per_device_tiled(): pl.pallas_call(functools.partial(conv_kernel, parts, few, chunks), out_sh...  4.44 us
    all_to_all x1, starting transfers between devices, per_device_tiled(): lax.all_to_all(conv.reshape(everyone, few, rows), ('ctx', 'dp'), 0, 0, ti...  3.67 us
    pallas_call x1, Pallas kernels, per_device_tiled(): pl.pallas_call(functools.partial(pack_kernel, few, chunks), out_shape=jax...  2.36 us
  transfers between devices with their start and end apart: 1, of which 1 were waited for; matrix products, arithmetic and copies ran while one was open for 0% of the time, Pallas kernels for 1%

profile of v11, /device:TPU:0, one launch (start us, length us, event | category | flops | bytes accessed | tf_op | source)
XLA Modules:
  0.0 71.9 jit_solution(10939527711485546223)
XLA Ops:
  0.0 2.4 %shard_map.109 = f32[32,49,2,128]{3,2,1,0:T(2,128)S(1)} custom-call(s32[1]{0:T(128)} %bitcast.part_ref, f32[256,512]{1,0:T(8,128)} %q_ref.3, f32[256,512]{1,0:T(8,128)} %k_ref.3, f32[256,512]{1,0:T(8,128)} %v_ref.3, f32[3,3,512]{2,1,0:T(4,128)} %taps_ref.3, f32[1,512]{1,0:T(1,128)} %bitcast.3, f32[2,512,512]{2,1,0:T(8,128)} %spec_ref.1), custom_call_target="tpu_custom_call" | custom-call | bytes 4194304 | tf_op jit(solution)/shard_map/pallas_call | solution.py:488
  2.4 0.0 copy-start.3
  2.4 0.0 copy-start.4
  2.4 0.0 copy-start.5
  2.4 0.0 copy-start.7
  2.4 0.0 copy-start.9
  2.4 45.3 %all_to_all.10.in_ref = f32[32,49,2,128]{3,2,1,0:T(2,128)S(1)} all-to-all(f32[32,49,2,128]{3,2,1,0:T(2,128)S(1)} %shard_map.109), channel_id=1, replica_groups=mesh['dp'=2,'ctx'=16] {'ctx','dp'}, dimensions={0} | all-to-all | bytes 3211264 | tf_op jit(solution)/shard_map/all_to_all | solution.py:508
  47.7 0.0 copy-done.3
  47.7 0.0 copy-done.4
  47.7 0.0 copy-done.5
  47.7 0.0 copy-done.7
  47.7 0.0 copy-done.9
  47.7 0.0 copy-start
  47.8 0.0 copy-start.1
  47.8 0.0 copy-start.2
  47.8 0.0 copy-start.6
  47.8 0.0 copy-start.8
  47.8 4.4 %shard_map.110 = f32[16,2,16,256]{3,2,1,0:T(8,128)} custom-call(f32[32,49,2,128]{3,2,1,0:T(2,128)S(1)} %all_to_all.10.in_ref, f32[4,17,256]{2,1,0:T(8,128)S(1)} %copy-done.5, f32[2,128]{1,0:T(2,128)S(1)} %copy-done.9, bf16[768,256]{1,0:T(8,128)(2,1)S(1)} %copy-done.3, bf16[768,256]{1,0:T(8,128)(2,1)S(1)} %copy-done.4, bf16[256,128]{1,0:T(8,128)(2,1)S(1)} %copy-done.7), custom_call_target="tpu_custom_call" | custom-call | bytes 4194304 | tf_op jit(solution)/shard_map/pallas_call | solution.py:520
  52.2 3.7 %all-to-all-start.1 = ((f32[32,16,256]{2,1,0:T(8,128)}), f32[32,16,256]{2,1,0:T(8,128)S(1)}, u32[]{:S(2)}, u32[]{:S(2)}) async-start(f32[32,16,256]{2,1,0:T(8,128)} %bitcast.2), calls=%async_computation.1 | async-start | bytes 1048576 | tf_op jit(solution)/shard_map/all_to_all | solution.py:539
  55.9 0.0 copy-done
  55.9 0.0 copy-done.1
  55.9 0.0 copy-done.2
  56.0 0.0 copy-done.6
  56.0 0.0 copy-done.8
  56.0 0.5 shard_map.111
  56.5 14.4 %all-to-all-done.1.conv_ref = f32[32,16,256]{2,1,0:T(8,128)S(1)} async-done(((f32[32,16,256]{2,1,0:T(8,128)}), f32[32,16,256]{2,1,0:T(8,128)S(1)}, u32[]{:S(2)}, u32[]{:S(2)}) %all-to-all-start.1) | async-done | bytes 524320 | tf_op jit(solution)/shard_map/all_to_all | solution.py:539
  70.9 0.9 %shard_map.112 = f32[256,512]{1,0:T(8,128)} custom-call(f32[32,16,256]{2,1,0:T(8,128)S(1)} %all-to-all-done.1.conv_ref, f32[256,512]{1,0:T(8,128)S(1)} %get-tuple-element.7.query_ref, f32[256,512]{1,0:T(8,128)S(1)} %get-tuple-element.8.direct_ref), custom_call_target="tpu_custom_call" | custom-call | bytes 2097152 | tf_op jit(solution)/shard_map/pallas_call | solution.py:540
Async XLA Ops:
  2.4 45.3 %copy-start.3 = (bf16[768,256]{1,0:T(8,128)(2,1)S(1)}, bf16[768,256]{1,0:T(8,128)(2,1)}, u32[]{:S(2)}) copy-start(bf16[768,256]{1,0:T(8,128)(2,1)} %constant.18.clone.fore_ref) | copy-start | bytes 1179652
  2.4 45.3 %copy-start.4 = (bf16[768,256]{1,0:T(8,128)(2,1)S(1)}, bf16[768,256]{1,0:T(8,128)(2,1)}, u32[]{:S(2)}) copy-start(bf16[768,256]{1,0:T(8,128)(2,1)} %constant.19.clone.back_ref) | copy-start | bytes 1179652
  2.4 45.3 %copy-start.5 = (f32[4,17,256]{2,1,0:T(8,128)S(1)}, f32[4,17,256]{2,1,0:T(8,128)}, u32[]{:S(2)}) copy-start(f32[4,17,256]{2,1,0:T(8,128)} %constant.16.clone.turn_ref) | copy-start | bytes 208900
  2.4 45.3 %copy-start.7 = (bf16[256,128]{1,0:T(8,128)(2,1)S(1)}, bf16[256,128]{1,0:T(8,128)(2,1)}, u32[]{:S(2)}) copy-start(bf16[256,128]{1,0:T(8,128)(2,1)} %constant.20.clone.flip_ref) | copy-start | bytes 196612
  2.4 45.3 %copy-start.9 = (f32[2,128]{1,0:T(2,128)S(1)}, f32[2,128]{1,0:T(2,128)}, u32[]{:S(2)}) copy-start(f32[2,128]{1,0:T(2,128)} %constant.17.clone.parity_ref) | copy-start | bytes 3076
  47.7 8.2 %copy-start = (f32[256,512]{1,0:T(8,128)S(1)}, f32[256,512]{1,0:T(8,128)}, u32[]{:S(2)}) copy-start(f32[256,512]{1,0:T(8,128)} %q_ref.3) | copy-start | bytes 1572868
  47.8 8.2 %copy-start.1 = (f32[256,512]{1,0:T(8,128)S(1)}, f32[256,512]{1,0:T(8,128)}, u32[]{:S(2)}) copy-start(f32[256,512]{1,0:T(8,128)} %k_ref.3) | copy-start | bytes 1572868
  47.8 8.2 %copy-start.2 = (f32[256,512]{1,0:T(8,128)S(1)}, f32[256,512]{1,0:T(8,128)}, u32[]{:S(2)}) copy-start(f32[256,512]{1,0:T(8,128)} %v_ref.3) | copy-start | bytes 1572868
  47.8 8.2 %copy-start.6 = (f32[3,3,512]{2,1,0:T(4,128)S(1)}, f32[3,3,512]{2,1,0:T(4,128)}, u32[]{:S(2)}) copy-start(f32[3,3,512]{2,1,0:T(4,128)} %taps_ref.3) | copy-start | bytes 55300
  47.8 8.2 %copy-start.8 = (f32[512]{0:T(512)S(1)}, f32[512]{0:T(512)}, u32[]{:S(2)}) copy-start(f32[512]{0:T(512)} %param.15) | copy-start | bytes 6148
  52.2 18.7 %all-to-all-start.1 = ((f32[32,16,256]{2,1,0:T(8,128)}), f32[32,16,256]{2,1,0:T(8,128)S(1)}, u32[]{:S(2)}, u32[]{:S(2)}) async-start(f32[32,16,256]{2,1,0:T(8,128)} %bitcast.2), calls=%async_computation.1 | async-start | bytes 1048576 | tf_op jit(solution)/shard_map/all_to_all | solution.py:539

commit v12 on v11

--- a/solution.py
+++ b/solution.py
@@ -253,13 +253,10 @@
     def columns(i):
         return slice(LANES * i, LANES * i + LANES)
 
-    def chunk_rows(m):
-        return spec_ref.at[:, pl.ds(start + 64 * m, 64), :]
-
     small = [(taps_ref, taps), (gain_ref, gain)]
     small += [(q_ref.at[0:8], ends.at[0:8]), (q_ref.at[rows - 8 : rows], ends.at[8:16])]
     small = [pltpu.make_async_copy(*pair, sems.at[i]) for i, pair in enumerate(small)]
-    large = [pltpu.make_async_copy(chunk_rows(m), held.at[m], held_sems.at[m]) for m in range(chunks)]
+    large = [pltpu.make_async_copy(spec_ref.at[:, pl.ds(start, 64 * chunks), :], held, held_sems.at[0])]
     inputs = [
         pltpu.make_async_copy(src, dst, key_sems.at[j])
         for j, (src, dst) in enumerate(((k_ref, keys), (v_ref, values)))
@@ -269,7 +266,7 @@
 
     def turn_chunk(m):
         for i in range(blocks):
-            both = held[m, :, :, columns(i)].reshape(LANES, LANES)
+            both = held[:, 64 * m : 64 * m + 64, columns(i)].reshape(LANES, LANES)
             place(out_ref, near, i, few * m, both.T)
 
     for copy in large:
@@ -497,9 +494,9 @@
             pltpu.VMEM((rows, channels), F32),
             pltpu.VMEM((3, 3, channels), F32),
             pltpu.VMEM((1, channels), F32),
-            pltpu.VMEM((chunks, 2, 64, channels), F32),
+            pltpu.VMEM((2, 64 * chunks, channels), F32),
             pltpu.SemaphoreType.DMA((4,)),
-            pltpu.SemaphoreType.DMA((chunks,)),
+            pltpu.SemaphoreType.DMA((1,)),
             pltpu.SemaphoreType.DMA((2,)),
         ],
         cost_estimate=pl.CostEstimate(flops=0, bytes_accessed=1 << 22, transcendentals=0),

time: 72.8 us -> 72.8 us (level)
  no operation moved by 1% of the time
where the time goes in v12:
time: 72.8 us; the launch traced here: 71.9 us
  blocking collectives  45.3 us (62%)
  waiting for transfers between devices  14.4 us (20%)
  Pallas kernels  8.27 us (11%)
  starting transfers between devices  3.67 us (5%)
    all_to_all x1, blocking collectives, per_device_tiled(): come = lax.all_to_all(sent, ('ctx', 'dp'), 0, 0, tiled=True)  45.3 us
    all_to_all x1, waiting for transfers between devices, per_device_tiled(): lax.all_to_all(conv.reshape(everyone, few, rows), ('ctx', 'dp'), 0, 0, ti...  14.4 us
    pallas_call x1, Pallas kernels, per_device_tiled(): pl.pallas_call(functools.partial(conv_kernel, parts, few, chunks), out_sh...  4.44 us
    all_to_all x1, starting transfers between devices, per_device_tiled(): lax.all_to_all(conv.reshape(everyone, few, rows), ('ctx', 'dp'), 0, 0, ti...  3.67 us
    pallas_call x1, Pallas kernels, per_device_tiled(): pl.pallas_call(functools.partial(pack_kernel, few, chunks), out_shape=jax...  2.37 us
  transfers between devices with their start and end apart: 1, of which 1 were waited for; matrix products, arithmetic and copies ran while one was open for 0% of the time, Pallas kernels for 1%

profile of v12, /device:TPU:0, one launch (start us, length us, event | category | flops | bytes accessed | tf_op | source)
XLA Modules:
  0.0 71.9 jit_solution(17353979731137147929)
XLA Ops:
  0.0 2.4 %shard_map.109 = f32[32,49,2,128]{3,2,1,0:T(2,128)S(1)} custom-call(s32[1]{0:T(128)} %bitcast.part_ref, f32[256,512]{1,0:T(8,128)} %q_ref.3, f32[256,512]{1,0:T(8,128)} %k_ref.3, f32[256,512]{1,0:T(8,128)} %v_ref.3, f32[3,3,512]{2,1,0:T(4,128)} %taps_ref.3, f32[1,512]{1,0:T(1,128)} %bitcast.3, f32[2,512,512]{2,1,0:T(8,128)} %spec_ref.1), custom_call_target="tpu_custom_call" | custom-call | bytes 4194304 | tf_op jit(solution)/shard_map/pallas_call | solution.py:485
  2.4 0.0 copy-start.3
  2.4 0.0 copy-start.4
  2.4 0.0 copy-start.5
  2.4 0.0 copy-start.7
  2.4 0.0 copy-start.9
  2.4 45.3 %all_to_all.10.in_ref = f32[32,49,2,128]{3,2,1,0:T(2,128)S(1)} all-to-all(f32[32,49,2,128]{3,2,1,0:T(2,128)S(1)} %shard_map.109), channel_id=1, replica_groups=mesh['dp'=2,'ctx'=16] {'ctx','dp'}, dimensions={0} | all-to-all | bytes 3211264 | tf_op jit(solution)/shard_map/all_to_all | solution.py:505
  47.7 0.0 copy-done.3
  47.7 0.0 copy-done.4
  47.7 0.0 copy-done.5
  47.7 0.0 copy-done.7
  47.7 0.0 copy-done.9
  47.8 0.0 copy-start
  47.8 0.0 copy-start.1
  47.8 0.0 copy-start.2
  47.8 0.0 copy-start.6
  47.8 0.0 copy-start.8
  47.8 4.4 %shard_map.110 = f32[16,2,16,256]{3,2,1,0:T(8,128)} custom-call(f32[32,49,2,128]{3,2,1,0:T(2,128)S(1)} %all_to_all.10.in_ref, f32[4,17,256]{2,1,0:T(8,128)S(1)} %copy-done.5, f32[2,128]{1,0:T(2,128)S(1)} %copy-done.9, bf16[768,256]{1,0:T(8,128)(2,1)S(1)} %copy-done.3, bf16[768,256]{1,0:T(8,128)(2,1)S(1)} %copy-done.4, bf16[256,128]{1,0:T(8,128)(2,1)S(1)} %copy-done.7), custom_call_target="tpu_custom_call" | custom-call | bytes 4194304 | tf_op jit(solution)/shard_map/pallas_call | solution.py:517
  52.3 3.7 %all-to-all-start.1 = ((f32[32,16,256]{2,1,0:T(8,128)}), f32[32,16,256]{2,1,0:T(8,128)S(1)}, u32[]{:S(2)}, u32[]{:S(2)}) async-start(f32[32,16,256]{2,1,0:T(8,128)} %bitcast.2), calls=%async_computation.1 | async-start | bytes 1048576 | tf_op jit(solution)/shard_map/all_to_all | solution.py:536
  55.9 0.0 copy-done
  56.0 0.0 copy-done.1
  56.0 0.0 copy-done.2
  56.0 0.0 copy-done.6
  56.0 0.0 copy-done.8
  56.0 0.5 shard_map.111
  56.5 14.4 %all-to-all-done.1.conv_ref = f32[32,16,256]{2,1,0:T(8,128)S(1)} async-done(((f32[32,16,256]{2,1,0:T(8,128)}), f32[32,16,256]{2,1,0:T(8,128)S(1)}, u32[]{:S(2)}, u32[]{:S(2)}) %all-to-all-start.1) | async-done | bytes 524320 | tf_op jit(solution)/shard_map/all_to_all | solution.py:536
  70.9 0.9 %shard_map.112 = f32[256,512]{1,0:T(8,128)} custom-call(f32[32,16,256]{2,1,0:T(8,128)S(1)} %all-to-all-done.1.conv_ref, f32[256,512]{1,0:T(8,128)S(1)} %get-tuple-element.7.query_ref, f32[256,512]{1,0:T(8,128)S(1)} %get-tuple-element.8.direct_ref), custom_call_target="tpu_custom_call" | custom-call | bytes 2097152 | tf_op jit(solution)/shard_map/pallas_call | solution.py:537
Async XLA Ops:
  2.4 45.3 %copy-start.3 = (bf16[768,256]{1,0:T(8,128)(2,1)S(1)}, bf16[768,256]{1,0:T(8,128)(2,1)}, u32[]{:S(2)}) copy-start(bf16[768,256]{1,0:T(8,128)(2,1)} %constant.18.clone.fore_ref) | copy-start | bytes 1179652
  2.4 45.3 %copy-start.4 = (bf16[768,256]{1,0:T(8,128)(2,1)S(1)}, bf16[768,256]{1,0:T(8,128)(2,1)}, u32[]{:S(2)}) copy-start(bf16[768,256]{1,0:T(8,128)(2,1)} %constant.19.clone.back_ref) | copy-start | bytes 1179652
  2.4 45.3 %copy-start.5 = (f32[4,17,256]{2,1,0:T(8,128)S(1)}, f32[4,17,256]{2,1,0:T(8,128)}, u32[]{:S(2)}) copy-start(f32[4,17,256]{2,1,0:T(8,128)} %constant.16.clone.turn_ref) | copy-start | bytes 208900
  2.4 45.3 %copy-start.7 = (bf16[256,128]{1,0:T(8,128)(2,1)S(1)}, bf16[256,128]{1,0:T(8,128)(2,1)}, u32[]{:S(2)}) copy-start(bf16[256,128]{1,0:T(8,128)(2,1)} %constant.20.clone.flip_ref) | copy-start | bytes 196612
  2.4 45.3 %copy-start.9 = (f32[2,128]{1,0:T(2,128)S(1)}, f32[2,128]{1,0:T(2,128)}, u32[]{:S(2)}) copy-start(f32[2,128]{1,0:T(2,128)} %constant.17.clone.parity_ref) | copy-start | bytes 3076
  47.8 8.2 %copy-start = (f32[256,512]{1,0:T(8,128)S(1)}, f32[256,512]{1,0:T(8,128)}, u32[]{:S(2)}) copy-start(f32[256,512]{1,0:T(8,128)} %q_ref.3) | copy-start | bytes 1572868
  47.8 8.2 %copy-start.1 = (f32[256,512]{1,0:T(8,128)S(1)}, f32[256,512]{1,0:T(8,128)}, u32[]{:S(2)}) copy-start(f32[256,512]{1,0:T(8,128)} %k_ref.3) | copy-start | bytes 1572868
  47.8 8.2 %copy-start.2 = (f32[256,512]{1,0:T(8,128)S(1)}, f32[256,512]{1,0:T(8,128)}, u32[]{:S(2)}) copy-start(f32[256,512]{1,0:T(8,128)} %v_ref.3) | copy-start | bytes 1572868
  47.8 8.2 %copy-start.6 = (f32[3,3,512]{2,1,0:T(4,128)S(1)}, f32[3,3,512]{2,1,0:T(4,128)}, u32[]{:S(2)}) copy-start(f32[3,3,512]{2,1,0:T(4,128)} %taps_ref.3) | copy-start | bytes 55300
  47.8 8.2 %copy-start.8 = (f32[512]{0:T(512)S(1)}, f32[512]{0:T(512)}, u32[]{:S(2)}) copy-start(f32[512]{0:T(512)} %param.15) | copy-start | bytes 6148
  52.3 18.7 %all-to-all-start.1 = ((f32[32,16,256]{2,1,0:T(8,128)}), f32[32,16,256]{2,1,0:T(8,128)S(1)}, u32[]{:S(2)}, u32[]{:S(2)}) async-start(f32[32,16,256]{2,1,0:T(8,128)} %bitcast.2), calls=%async_computation.1 | async-start | bytes 1048576 | tf_op jit(solution)/shard_map/all_to_all | solution.py:536
